TPU v7x, 32 devices: a whole 2x2x4 slice. The times are simulated.
32 devices in a mesh: fsdp: 4 (over z), ctx: 4 (over y, x), tp: 2 (over core).
Axes of the slice: x: 2, y: 2, z: 4, core: 2. Of those that a mesh axis runs over, the one named last changes fastest.
Arguments:
- layer_input: bfloat16 [4096, 1536], P(('fsdp', 'ctx')), may hold values from -6 to 6
- segments: int32 [4, 1024], P('fsdp'), may hold values from 0 to 7, as said below
- routes: int32 [4096, 8], P(('fsdp', 'ctx')), may hold values from 0 to 15, all different within a row; in each aligned block of 256 rows (0 to 255, 256 to 511, ...) at most 192 rows name the same one
- norm_gain: bfloat16 [1536], P(('fsdp', 'ctx')), may hold values from 0.5 to 1.5
- query_weight: bfloat16 [1536, 1536], P(('fsdp', 'ctx'), 'tp'), may hold values from -0.3125 to 0.3125
- key_weight: bfloat16 [1536, 512], P(('fsdp', 'ctx'), 'tp'), may hold values from -0.15625 to 0.15625
- value_weight: bfloat16 [1536, 512], P(('fsdp', 'ctx'), 'tp'), may hold values from -0.15625 to 0.15625
- output_weight: bfloat16 [1536, 1536], P('tp', ('fsdp', 'ctx')), may hold values from -0.625 to 0.625
- ffn_gain: bfloat16 [1536], P(('fsdp', 'ctx')), may hold values from 0.5 to 1.5
- router_weight: bfloat16 [1536, 16], P(('fsdp', 'ctx')), may hold values from -0.078125 to 0.078125
- gate_weight: bfloat16 [16, 1536, 512], P(None, ('fsdp', 'ctx'), 'tp'), may hold values from -0.15625 to 0.15625
- up_weight: bfloat16 [16, 1536, 512], P(None, ('fsdp', 'ctx'), 'tp'), may hold values from -0.15625 to 0.15625
- down_weight: bfloat16 [16, 512, 1536], P(None, 'tp', ('fsdp', 'ctx')), may hold values from -0.5 to 0.5
- cotangent: bfloat16 [4096, 1536], P(('fsdp', 'ctx')), may hold values from -6 to 6
Outputs:
- layer_output: bfloat16 [4096, 1536], P(('fsdp', 'ctx'))
- input_grad: float32 [4096, 1536], P(('fsdp', 'ctx'))
- norm_gain_grad: float32 [1536], P(('fsdp', 'ctx'))
- query_grad: float32 [1536, 1536], P(('fsdp', 'ctx'), 'tp')
- key_grad: float32 [1536, 512], P(('fsdp', 'ctx'), 'tp')
- value_grad: float32 [1536, 512], P(('fsdp', 'ctx'), 'tp')
- output_grad: float32 [1536, 1536], P('tp', ('fsdp', 'ctx'))
- ffn_gain_grad: float32 [1536], P(('fsdp', 'ctx'))
- router_grad: float32 [1536, 16], P(('fsdp', 'ctx'))
- gate_grad: float32 [16, 1536, 512], P(None, ('fsdp', 'ctx'), 'tp')
- up_grad: float32 [16, 1536, 512], P(None, ('fsdp', 'ctx'), 'tp')
- down_grad: float32 [16, 512, 1536], P(None, 'tp', ('fsdp', 'ctx'))
Inputs may be any that keep to these rules, and one draw needn't show every extreme that they name: Each row of segments never falls and numbers its documents from 0 in order. One row, drawn from the seed, holds three documents: the first and the last have 256/8 to 127 tokens, the middle one the rest. Every other row holds eight documents, cut at seven distinct places drawn from the seed. `routes`: each row names 8 different experts. Among the 256 rows of one device no expert is named by more than 192 rows.
All inputs are finite; a program needn't handle non-finite values.
Results may differ from a plain program's by a relative error of at most 0.025.
Values may be sent and summed in bfloat16 or wider, within the bound.
A program may use at most 256 MiB of HBM per device.

v0:
```python
import jax
import jax.numpy as jnp
from jax import lax
from jax.sharding import PartitionSpec as P

D = 1536
HD = 64
EXPERTS = 16
CAP = 192


EPSILON = 1e-05
MASKED_SCORE = -1e30


def rotate(values, place, sign):
    rows = values.shape[0]
    shaped = values.reshape(rows, -1, HD)
    half = HD // 2
    freq = 10000.0 ** (-2.0 * jnp.arange(half, dtype=jnp.float32) / HD)
    angle = place.astype(jnp.float32)[:, None] * freq[None, :]
    cosine = jnp.cos(angle)[:, None, :]
    sine = sign * jnp.sin(angle)[:, None, :]
    former = shaped[..., :half]
    latter = shaped[..., half:]
    turned = jnp.concatenate([former * cosine - latter * sine, latter * cosine + former * sine], -1)
    return turned.reshape(rows, -1)


def normalize(values, gain):
    inverse = lax.rsqrt(jnp.mean(values * values, -1, keepdims=True) + EPSILON)
    return (values * inverse * gain.astype(jnp.float32), inverse)


def norm_back(grad, values, inverse, gain):
    scaled = grad * gain.astype(jnp.float32)
    gain_grad = jnp.sum(grad * values * inverse, 0)
    mean_term = jnp.mean(scaled * values, -1, keepdims=True)
    return (inverse * scaled - values * inverse**3 * mean_term, gain_grad)


def document_place(segment_row):
    length = segment_row.shape[0]
    order = jnp.arange(length, dtype=jnp.int32)
    fresh = jnp.concatenate([jnp.ones((1,), jnp.bool_), segment_row[1:] != segment_row[:-1]])
    starts = lax.cummax(jnp.where(fresh, order, 0), axis=0)
    return order - starts


def contract_rows(left, right):
    return lax.dot_general(
        left, right, (((0,), (0,)), ((), ())), preferred_element_type=jnp.float32
    )


def times_transpose(left, right):
    return lax.dot_general(
        left, right, (((1,), (1,)), ((), ())), preferred_element_type=jnp.float32
    )


def shards(
    layer_input,
    segments,
    routes,
    norm_gain,
    query_weight,
    key_weight,
    value_weight,
    output_weight,
    ffn_gain,
    router_weight,
    gate_weight,
    up_weight,
    down_weight,
    cotangent,
):
    (
        gain_one,
        query_full,
        key_full,
        value_full,
        output_full,
        gain_two,
        router_full,
        gate_full,
        up_full,
        down_full,
    ) = (
        lax.all_gather(norm_gain, ("fsdp", "ctx"), axis=0, tiled=True),
        lax.all_gather(query_weight, ("fsdp", "ctx"), axis=0, tiled=True),
        lax.all_gather(key_weight, ("fsdp", "ctx"), axis=0, tiled=True),
        lax.all_gather(value_weight, ("fsdp", "ctx"), axis=0, tiled=True),
        lax.all_gather(output_weight, ("fsdp", "ctx"), axis=1, tiled=True),
        lax.all_gather(ffn_gain, ("fsdp", "ctx"), axis=0, tiled=True),
        lax.all_gather(router_weight, ("fsdp", "ctx"), axis=0, tiled=True),
        lax.all_gather(gate_weight, ("fsdp", "ctx"), axis=1, tiled=True),
        lax.all_gather(up_weight, ("fsdp", "ctx"), axis=1, tiled=True),
        lax.all_gather(down_weight, ("fsdp", "ctx"), axis=2, tiled=True),
    )
    tokens = layer_input.shape[0]
    seq_len = segments.shape[1]
    begin = lax.axis_index("ctx") * tokens
    segment_row = segments[0]
    place = lax.dynamic_slice_in_dim(document_place(segment_row), begin, tokens)
    query_doc = lax.dynamic_slice_in_dim(segment_row, begin, tokens)
    query_order = begin + jnp.arange(tokens, dtype=jnp.int32)
    scale = HD ** (-0.5)
    inputs = layer_input.astype(jnp.float32)
    first_norm, first_inverse = normalize(inputs, gain_one)
    normed1 = first_norm.astype(jnp.bfloat16)
    query = rotate(
        jnp.dot(normed1, query_full, preferred_element_type=jnp.float32), place, 1.0
    ).astype(jnp.bfloat16)
    key = rotate(jnp.dot(normed1, key_full, preferred_element_type=jnp.float32), place, 1.0).astype(
        jnp.bfloat16
    )
    value = jnp.dot(normed1, value_full, preferred_element_type=jnp.float32).astype(jnp.bfloat16)
    key_groups = key.shape[1] // HD
    groups = query.shape[1] // key.shape[1]
    grouped = query.reshape(tokens, key_groups, groups, HD)

    def block_scores(key_piece, offset):
        count = key_piece.shape[0]
        key_heads = key_piece.reshape(count, key_groups, HD)
        scores = (
            jnp.einsum("qkgd,nkd->qkgn", grouped, key_heads, preferred_element_type=jnp.float32)
            * scale
        )
        key_doc = lax.dynamic_slice_in_dim(segment_row, offset, count)
        key_order = offset + jnp.arange(count, dtype=jnp.int32)
        seen = (key_doc[None, :] == query_doc[:, None]) & (
            key_order[None, :] <= query_order[:, None]
        )
        return (scores, seen[:, None, None, :], key_heads)

    def masked_away(offset, count):
        last_doc = lax.dynamic_index_in_dim(segment_row, offset + count - 1, keepdims=False)
        return (offset > query_order[tokens - 1]) | (last_doc < query_doc[0])

    start_state = (
        jnp.zeros((tokens, key_groups, groups, HD), jnp.float32),
        jnp.full((tokens, key_groups, groups), MASKED_SCORE, jnp.float32),
        jnp.zeros((tokens, key_groups, groups), jnp.float32),
    )
    pieces = (
        lax.all_gather(key, "ctx", axis=0, tiled=True),
        lax.all_gather(value, "ctx", axis=0, tiled=True),
    )
    offset = jnp.int32(0)
    count = pieces[0].shape[0]

    def attend_compute(state):
        summed, running, totals = state
        scores, seen, key_heads = block_scores(pieces[0], offset)
        scores = jnp.where(seen, scores, MASKED_SCORE)
        new_top = jnp.maximum(running, jnp.max(scores, -1))
        weights = jnp.where(seen, jnp.exp(scores - new_top[..., None]), 0.0)
        value_heads = pieces[1].reshape(count, key_groups, HD)
        summed = jnp.einsum(
            "qkgn,nkd->qkgd",
            weights.astype(jnp.bfloat16),
            value_heads,
            preferred_element_type=jnp.float32,
        )
        return (summed, new_top, jnp.sum(weights, -1))

    summed, running, totals = lax.cond(
        masked_away(offset, count), lambda state: state, attend_compute, start_state
    )
    mixed = summed / totals[..., None]
    log_total = running + jnp.log(totals)
    mixed_low = mixed.reshape(tokens, -1).astype(jnp.bfloat16)
    attention = lax.psum(
        jnp.dot(mixed_low, output_full, preferred_element_type=jnp.float32).astype(jnp.bfloat16),
        "tp",
    ).astype(jnp.float32)
    middle = inputs + attention
    second_norm, second_inverse = normalize(middle, gain_two)
    normed2 = second_norm.astype(jnp.bfloat16)
    logits = jnp.dot(normed2, router_full, preferred_element_type=jnp.float32)
    chosen_mask = routes[:, :, None] == jnp.arange(EXPERTS, dtype=jnp.int32)[None, None, :]
    picks = chosen_mask.astype(jnp.float32)
    gates = jax.nn.softmax(jnp.take_along_axis(logits, routes, 1), axis=-1)
    gate_table = jnp.sum(gates[:, :, None] * picks, 1)
    member = jnp.sum(chosen_mask.astype(jnp.int32), 1)
    slots = jnp.cumsum(member, 0) - 1
    target = jnp.where(
        member > 0, jnp.arange(EXPERTS, dtype=jnp.int32)[None, :] * CAP + slots, EXPERTS * CAP
    )
    owners = jnp.broadcast_to(jnp.arange(tokens, dtype=jnp.int32)[:, None], (tokens, EXPERTS))
    table = (
        jnp.full((EXPERTS * CAP,), tokens, jnp.int32)
        .at[target.reshape(-1)]
        .set(owners.reshape(-1), mode="drop")
    )
    flat_table = table
    table = table.reshape(EXPERTS, CAP)
    expert_ids = jnp.arange(EXPERTS, dtype=jnp.int32)[:, None]
    routed = jnp.concatenate([normed2, jnp.zeros((1, D), jnp.bfloat16)], 0)[table]
    slot_gate = jnp.concatenate([gate_table, jnp.zeros((1, EXPERTS), jnp.float32)], 0)[
        table, expert_ids
    ]
    outer_grad = cotangent.astype(jnp.float32)
    routed_outer = jnp.concatenate([outer_grad, jnp.zeros((1, D), jnp.float32)], 0)[table]
    former = jnp.einsum("ecd,edf->ecf", routed, gate_full, preferred_element_type=jnp.float32)
    latter = jnp.einsum("ecd,edf->ecf", routed, up_full, preferred_element_type=jnp.float32)
    hidden = (jax.nn.silu(former) * latter).astype(jnp.bfloat16)
    result = jnp.einsum("ecf,efd->ecd", hidden, down_full, preferred_element_type=jnp.float32)
    mixture_part = (
        jnp.zeros((tokens + 1, D), jnp.float32)
        .at[flat_table]
        .add((slot_gate[..., None] * result).reshape(-1, D))[:tokens]
    )
    mixture = lax.psum(mixture_part.astype(jnp.bfloat16), "tp").astype(jnp.float32)
    layer_output = (middle + mixture).astype(jnp.bfloat16)
    slot_dgate = jnp.sum(routed_outer * result, -1)
    result_grad = (slot_gate[..., None] * routed_outer).astype(jnp.bfloat16)
    hidden_grad = jnp.einsum(
        "ecd,efd->ecf", result_grad, down_full, preferred_element_type=jnp.float32
    )
    down_sums = jnp.einsum("ecf,ecd->efd", hidden, result_grad, preferred_element_type=jnp.float32)
    logistic = jax.nn.sigmoid(former)
    former_grad = (hidden_grad * latter * logistic * (1.0 + former * (1.0 - logistic))).astype(
        jnp.bfloat16
    )
    latter_grad = (hidden_grad * former * logistic).astype(jnp.bfloat16)
    gate_sums = jnp.einsum("ecd,ecf->edf", routed, former_grad, preferred_element_type=jnp.float32)
    up_sums = jnp.einsum("ecd,ecf->edf", routed, latter_grad, preferred_element_type=jnp.float32)
    routed_grad = jnp.einsum(
        "ecf,edf->ecd", former_grad, gate_full, preferred_element_type=jnp.float32
    ) + jnp.einsum("ecf,edf->ecd", latter_grad, up_full, preferred_element_type=jnp.float32)
    input_part = (
        jnp.zeros((tokens + 1, D), jnp.float32)
        .at[flat_table]
        .add(routed_grad.reshape(-1, D))[:tokens]
    )
    gate_part = (
        jnp.zeros((tokens + 1, EXPERTS), jnp.float32).at[table, expert_ids].add(slot_dgate)[:tokens]
    )
    input_part, gate_part = (
        lax.psum(input_part.astype(jnp.bfloat16), "tp").astype(jnp.float32),
        lax.psum(gate_part.astype(jnp.bfloat16), "tp").astype(jnp.float32),
    )
    picked_grad = jnp.take_along_axis(gate_part, routes, 1)
    logit_pick = gates * (picked_grad - jnp.sum(gates * picked_grad, -1, keepdims=True))
    logit_grad = jnp.sum(logit_pick[:, :, None] * picks, 1).astype(jnp.bfloat16)
    router_sums = contract_rows(normed2, logit_grad)
    second_grad = input_part + times_transpose(logit_grad, router_full)
    middle_back, gain_two_sums = norm_back(second_grad, middle, second_inverse, gain_two)
    middle_grad = outer_grad + middle_back
    attention_grad = middle_grad.astype(jnp.bfloat16)
    output_sums = contract_rows(mixed_low, attention_grad)
    mixed_grad = times_transpose(attention_grad, output_full).astype(jnp.bfloat16)
    mixed_heads = mixed_grad.reshape(tokens, key_groups, groups, HD)
    delta = jnp.sum(mixed_heads.astype(jnp.float32) * mixed, -1)
    key_all, value_all = (
        lax.all_gather(key, "ctx", axis=0, tiled=True),
        lax.all_gather(value, "ctx", axis=0, tiled=True),
    )

    def back_step(number, state):
        offset = number * tokens
        key_piece = lax.dynamic_slice_in_dim(key_all, offset, tokens, 0)
        value_piece = lax.dynamic_slice_in_dim(value_all, offset, tokens, 0)

        def back_compute(inner):
            query_sum, key_sum, value_sum = inner
            scores, seen, key_heads = block_scores(key_piece, offset)
            probs = jnp.where(seen, jnp.exp(scores - log_total[..., None]), 0.0)
            value_heads = value_piece.reshape(tokens, key_groups, HD)
            prob_grad = jnp.einsum(
                "qkgd,nkd->qkgn", mixed_heads, value_heads, preferred_element_type=jnp.float32
            )
            score_grad = (probs * (prob_grad - delta[..., None])).astype(jnp.bfloat16)
            query_sum = (
                query_sum
                + jnp.einsum(
                    "qkgn,nkd->qkgd", score_grad, key_heads, preferred_element_type=jnp.float32
                )
                * scale
            )
            key_block = (
                jnp.einsum(
                    "qkgn,qkgd->nkd", score_grad, grouped, preferred_element_type=jnp.float32
                )
                * scale
            )
            value_block = jnp.einsum(
                "qkgn,qkgd->nkd",
                probs.astype(jnp.bfloat16),
                mixed_heads,
                preferred_element_type=jnp.float32,
            )
            key_sum = lax.dynamic_update_slice_in_dim(
                key_sum,
                lax.dynamic_slice_in_dim(key_sum, offset, tokens, 0)
                + key_block.reshape(tokens, -1),
                offset,
                0,
            )
            value_sum = lax.dynamic_update_slice_in_dim(
                value_sum,
                lax.dynamic_slice_in_dim(value_sum, offset, tokens, 0)
                + value_block.reshape(tokens, -1),
                offset,
                0,
            )
            return (query_sum, key_sum, value_sum)

        return lax.cond(masked_away(offset, tokens), lambda inner: inner, back_compute, state)

    back_state = (
        jnp.zeros((tokens, key_groups, groups, HD), jnp.float32),
        jnp.zeros((seq_len, key.shape[1]), jnp.float32),
        jnp.zeros((seq_len, key.shape[1]), jnp.float32),
    )
    query_sum, key_sum, value_sum = lax.fori_loop(0, seq_len // tokens, back_step, back_state)
    key_local, value_local = (
        lax.psum_scatter(
            key_sum.astype(jnp.bfloat16), "ctx", scatter_dimension=0, tiled=True
        ).astype(jnp.float32),
        lax.psum_scatter(
            value_sum.astype(jnp.bfloat16), "ctx", scatter_dimension=0, tiled=True
        ).astype(jnp.float32),
    )
    query_back = rotate(query_sum.reshape(tokens, -1), place, -1.0).astype(jnp.bfloat16)
    key_back = rotate(key_local, place, -1.0).astype(jnp.bfloat16)
    value_back = value_local.astype(jnp.bfloat16)
    query_sums = contract_rows(normed1, query_back)
    key_sums = contract_rows(normed1, key_back)
    value_sums = contract_rows(normed1, value_back)
    first_part = (
        times_transpose(query_back, query_full)
        + times_transpose(key_back, key_full)
        + times_transpose(value_back, value_full)
    )
    first_grad = lax.psum(first_part.astype(jnp.bfloat16), "tp").astype(jnp.float32)
    input_back, gain_one_sums = norm_back(first_grad, inputs, first_inverse, gain_one)
    input_grad = middle_grad + input_back
    (
        gain_one_out,
        query_out,
        key_out,
        value_out,
        output_out,
        gain_two_out,
        router_out,
        gate_out,
        up_out,
        down_out,
    ) = (
        lax.psum_scatter(gain_one_sums, ("fsdp", "ctx"), scatter_dimension=0, tiled=True),
        lax.psum_scatter(query_sums, ("fsdp", "ctx"), scatter_dimension=0, tiled=True),
        lax.psum_scatter(key_sums, ("fsdp", "ctx"), scatter_dimension=0, tiled=True),
        lax.psum_scatter(value_sums, ("fsdp", "ctx"), scatter_dimension=0, tiled=True),
        lax.psum_scatter(output_sums, ("fsdp", "ctx"), scatter_dimension=1, tiled=True),
        lax.psum_scatter(gain_two_sums, ("fsdp", "ctx"), scatter_dimension=0, tiled=True),
        lax.psum_scatter(router_sums, ("fsdp", "ctx"), scatter_dimension=0, tiled=True),
        lax.psum_scatter(gate_sums, ("fsdp", "ctx"), scatter_dimension=1, tiled=True),
        lax.psum_scatter(up_sums, ("fsdp", "ctx"), scatter_dimension=1, tiled=True),
        lax.psum_scatter(down_sums, ("fsdp", "ctx"), scatter_dimension=2, tiled=True),
    )
    return (
        layer_output,
        input_grad,
        gain_one_out,
        query_out,
        key_out,
        value_out,
        output_out,
        gain_two_out,
        router_out,
        gate_out,
        up_out,
        down_out,
    )


def solution(mesh):
    in_specs = (
        P(("fsdp", "ctx"), None),
        P("fsdp", None),
        P(("fsdp", "ctx"), None),
        P(("fsdp", "ctx")),
        P(("fsdp", "ctx"), "tp"),
        P(("fsdp", "ctx"), "tp"),
        P(("fsdp", "ctx"), "tp"),
        P("tp", ("fsdp", "ctx")),
        P(("fsdp", "ctx")),
        P(("fsdp", "ctx"), None),
        P(None, ("fsdp", "ctx"), "tp"),
        P(None, ("fsdp", "ctx"), "tp"),
        P(None, "tp", ("fsdp", "ctx")),
        P(("fsdp", "ctx"), None),
    )
    out_specs = (
        P(("fsdp", "ctx"), None),
        P(("fsdp", "ctx"), None),
        P(("fsdp", "ctx")),
        P(("fsdp", "ctx"), "tp"),
        P(("fsdp", "ctx"), "tp"),
        P(("fsdp", "ctx"), "tp"),
        P("tp", ("fsdp", "ctx")),
        P(("fsdp", "ctx")),
        P(("fsdp", "ctx"), None),
        P(None, ("fsdp", "ctx"), "tp"),
        P(None, ("fsdp", "ctx"), "tp"),
        P(None, "tp", ("fsdp", "ctx")),
    )
    return jax.shard_map(shards, mesh=mesh, in_specs=in_specs, out_specs=out_specs, check_vma=False)
```

profile of v0, /device:TPU:9, one launch (start us, length us, event | category | flops | bytes accessed | tf_op | source)
XLA Modules:
  0.0 2793.4 jit_solution(5384261846496650554)
XLA Ops:
  16.3 30.2 %all-reduce.8 = (bf16[1536]{0:T(1024)(128)(2,1)S(1)}, bf16[1536]{0:T(1024)(128)(2,1)S(1)}) all-reduce(bf16[1536]{0:T(1024)(128)(2,1)S(1)} %dynamic-update-slice, bf16[1536]{0:T(1024)(128)(2,1)S(1)} %dynamic-update-slice.1), channel_id=1, replica_groups=mesh['fsdp'=4,'ctx'=4,'tp'=2] {'fsdp','ctx'}, use_global_device_ids=true, to_apply=%add.3 | all-reduce | flops 3072 | bytes 12288
  50.8 36.6 %all_gather.39 = bf16[1536,256]{1,0:T(8,128)(2,1)S(1)} all-gather(bf16[96,256]{1,0:T(8,128)(2,1)} %param.27), channel_id=1, replica_groups=mesh['fsdp'=4,'ctx'=4,'tp'=2] {'fsdp','ctx'}, dimensions={0}, use_global_device_ids=true | all-gather | bytes 835584 | tf_op jit(solution)/shard_map/all_gather | solution.py:92
  87.4 2.0 fusion.68
  89.5 11.1 all_gather.40
  100.7 38.6 %all_gather.42 = bf16[1536,256]{1,0:T(8,128)(2,1)S(1)} all-gather(bf16[96,256]{1,0:T(8,128)(2,1)S(1)} %copy-done.42), channel_id=1, replica_groups=mesh['fsdp'=4,'ctx'=4,'tp'=2] {'fsdp','ctx'}, dimensions={0}, use_global_device_ids=true | all-gather | bytes 835584 | tf_op jit(solution)/shard_map/all_gather | solution.py:93
  140.6 10.6 all_gather.43
  151.3 2.9 fusion.66
  155.2 10.1 conditional.2
  155.7 3.0 fusion
  158.7 3.5 fusion.6
  162.2 3.1 fusion.1
  165.5 3.7 convolution_convert_fusion
  171.1 28.6 %all-gather = bf16[16,96,16]{1,2,0:T(8,128)(2,1)S(1)} all-gather(bf16[1,96,16]{1,2,0:T(8,128)(2,1)S(1)} %bitcast.223), channel_id=1, replica_groups=mesh['fsdp'=4,'ctx'=4,'tp'=2] {'fsdp','ctx'}, dimensions={0}, use_global_device_ids=true | all-gather | bytes 52224 | tf_op jit(solution)/shard_map/all_gather | solution.py:96
  201.5 15.5 scatter_custom_fusion
  218.9 15.9 gather_fusion.2
  239.2 16.8 gather_fusion.3
  256.3 14.7 gather_fusion.1
  271.1 93.4 %all-gather.11.cloned.1.call-done = bf16[16,1536,256]{2,1,0:T(8,128)(2,1)} async-done(((bf16[16,96,256]{2,1,0:T(8,128)(2,1)}), bf16[16,1536,256]{2,1,0:T(8,128)(2,1)}) %all-gather.11.cloned.1.call-update) | async-done | bytes 12582928 | tf_op jit(solution)/shard_map/all_gather | solution.py:97
  364.5 11.5 fusion.74
  376.0 141.6 %all-gather.13.cloned.1.call-done = bf16[16,1536,256]{2,1,0:T(8,128)(2,1)} async-done(((bf16[16,96,256]{2,1,0:T(8,128)(2,1)}), bf16[16,1536,256]{2,1,0:T(8,128)(2,1)}) %all-gather.13.cloned.1.call-update) | async-done | bytes 12582928 | tf_op jit(solution)/shard_map/all_gather | solution.py:98
  517.6 12.8 multiply_convert_fusion.5
  530.4 140.4 %all-gather.15.cloned.1.call-done = bf16[16,256,1536]{1,2,0:T(8,128)(2,1)} async-done(((bf16[16,256,96]{1,2,0:T(8,128)(2,1)}), bf16[16,256,1536]{1,2,0:T(8,128)(2,1)}) %all-gather.15.cloned.1.call-update) | async-done | bytes 12582928 | tf_op jit(solution)/shard_map/all_gather | solution.py:99
  670.7 19.0 multiply_reduce_fusion
  689.8 21.9 scatter_custom_fusion.3
  711.8 3.6 psum.38
  715.5 16.8 gather_fusion.4
  732.7 20.2 gather_fusion
  752.9 14.4 multiply_convert_fusion.3
  767.4 16.5 fusion.75
  783.8 19.9 convolution_add_fusion
  803.8 32.8 %scatter_custom_fusion.2 = f32[257,1536]{1,0:T(8,128)} fusion(s32[3072]{0:T(1024)} %compare_select_fusion.2, f32[3072,1536]{1,0:T(8,128)} %bitcast.197, f32[]{:T(128)} %constant.190.clone.1), kind=kCustom, calls=%fused_computation.89 | custom fusion | flops 4718592 | bytes 1579520 | tf_op jit(solution)/shard_map/scatter-add | solution.py:236
  836.6 2.4 slice.155
  840.7 18.1 all-reduce.16.cloned.1.call-done
  858.8 2.5 multiply_reduce_fusion.1
  861.3 1.9 subtract_add_fusion
  869.1 33.0 %while.21 = (s32[]{:T(128)}, f32[256,4,3,64]{0,3,2,1:T(8,128)S(1)}, f32[1024,256]{0,1:T(8,128)}, f32[1024,256]{0,1:T(8,128)}, s32[256]{0:T(256)}, /*index=5*/s32...) while((s32[]{:T(128)}, f32[256,4,3,64]{0,3,2,1:T(8,128)S(1)}, ...), condition=%wide.region_30.32_spmd, body=%wide.region_27.31_spmd.sunk | while | flops 511967488 | bytes 20663908 | solution.py:318
  874.8 10.1 conditional.4
  883.0 1.9 constant_dynamic-update-slice_fusion
  902.1 2.1 convert_element_type.176
  904.3 2.1 convert_element_type.178
  906.4 12.9 broadcast_multiply_fusion
  919.3 32.4 %scatter_custom_fusion.1 = f32[257,1536]{1,0:T(8,128)} fusion(s32[3072]{0:T(1024)} %compare_select_fusion.2, f32[3072,1536]{1,0:T(8,128)} %bitcast.201, f32[]{:T(128)} %constant.190.clone.1), kind=kCustom, calls=%fused_computation.91 | custom fusion | flops 4718592 | bytes 1579520 | tf_op jit(solution)/shard_map/scatter-add | solution.py:213
  951.7 2.4 slice.156
  954.1 2.5 fusion.79
  956.9 3.7 fusion.76
  961.5 3.2 convolution_add_fusion.3
  964.8 22.0 reduce-scatter.15.cloned.1.call-done
  986.7 3.1 fusion.28
  993.4 3.1 fusion.63
  997.4 2.9 fusion.43
  1000.4 13.5 fusion.77
  1014.0 13.2 fusion.78
  1027.2 15.1 fusion.26
  1043.1 69.0 %reduce-scatter.31.cloned.1.call-done = f32[96,16]{1,0:T(8,128)} async-done(((f32[1536,16]{1,0:T(8,128)}), f32[96,16]{1,0:T(8,128)}) %reduce-scatter.31.cloned.1.call-update) | async-done | bytes 6160
  1113.6 23.6 all-reduce.18.cloned.1.call-done
  1138.8 57.1 %all-reduce.7 = (f32[1536]{0:T(1024)S(1)}, f32[1536]{0:T(1024)S(1)}) all-reduce(f32[1536]{0:T(1024)S(1)} %get-tuple-element.724, f32[1536]{0:T(1024)S(1)} %copy-done.51), channel_id=4, replica_groups=mesh['fsdp'=4,'ctx'=4,'tp'=2] {'fsdp','ctx'}, use_global_device_ids=true, to_apply=%region_36.38.clone | all-reduce | flops 3072 | bytes 24576
  1197.0 3.5 fusion.31
  1200.5 65.8 %reduce-scatter.19.cloned.1.call-done = f32[96,256]{1,0:T(8,128)} async-done(((f32[1536,256]{1,0:T(8,128)}), f32[96,256]{1,0:T(8,128)}) %reduce-scatter.19.cloned.1.call-update) | async-done | bytes 98320 | tf_op jit(solution)/shard_map/reduce_scatter | solution.py:355
  1266.3 129.6 %reduce-scatter.21.cloned.1.call-done = f32[96,256]{1,0:T(8,128)} async-done(((f32[1536,256]{1,0:T(8,128)}), f32[96,256]{1,0:T(8,128)}) %reduce-scatter.21.cloned.1.call-update) | async-done | bytes 98320 | tf_op jit(solution)/shard_map/reduce_scatter | solution.py:356
  1395.9 142.0 %reduce-scatter.17.cloned.1.call-done = f32[96,768]{1,0:T(8,128)} async-done(((f32[1536,768]{1,0:T(8,128)}), f32[96,768]{1,0:T(8,128)}) %reduce-scatter.17.cloned.1.call-update) | async-done | bytes 294928 | tf_op jit(solution)/shard_map/reduce_scatter | solution.py:354
  1537.9 142.0 %reduce-scatter.23.cloned.1.call-done = f32[768,96]{0,1:T(8,128)} async-done(((f32[768,1536]{0,1:T(8,128)}), f32[768,96]{0,1:T(8,128)}) %reduce-scatter.23.cloned.1.call-update) | async-done | bytes 294928 | tf_op jit(solution)/shard_map/reduce_scatter | solution.py:357
  1679.9 369.3 %reduce-scatter.25.cloned.1.call-done = f32[16,96,256]{2,1,0:T(8,128)} async-done(((f32[16,1536,256]{2,1,0:T(8,128)}), f32[16,96,256]{2,1,0:T(8,128)}) %reduce-scatter.25.cloned.1.call-update) | async-done | bytes 1572880 | tf_op jit(solution)/shard_map/reduce_scatter | solution.py:360
  2049.2 368.5 %reduce-scatter.27.cloned.1.call-done = f32[16,96,256]{2,1,0:T(8,128)} async-done(((f32[16,1536,256]{2,1,0:T(8,128)}), f32[16,96,256]{2,1,0:T(8,128)}) %reduce-scatter.27.cloned.1.call-update) | async-done | bytes 1572880 | tf_op jit(solution)/shard_map/reduce_scatter | solution.py:361
  2417.7 368.4 %reduce-scatter.29.cloned.1.call-done = f32[16,256,96]{1,2,0:T(8,128)} async-done(((f32[16,256,1536]{1,2,0:T(8,128)}), f32[16,256,96]{1,2,0:T(8,128)}) %reduce-scatter.29.cloned.1.call-update) | async-done | bytes 1572880 | tf_op jit(solution)/shard_map/reduce_scatter | solution.py:362
  (285 shorter events, 65.2 us)
Async XLA Ops:
  7.2 144.1 %all-gather.7.cloned.1.call-start = ((), (), s32[]{:S(2)}) async-start(), calls=%async_computation.10 | async-start | bytes 2506752 | tf_op jit(solution)/shard_map/all_gather | solution.py:91
  7.9 157.6 %all-gather.9.cloned.1.call-start = ((), (), s32[]{:S(2)}) async-start(), calls=%async_computation.11 | async-start | bytes 2506752 | tf_op jit(solution)/shard_map/all_gather | solution.py:94
  8.7 226.7 %all-reduce.14.cloned.1.call-start = ((), (), s32[]{:S(2)}) async-start(), calls=%async_computation.12 | async-start | bytes 1572864 | tf_op jit(solution)/shard_map/psum | solution.py:174
  8.7 146.5 %copy-start.43 = (s32[256]{0:T(256)}, s32[256]{0:T(256)S(1)}, u32[]{:S(2)}) copy-start(s32[256]{0:T(256)S(1)} %iota_add_fusion.1) | copy-start | bytes 3076
  46.5 104.8 %copy-start.23 = (f32[1536]{0:T(1024)}, f32[1536]{0:T(1024)S(1)}, u32[]{:S(2)}) copy-start(f32[1536]{0:T(1024)S(1)} %convert_element_type.149) | copy-start | bytes 18436
  49.5 51.2 %copy-start.42 = (bf16[96,256]{1,0:T(8,128)(2,1)S(1)}, bf16[96,256]{1,0:T(8,128)(2,1)}, u32[]{:S(2)}) copy-start(bf16[96,256]{1,0:T(8,128)(2,1)} %param.28) | copy-start | bytes 147460
  50.0 101.3 %copy-start.38 = (f32[256]{0:T(256)}, f32[256]{0:T(256)S(1)}, u32[]{:S(2)}) copy-start(f32[256]{0:T(256)S(1)} %get-tuple-element.788) | copy-start | bytes 3076
  50.8 103.4 %copy-start.21 = (f32[256,32]{0,1:T(8,128)}, f32[256,32]{0,1:T(8,128)S(1)}, u32[]{:S(2)}) copy-start(f32[256,32]{0,1:T(8,128)S(1)} %get-tuple-element.786) | copy-start | bytes 98308
  87.4 53.2 %copy-start.15 = (bf16[1536,256]{1,0:T(8,128)(2,1)}, bf16[1536,256]{1,0:T(8,128)(2,1)S(1)}, u32[]{:S(2)}) copy-start(bf16[1536,256]{1,0:T(8,128)(2,1)S(1)} %all_gather.39) | copy-start | bytes 2359300
  87.4 52.8 %copy-start.1 = (bf16[256,1536]{1,0:T(8,128)(2,1)S(1)}, bf16[256,1536]{1,0:T(8,128)(2,1)}, u32[]{:S(2)}) copy-start(bf16[256,1536]{1,0:T(8,128)(2,1)} %param.22) | copy-start | bytes 2359300
  89.5 61.8 %copy-start.33 = (s32[1,1024]{1,0:T(1,128)S(1)}, s32[1,1024]{1,0:T(1,128)}, u32[]{:S(2)}) copy-start(s32[1,1024]{1,0:T(1,128)} %param.23) | copy-start | bytes 12292
  100.7 54.5 %copy-start.9 = (bf16[1024,256]{0,1:T(8,128)(2,1)}, bf16[1024,256]{0,1:T(8,128)(2,1)S(1)}, u32[]{:S(2)}) copy-start(bf16[1024,256]{0,1:T(8,128)(2,1)S(1)} %all_gather.40) | copy-start | bytes 1572868
  151.2 4.0 copy-start.10
  165.5 4.4 copy-start.17
  169.2 30.7 %copy-start.32 = (s32[256,8]{0,1:T(8,128)S(1)}, s32[256,8]{0,1:T(8,128)}, u32[]{:S(2)}) copy-start(s32[256,8]{0,1:T(8,128)} %param.24) | copy-start | bytes 24580
  169.2 48.0 %copy-start.56 = (s32[2]{0:T(128)S(1)}, s32[2]{0:T(128)}, u32[]{:S(2)}) copy-start(s32[2]{0:T(128)} %constant.213) | copy-start | bytes 28
  169.2 48.0 %copy-start.55 = (s32[2]{0:T(128)S(1)}, s32[2]{0:T(128)}, u32[]{:S(2)}) copy-start(s32[2]{0:T(128)} %constant.216) | copy-start | bytes 28
  169.2 49.5 %copy-start.16 = (bf16[256,1536]{1,0:T(8,128)(2,1)S(1)}, bf16[256,1536]{1,0:T(8,128)(2,1)}, u32[]{:S(2)}) copy-start(bf16[256,1536]{1,0:T(8,128)(2,1)} %param.35) | copy-start | bytes 2359300
  169.3 195.2 %all-gather.11.cloned.1.call-start = ((), (), s32[]{:S(2)}) async-start(), calls=%async_computation.13 | async-start | bytes 13369344 | tf_op jit(solution)/shard_map/all_gather | solution.py:97
  169.9 347.7 %all-gather.13.cloned.1.call-start = ((), (), s32[]{:S(2)}) async-start(), calls=%async_computation.14 | async-start | bytes 13369344 | tf_op jit(solution)/shard_map/all_gather | solution.py:98
  170.5 500.3 %all-gather.15.cloned.1.call-start = ((), (), s32[]{:S(2)}) async-start(), calls=%async_computation.15 | async-start | bytes 13369344 | tf_op jit(solution)/shard_map/all_gather | solution.py:99
  171.0 687.7 %all-reduce.16.cloned.1.call-start = ((), (), s32[]{:S(2)}) async-start(), calls=%async_computation.16 | async-start | bytes 1572864 | tf_op jit(solution)/shard_map/psum | solution.py:242
  171.1 66.4 %copy-start.34 = (f32[1536]{0:T(1024)}, f32[1536]{0:T(1024)S(1)}, u32[]{:S(2)}) copy-start(f32[1536]{0:T(1024)S(1)} %convert_element_type.160) | copy-start | bytes 18436
  199.9 39.0 %copy-start.28 = (bf16[1536,16]{0,1:T(8,128)(2,1)}, bf16[1536,16]{0,1:T(8,128)(2,1)S(1)}, u32[]{:S(2)}) copy-start(bf16[1536,16]{0,1:T(8,128)(2,1)S(1)} %reshape.529) | copy-start | bytes 147460
  237.5 18.6 copy-start.49
  238.9 17.3 copy-start.6
  530.4 159.4 %copy-start.4 = (bf16[16,192,256]{2,1,0:T(8,128)(2,1)}, bf16[16,192,256]{2,1,0:T(8,128)(2,1)S(1)}, u32[]{:S(2)}) copy-start(bf16[16,192,256]{2,1,0:T(8,128)(2,1)S(1)} %get-tuple-element.793) | copy-start | bytes 4718596
  715.5 17.2 copy-start
  732.5 126.2 %copy-start.45 = (bf16[256,16]{0,1:T(8,128)(2,1)}, bf16[256,16]{0,1:T(8,128)(2,1)S(1)}, u32[]{:S(2)}) copy-start(bf16[256,16]{0,1:T(8,128)(2,1)S(1)} %get-tuple-element.726) | copy-start | bytes 24580
  767.3 16.5 copy-start.3
  767.4 16.5 copy-start.5
  803.7 35.3 %copy-start.11 = (bf16[1024,256]{1,0:T(8,128)(2,1)S(1)}, bf16[1024,256]{1,0:T(8,128)(2,1)}, u32[]{:S(2)}) copy-start(bf16[1024,256]{1,0:T(8,128)(2,1)} %copy-done.10) | copy-start | bytes 1572868
  803.8 36.3 %copy-start.31 = (f32[256,4,3]{0,2,1:T(4,128)S(1)}, f32[256,4,3]{0,2,1:T(4,128)}, u32[]{:S(2)}) copy-start(f32[256,4,3]{0,2,1:T(4,128)} %copy-done.30) | copy-start | bytes 36868
  803.8 36.3 %copy-start.37 = (f32[256,4,3]{0,2,1:T(4,128)S(1)}, f32[256,4,3]{0,2,1:T(4,128)}, u32[]{:S(2)}) copy-start(f32[256,4,3]{0,2,1:T(4,128)} %copy-done.36) | copy-start | bytes 36868
  803.8 55.0 %copy-start.2 = (bf16[256,1536]{1,0:T(8,128)(2,1)S(1)}, bf16[256,1536]{1,0:T(8,128)(2,1)}, u32[]{:S(2)}) copy-start(bf16[256,1536]{1,0:T(8,128)(2,1)} %param.22) | copy-start | bytes 2359300
  803.8 55.0 %copy-start.7 = (bf16[256,1536]{1,0:T(8,128)(2,1)S(1)}, bf16[256,1536]{1,0:T(8,128)(2,1)}, u32[]{:S(2)}) copy-start(bf16[256,1536]{1,0:T(8,128)(2,1)} %all-reduce.14.cloned.1.call-done) | copy-start | bytes 2359300
  803.8 55.0 %copy-start.29 = (bf16[1536,16]{0,1:T(8,128)(2,1)S(1)}, bf16[1536,16]{0,1:T(8,128)(2,1)}, u32[]{:S(2)}) copy-start(bf16[1536,16]{0,1:T(8,128)(2,1)} %copy-done.28) | copy-start | bytes 147460
  803.8 55.0 %copy-start.35 = (f32[1536]{0:T(1024)S(1)}, f32[1536]{0:T(1024)}, u32[]{:S(2)}) copy-start(f32[1536]{0:T(1024)} %copy-done.34) | copy-start | bytes 18436
  803.8 55.0 %copy-start.50 = (f32[256]{0:T(256)S(1)}, f32[256]{0:T(256)}, u32[]{:S(2)}) copy-start(f32[256]{0:T(256)} %copy-done.49) | copy-start | bytes 3076
  839.0 121.6 %reduce-scatter.13.cloned.1.call-start = ((), (), s32[]{:S(2)}) async-start(), calls=%async_computation.17 | async-start | bytes 655360 | tf_op jit(solution)/shard_map/reduce_scatter | solution.py:320
  840.1 21.3 copy-start.54
  865.0 4.1 copy-start.20
  874.8 4.3 copy-start.41
  874.8 4.3 copy-start.44
  874.8 4.4 copy-start.47
  874.8 4.4 copy-start.48
  904.2 82.5 %reduce-scatter.15.cloned.1.call-start = ((), (), s32[]{:S(2)}) async-start(), calls=%async_computation.18 | async-start | bytes 655360 | tf_op jit(solution)/shard_map/reduce_scatter | solution.py:323
  906.4 205.7 %reduce-scatter.31.cloned.1.call-start = ((), (), s32[]{:S(2)}) async-start(), calls=%async_computation.26 | async-start | bytes 835584
  919.3 34.8 %copy-start.46 = (bf16[256,16]{0,1:T(8,128)(2,1)S(1)}, bf16[256,16]{0,1:T(8,128)(2,1)}, u32[]{:S(2)}) copy-start(bf16[256,16]{0,1:T(8,128)(2,1)} %copy-done.45) | copy-start | bytes 24580
  951.7 5.0 copy-start.22
  951.7 5.0 copy-start.26
  956.7 180.5 %all-reduce.18.cloned.1.call-start = ((), (), s32[]{:S(2)}) async-start(), calls=%async_computation.27 | async-start | bytes 3145728 | tf_op jit(solution)/shard_map/psum | solution.py:215
  964.8 25.1 copy-start.24
  964.8 25.1 copy-start.39
  989.8 276.5 %reduce-scatter.19.cloned.1.call-start = ((), (), s32[]{:S(2)}) async-start(), calls=%async_computation.20 | async-start | bytes 1671168 | tf_op jit(solution)/shard_map/reduce_scatter | solution.py:355
  991.6 404.3 %reduce-scatter.21.cloned.1.call-start = ((), (), s32[]{:S(2)}) async-start(), calls=%async_computation.21 | async-start | bytes 1671168 | tf_op jit(solution)/shard_map/reduce_scatter | solution.py:356
  993.3 544.6 %reduce-scatter.17.cloned.1.call-start = ((), (), s32[]{:S(2)}) async-start(), calls=%async_computation.19 | async-start | bytes 5013504 | tf_op jit(solution)/shard_map/reduce_scatter | solution.py:354
  996.4 683.5 %reduce-scatter.23.cloned.1.call-start = ((), (), s32[]{:S(2)}) async-start(), calls=%async_computation.22 | async-start | bytes 5013504 | tf_op jit(solution)/shard_map/reduce_scatter | solution.py:357
  1000.4 1048.9 %reduce-scatter.25.cloned.1.call-start = ((), (), s32[]{:S(2)}) async-start(), calls=%async_computation.23 | async-start | bytes 26738688 | tf_op jit(solution)/shard_map/reduce_scatter | solution.py:360
  1013.9 1403.8 %reduce-scatter.27.cloned.1.call-start = ((), (), s32[]{:S(2)}) async-start(), calls=%async_computation.24 | async-start | bytes 26738688 | tf_op jit(solution)/shard_map/reduce_scatter | solution.py:361
  1027.2 1758.9 %reduce-scatter.29.cloned.1.call-start = ((), (), s32[]{:S(2)}) async-start(), calls=%async_computation.25 | async-start | bytes 26738688 | tf_op jit(solution)/shard_map/reduce_scatter | solution.py:362
  1042.3 96.4 %copy-start.51 = (f32[1536]{0:T(1024)S(1)}, f32[1536]{0:T(1024)}, u32[]{:S(2)}) copy-start(f32[1536]{0:T(1024)} %get-tuple-element.722) | copy-start | bytes 18436
  1042.3 154.6 %copy-start.8 = (bf16[256,1536]{1,0:T(8,128)(2,1)S(1)}, bf16[256,1536]{1,0:T(8,128)(2,1)}, u32[]{:S(2)}) copy-start(bf16[256,1536]{1,0:T(8,128)(2,1)} %all-reduce.14.cloned.1.call-done) | copy-start | bytes 2359300
  1042.3 154.6 %copy-start.52 = (f32[256]{0:T(256)S(1)}, f32[256]{0:T(256)}, u32[]{:S(2)}) copy-start(f32[256]{0:T(256)} %get-tuple-element.787) | copy-start | bytes 3076
  (11 other events, 28.5 us)
Sparse Core Ops, SparseCore 0:
  10.8 66.7 all-gather.6
  80.4 69.4 all-gather.8
  169.4 41.8 all-reduce.13
  214.2 150.2 all-gather.10
  367.4 150.2 all-gather.12
  520.5 150.2 all-gather.14
  839.1 19.6 all-reduce.15
  904.3 54.4 reduce-scatter.12
  961.9 24.7 reduce-scatter.14
  991.3 120.7 reduce-scatter.30
  1115.0 22.0 all-reduce.17
  1143.1 123.1 reduce-scatter.18
  1272.4 123.4 reduce-scatter.20
  1402.3 135.5 reduce-scatter.16
  1543.5 136.3 reduce-scatter.22
  1687.0 362.1 reduce-scatter.24
  2056.3 361.2 reduce-scatter.26
  2424.8 361.2 reduce-scatter.28
where the time goes:
time: 2810 us; the launch traced here: 2790 us
  waiting for transfers between devices  2100 us (75%)
  blocking collectives  216 us (8%)
  matrix products  182 us (6%)
  local copies, waits for them, and re-layouts  140 us (5%)
  other arithmetic  130 us (5%)
    reduce_scatter x1, waiting for transfers between devices, shards(): lax.psum_scatter(gate_sums, ('fsdp', 'ctx'), scatter_dimension=1, tiled=T...  369 us
    reduce_scatter x1, waiting for transfers between devices, shards(): lax.psum_scatter(up_sums, ('fsdp', 'ctx'), scatter_dimension=1, tiled=True)  368 us
    reduce_scatter x1, waiting for transfers between devices, shards(): lax.psum_scatter(down_sums, ('fsdp', 'ctx'), scatter_dimension=2, tiled=T...  368 us
    reduce_scatter x1, waiting for transfers between devices, shards(): lax.psum_scatter(output_sums, ('fsdp', 'ctx'), scatter_dimension=1, tiled...  142 us
    reduce_scatter x1, waiting for transfers between devices, shards(): lax.psum_scatter(query_sums, ('fsdp', 'ctx'), scatter_dimension=0, tiled=...  142 us
    all_gather x1, waiting for transfers between devices, shards(): lax.all_gather(up_weight, ('fsdp', 'ctx'), axis=1, tiled=True)  142 us
    all_gather x1, waiting for transfers between devices, shards(): lax.all_gather(down_weight, ('fsdp', 'ctx'), axis=2, tiled=True)  140 us
    reduce_scatter x1, waiting for transfers between devices, shards(): lax.psum_scatter(value_sums, ('fsdp', 'ctx'), scatter_dimension=0, tiled=...  130 us
  transfers between devices with their start and end apart: 18, of which 14 were waited for; matrix products, arithmetic and copies ran while one was open for 9% of the time, Pallas kernels for 0%

commit v1 on v0

v1 whole, which is shorter than its diff:
```python
import jax
import jax.numpy as jnp
from jax import lax
from jax.experimental import pallas as pl
from jax.experimental.pallas import tpu as pltpu
from jax.sharding import PartitionSpec as P

MESH = pl.DeviceIdType.MESH

D = 1536
HD = 64
EXPERTS = 16


EPSILON = 1e-05
MASKED_SCORE = -1e30


def rotate(values, place, sign):
    rows = values.shape[0]
    shaped = values.reshape(rows, -1, HD)
    half = HD // 2
    freq = 10000.0 ** (-2.0 * jnp.arange(half, dtype=jnp.float32) / HD)
    angle = place.astype(jnp.float32)[:, None] * freq[None, :]
    cosine = jnp.cos(angle)[:, None, :]
    sine = sign * jnp.sin(angle)[:, None, :]
    former = shaped[..., :half]
    latter = shaped[..., half:]
    turned = jnp.concatenate([former * cosine - latter * sine, latter * cosine + former * sine], -1)
    return turned.reshape(rows, -1)


def normalize(values, gain):
    inverse = lax.rsqrt(jnp.mean(values * values, -1, keepdims=True) + EPSILON)
    return (values * inverse * gain.astype(jnp.float32), inverse)


def norm_back(grad, values, inverse, gain):
    scaled = grad * gain.astype(jnp.float32)
    gain_grad = jnp.sum(grad * values * inverse, 0)
    mean_term = jnp.mean(scaled * values, -1, keepdims=True)
    return (inverse * scaled - values * inverse**3 * mean_term, gain_grad)


def document_place(segment_row):
    length = segment_row.shape[0]
    order = jnp.arange(length, dtype=jnp.int32)
    fresh = jnp.concatenate([jnp.ones((1,), jnp.bool_), segment_row[1:] != segment_row[:-1]])
    starts = lax.cummax(jnp.where(fresh, order, 0), axis=0)
    return order - starts


def contract_rows(left, right):
    return lax.dot_general(
        left, right, (((0,), (0,)), ((), ())), preferred_element_type=jnp.float32
    )


def times_transpose(left, right):
    return lax.dot_general(
        left, right, (((1,), (1,)), ((), ())), preferred_element_type=jnp.float32
    )


def spread_experts(packed):
    ep = lax.axis_size("fsdp")
    local = packed.shape[0] // ep
    rows = packed.shape[1]
    swapped = lax.all_to_all(packed, "fsdp", 0, 0, tiled=True)
    swapped = swapped.reshape(ep, local, rows, -1).transpose(0, 2, 1, 3)
    swapped = swapped.reshape(ep, rows, -1)
    whole = lax.all_gather(swapped, "ctx", axis=1)
    return whole.reshape(ep * lax.axis_size("ctx") * rows, -1)


def collect_experts(sums, rows):
    ep, ring = lax.axis_size("fsdp"), lax.axis_size("ctx")
    turned = sums.reshape(ep, ring, rows, -1).transpose(1, 0, 2, 3).reshape(sums.shape)
    mine = lax.psum_scatter(turned, "ctx", scatter_dimension=0, tiled=True)
    return lax.all_to_all(mine, "fsdp", 0, 0, tiled=True)


def at_device(fsdp, ctx, tp):
    return {"fsdp": fsdp, "ctx": ctx, "tp": tp}


def greet(partners):
    barrier = pltpu.get_barrier_semaphore()
    for device in partners:
        pl.semaphore_signal(barrier, inc=1, device_id=device, device_id_type=MESH)
    pl.semaphore_wait(barrier, len(partners))


def remote(source, target, send, recv, device):
    return pltpu.make_async_remote_copy(
        src_ref=source, dst_ref=target, send_sem=send, recv_sem=recv, device_id=device, device_id_type=MESH
    )


def gather_kernel(
    attn_ref, gate_ref, up_ref, down_ref, outer_ref,
    attn_out, expert_out, outer_out,
    local_sem, z_send, z_recv, plane_send, plane_recv, relay_send, relay_recv, core_send, core_recv,
):
    ep = z_send.shape[1] + 1
    f, c, t = lax.axis_index("fsdp"), lax.axis_index("ctx"), lax.axis_index("tp")
    rows = attn_ref.shape[0]
    local = gate_ref.shape[0] // ep
    hidden = gate_ref.shape[2]
    tokens = outer_ref.shape[0]
    half = tokens // 2
    outs = (attn_out, expert_out)
    cuts = [(out.shape[1] // 256) * 128 for out in outs]

    def peer(distance):
        return lax.rem(f + distance, ep)

    def shard_rows(fsdp, ctx):
        return pl.ds(pl.multiple_of((fsdp * 4 + ctx) * rows, 16), rows)

    def columns(kind, side):
        cut, width = cuts[kind], outs[kind].shape[1]
        return pl.ds(0, cut) if side == 0 else pl.ds(cut, width - cut)

    x_device = at_device(f, c ^ 1, t)
    y_device = at_device(f, c ^ 2, t)
    core = at_device(f, c, 1 - t)
    greet([at_device(peer(d), c, t) for d in range(1, ep)] + [x_device, y_device, core])

    mine = shard_rows(f, c)
    sent = []
    for d in range(1, ep):
        device = at_device(peer(d), c, t)
        copy = remote(attn_ref, attn_out.at[mine], z_send.at[0, d - 1], z_recv.at[0, d - 1], device)
        copy.start()
        sent.append(copy)
    copies = [pltpu.make_async_copy(attn_ref, attn_out.at[mine], local_sem.at[0])]
    copies[0].start()
    for d in range(ep):
        for kind, ref in enumerate((gate_ref, up_ref, down_ref)):
            for e in range(local):
                target = expert_out.at[mine, pl.ds((kind * local + e) * hidden, hidden)]
                source = ref.at[peer(d) * local + e]
                if d == 0:
                    pltpu.make_async_copy(source, target, local_sem.at[1]).start()
                else:
                    remote(
                        source, target, z_send.at[1, d - 1], z_recv.at[1, d - 1], at_device(peer(d), c, t)
                    ).start()
    here = pl.ds(pl.multiple_of(f * tokens + t * half, 16), half)
    my_half = outer_ref.at[pl.ds(pl.multiple_of(t * half, 16), half)]
    for d in range(1, ep):
        copy = remote(
            my_half, outer_out.at[here], z_send.at[2, d - 1], z_recv.at[2, d - 1], at_device(peer(d), c, t)
        )
        copy.start()
        sent.append(copy)
    copies.append(
        pltpu.make_async_copy(
            outer_ref, outer_out.at[pl.ds(pl.multiple_of(f * tokens, 16), tokens)], local_sem.at[2]
        )
    )
    copies[1].start()

    def z_arrival(kind, d):
        back = lax.rem(f + ep - d, ep)
        place = shard_rows(back, c)
        remote(
            outs[kind].at[place], outs[kind].at[place], z_send.at[kind, d - 1], z_recv.at[kind, d - 1], x_device
        ).wait_recv()

    def spread(kind, d):
        place = shard_rows(lax.rem(f + ep - d, ep), c)
        for step in range(2):
            for way, device in enumerate((x_device, y_device)):
                side = step ^ way
                block = outs[kind].at[place, columns(kind, side)]
                copy = remote(
                    block, block, plane_send.at[kind, d, way, side], plane_recv.at[kind, d, way, side], device
                )
                copy.start()
                sent.append(copy)

    def pass_on(kind, d):
        for way, device in enumerate((y_device, x_device)):
            origin = c ^ (1 if way == 0 else 2)
            place = shard_rows(lax.rem(f + ep - d, ep), origin)
            block = outs[kind].at[place, columns(kind, way)]
            remote(
                block, block, plane_send.at[kind, d, way, way], plane_recv.at[kind, d, way, way], device
            ).wait_recv()
            copy = remote(block, block, relay_send.at[kind, d, way], relay_recv.at[kind, d, way], device)
            copy.start()
            sent.append(copy)

    copies[0].wait()
    spread(0, 0)
    pltpu.make_async_copy(expert_out.at[mine], expert_out.at[mine], local_sem.at[1]).wait()
    spread(1, 0)
    for d in range(1, ep):
        z_arrival(0, d)
        spread(0, d)
        pass_on(0, d - 1)
    pass_on(1, 0)
    pass_on(0, ep - 1)
    for d in range(1, ep):
        z_arrival(1, d)
        spread(1, d)
        if d > 1:
            pass_on(1, d - 1)
    pass_on(1, ep - 1)
    for d in range(1, ep):
        back = lax.rem(f + ep - d, ep)
        place = pl.ds(pl.multiple_of(back * tokens + t * half, 16), half)
        remote(
            outer_out.at[place], outer_out.at[place], z_send.at[2, d - 1], z_recv.at[2, d - 1], core
        ).wait_recv()
        copy = remote(
            outer_out.at[place], outer_out.at[place], core_send.at[d - 1], core_recv.at[d - 1], core
        )
        copy.start()
        sent.append(copy)
    copies[1].wait()
    for kind in range(2):
        for d in range(ep):
            back = lax.rem(f + ep - d, ep)
            for way, device in enumerate((x_device, y_device)):
                side = 1 - way
                block = outs[kind].at[shard_rows(back, c ^ (1 << way)), columns(kind, side)]
                remote(
                    block, block, plane_send.at[kind, d, way, side], plane_recv.at[kind, d, way, side], device
                ).wait_recv()
                block = outs[kind].at[shard_rows(back, c ^ 3), columns(kind, way)]
                remote(
                    block, block, relay_send.at[kind, d, way], relay_recv.at[kind, d, way], device
                ).wait_recv()
    for d in range(1, ep):
        back = lax.rem(f + ep - d, ep)
        place = pl.ds(pl.multiple_of(back * tokens + (1 - t) * half, 16), half)
        remote(
            outer_out.at[place], outer_out.at[place], core_send.at[d - 1], core_recv.at[d - 1], core
        ).wait_recv()
        remote(
            expert_out.at[mine], expert_out.at[mine], z_send.at[1, d - 1], z_recv.at[1, d - 1], core
        ).wait_send()
    for copy in sent:
        copy.wait_send()


def gather_all(attn, gate, up, down, outer):
    ep = lax.axis_size("fsdp")
    rows = attn.shape[0]
    total = rows * ep * lax.axis_size("ctx")
    local = gate.shape[0] // ep
    low = jnp.bfloat16
    dma = pltpu.SemaphoreType.DMA
    anywhere = pl.BlockSpec(memory_space=pl.ANY)
    return pl.pallas_call(
        gather_kernel,
        out_shape=(
            jax.ShapeDtypeStruct((total, attn.shape[1]), low),
            jax.ShapeDtypeStruct((total, 3 * local * gate.shape[2]), low),
            jax.ShapeDtypeStruct((ep * outer.shape[0], outer.shape[1]), low),
        ),
        in_specs=[anywhere] * 5,
        out_specs=(anywhere,) * 3,
        scratch_shapes=[
            dma((3,)),
            dma((3, ep - 1)),
            dma((3, ep - 1)),
            dma((2, ep, 2, 2)),
            dma((2, ep, 2, 2)),
            dma((2, ep, 2)),
            dma((2, ep, 2)),
            dma((ep - 1,)),
            dma((ep - 1,)),
        ],
        compiler_params=pltpu.CompilerParams(collective_id=1, has_side_effects=True),
        name="gather_all",
    )(attn, gate, up, down, outer)


def along_z_kernel(mine_ref, all_ref, local_sem, z_send, z_recv, core_send, core_recv):
    ep = z_send.shape[0] + 1
    f, c, t = lax.axis_index("fsdp"), lax.axis_index("ctx"), lax.axis_index("tp")
    tokens = mine_ref.shape[0]
    half = tokens // 2

    def peer(distance):
        return lax.rem(f + distance, ep)

    def place(fsdp, part):
        return pl.ds(pl.multiple_of(fsdp * tokens + part * half, 16), half)

    core = at_device(f, c, 1 - t)
    greet([at_device(peer(d), c, t) for d in range(1, ep)] + [core])
    sent = []
    source = mine_ref.at[pl.ds(pl.multiple_of(t * half, 16), half)]
    for d in range(1, ep):
        copy = remote(
            source, all_ref.at[place(f, t)], z_send.at[d - 1], z_recv.at[d - 1], at_device(peer(d), c, t)
        )
        copy.start()
        sent.append(copy)
    own = pltpu.make_async_copy(
        mine_ref, all_ref.at[pl.ds(pl.multiple_of(f * tokens, 16), tokens)], local_sem
    )
    own.start()
    for d in range(1, ep):
        block = all_ref.at[place(peer(ep - d), t)]
        remote(block, block, z_send.at[d - 1], z_recv.at[d - 1], core).wait_recv()
        copy = remote(block, block, core_send.at[d - 1], core_recv.at[d - 1], core)
        copy.start()
        sent.append(copy)
    for d in range(1, ep):
        block = all_ref.at[place(peer(ep - d), 1 - t)]
        remote(block, block, core_send.at[d - 1], core_recv.at[d - 1], core).wait_recv()
    own.wait()
    for copy in sent:
        copy.wait_send()


def along_z(mine):
    ep = lax.axis_size("fsdp")
    dma = pltpu.SemaphoreType.DMA
    anywhere = pl.BlockSpec(memory_space=pl.ANY)
    return pl.pallas_call(
        along_z_kernel,
        out_shape=jax.ShapeDtypeStruct((ep * mine.shape[0], mine.shape[1]), mine.dtype),
        in_specs=[anywhere],
        out_specs=anywhere,
        scratch_shapes=[dma, dma((ep - 1,)), dma((ep - 1,)), dma((ep - 1,)), dma((ep - 1,))],
        compiler_params=pltpu.CompilerParams(collective_id=2, has_side_effects=True),
        name="along_z",
    )(mine)


def sum_z_kernel(
    part_ref, sum_ref, core_in, z_out, z_in, core_send, core_recv, z_send, z_recv, back_send, back_recv
):
    ep = z_send.shape[0] + 1
    f, c, t = lax.axis_index("fsdp"), lax.axis_index("ctx"), lax.axis_index("tp")
    tokens = sum_ref.shape[0]
    half = tokens // 2

    def peer(distance):
        return lax.rem(f + distance, ep)

    def place(fsdp, part):
        return pl.ds(pl.multiple_of(fsdp * tokens + part * half, 16), half)

    core = at_device(f, c, 1 - t)
    greet([at_device(peer(d), c, t) for d in range(1, ep)] + [core])
    sent = []
    order = list(range(1, ep)) + [0]
    for d in order:
        copy = remote(
            part_ref.at[place(peer(d), 1 - t)], core_in.at[d], core_send.at[d], core_recv.at[d], core
        )
        copy.start()
        sent.append(copy)
    for d in order:
        remote(core_in.at[d], core_in.at[d], core_send.at[d], core_recv.at[d], core).wait_recv()
        added = part_ref[place(peer(d), t), :].astype(jnp.float32) + core_in[d].astype(jnp.float32)
        if d == 0:
            total = added
            continue
        z_out[d - 1] = added.astype(z_out.dtype)
        copy = remote(
            z_out.at[d - 1], z_in.at[d - 1], z_send.at[d - 1], z_recv.at[d - 1], at_device(peer(d), c, t)
        )
        copy.start()
        sent.append(copy)
    for d in range(1, ep):
        remote(z_in.at[d - 1], z_in.at[d - 1], z_send.at[d - 1], z_recv.at[d - 1], core).wait_recv()
        total = total + z_in[d - 1].astype(jnp.float32)
    rows = pl.ds(pl.multiple_of(t * half, 16), half)
    sum_ref[rows, :] = total
    copy = remote(sum_ref.at[rows], sum_ref.at[rows], back_send, back_recv, core)
    copy.start()
    other = sum_ref.at[pl.ds(pl.multiple_of((1 - t) * half, 16), half)]
    remote(other, other, back_send, back_recv, core).wait_recv()
    sent.append(copy)
    for copy in sent:
        copy.wait_send()


def sum_z(part, collective_id):
    ep = lax.axis_size("fsdp")
    tokens = part.shape[0] // ep
    width = part.shape[1]
    dma = pltpu.SemaphoreType.DMA
    vmem = pl.BlockSpec(memory_space=pltpu.VMEM)
    return pl.pallas_call(
        sum_z_kernel,
        out_shape=jax.ShapeDtypeStruct((tokens, width), jnp.float32),
        in_specs=[vmem],
        out_specs=vmem,
        scratch_shapes=[
            pltpu.VMEM((ep, tokens // 2, width), part.dtype),
            pltpu.VMEM((ep - 1, tokens // 2, width), part.dtype),
            pltpu.VMEM((ep - 1, tokens // 2, width), part.dtype),
            dma((ep,)),
            dma((ep,)),
            dma((ep - 1,)),
            dma((ep - 1,)),
            dma,
            dma,
        ],
        compiler_params=pltpu.CompilerParams(
            collective_id=collective_id, has_side_effects=True, vmem_limit_bytes=40 * 1024 * 1024
        ),
        name="sum_z",
    )(part)


def pair_kernel(part_ref, sum_ref, other, send, recv):
    f, c, t = lax.axis_index("fsdp"), lax.axis_index("ctx"), lax.axis_index("tp")
    core = at_device(f, c, 1 - t)
    greet([core])
    copy = remote(part_ref, other, send, recv, core)
    copy.start()
    copy.wait()
    sum_ref[...] = part_ref[...].astype(jnp.float32) + other[...].astype(jnp.float32)


def add_pair(part, collective_id):
    dma = pltpu.SemaphoreType.DMA
    vmem = pl.BlockSpec(memory_space=pltpu.VMEM)
    return pl.pallas_call(
        pair_kernel,
        out_shape=jax.ShapeDtypeStruct(part.shape, jnp.float32),
        in_specs=[vmem],
        out_specs=vmem,
        scratch_shapes=[pltpu.VMEM(part.shape, part.dtype), dma, dma],
        compiler_params=pltpu.CompilerParams(
            collective_id=collective_id, has_side_effects=True, vmem_limit_bytes=32 * 1024 * 1024
        ),
        name="add_pair",
    )(part)


def scatter_kernel(
    part_ref, sum_ref, first_in_x, first_in_y, second_out_x, second_out_y, second_in_x, second_in_y, z_out, z_in,
    first_send, first_recv, second_send, second_recv, z_send, z_recv,
):
    ep = z_send.shape[0] + 1
    f, c, t = lax.axis_index("fsdp"), lax.axis_index("ctx"), lax.axis_index("tp")
    rows, width = sum_ref.shape
    first_in, second_out, second_in = (first_in_x, first_in_y), (second_out_x, second_out_y), (second_in_x, second_in_y)
    cut = first_in_x.shape[-1]
    columns = (pl.ds(0, cut), pl.ds(cut, width - cut))
    low = part_ref.dtype

    def peer(distance):
        return lax.rem(f + distance, ep)

    def block(distance, ctx, way):
        start = pl.multiple_of((peer(distance) * 4 + ctx) * rows, 16)
        return pl.ds(start, rows), columns[way]

    neighbours = (at_device(f, c ^ 1, t), at_device(f, c ^ 2, t))
    greet([at_device(peer(d), c, t) for d in range(1, ep)] + list(neighbours))
    sent = []
    order = list(range(1, ep)) + [0]
    for d in order:
        for number in range(2):
            for way in range(2):
                target = c ^ 3 if number == 0 else c ^ (1 << way)
                copy = remote(
                    part_ref.at[block(d, target, way)], first_in[way].at[d, number],
                    first_send.at[way, d, number], first_recv.at[way, d, number], neighbours[way],
                )
                copy.start()
                sent.append(copy)
    for d in order:
        for way in range(2):
            for number in range(2):
                landing = first_in[way].at[d, number]
                remote(
                    landing, landing, first_send.at[way, d, number], first_recv.at[way, d, number], neighbours[way]
                ).wait_recv()
                if number == 0:
                    own = part_ref[block(d, c ^ (2 >> way), way)]
                    second_out[way][d] = (
                        own.astype(jnp.float32) + first_in[way][d, 0].astype(jnp.float32)
                    ).astype(low)
                    copy = remote(
                        second_out[way].at[d], second_in[way].at[d],
                        second_send.at[way, d], second_recv.at[way, d], neighbours[1 - way],
                    )
                    copy.start()
                    sent.append(copy)
    for d in order:
        for way in range(2):
            landing = second_in[way].at[d]
            remote(
                landing, landing, second_send.at[way, d], second_recv.at[way, d], neighbours[1 - way]
            ).wait_recv()
            total = (
                part_ref[block(d, c, way)].astype(jnp.float32)
                + first_in[way][d, 1].astype(jnp.float32)
                + second_in[way][d].astype(jnp.float32)
            )
            if d == 0:
                sum_ref[:, columns[way]] = total
            else:
                z_out[d - 1, :, columns[way]] = total.astype(low)
        if d > 0:
            copy = remote(
                z_out.at[d - 1], z_in.at[d - 1], z_send.at[d - 1], z_recv.at[d - 1], at_device(peer(d), c, t)
            )
            copy.start()
            sent.append(copy)
    for d in range(1, ep):
        remote(z_in.at[d - 1], z_in.at[d - 1], z_send.at[d - 1], z_recv.at[d - 1], neighbours[0]).wait_recv()
        sum_ref[...] += z_in[d - 1].astype(jnp.float32)
    for copy in sent:
        copy.wait_send()


def scatter_sums(part, collective_id):
    ep = lax.axis_size("fsdp")
    rows = part.shape[0] // (ep * lax.axis_size("ctx"))
    width = part.shape[1]
    low = part.dtype
    cut = -(-width // 256) * 128
    dma = pltpu.SemaphoreType.DMA
    vmem = pl.BlockSpec(memory_space=pltpu.VMEM)
    return pl.pallas_call(
        scatter_kernel,
        out_shape=jax.ShapeDtypeStruct((rows, width), jnp.float32),
        in_specs=[vmem],
        out_specs=vmem,
        scratch_shapes=[
            pltpu.VMEM((ep, 2, rows, cut), low),
            pltpu.VMEM((ep, 2, rows, width - cut), low),
            pltpu.VMEM((ep, rows, cut), low),
            pltpu.VMEM((ep, rows, width - cut), low),
            pltpu.VMEM((ep, rows, cut), low),
            pltpu.VMEM((ep, rows, width - cut), low),
            pltpu.VMEM((ep - 1, rows, width), low),
            pltpu.VMEM((ep - 1, rows, width), low),
            dma((2, ep, 2)),
            dma((2, ep, 2)),
            dma((2, ep)),
            dma((2, ep)),
            dma((ep - 1,)),
            dma((ep - 1,)),
        ],
        compiler_params=pltpu.CompilerParams(
            collective_id=collective_id, has_side_effects=True, vmem_limit_bytes=48 * 1024 * 1024
        ),
        name="scatter_sums",
    )(part)


def shards(
    layer_input,
    segments,
    routes,
    norm_gain,
    query_weight,
    key_weight,
    value_weight,
    output_weight,
    ffn_gain,
    router_weight,
    gate_weight,
    up_weight,
    down_weight,
    cotangent,
):
    low = jnp.bfloat16
    both = ("fsdp", "ctx")
    ep = lax.axis_size("fsdp")
    tokens = layer_input.shape[0]
    seq_len = segments.shape[1]
    rows = query_weight.shape[0]
    width = query_weight.shape[1]
    kv_width = key_weight.shape[1]
    hidden_width = gate_weight.shape[2]
    local = EXPERTS // ep
    span = local * hidden_width

    qkv_width = width + 2 * kv_width
    extra = jnp.concatenate([router_weight, norm_gain[:, None], ffn_gain[:, None]], 1)
    extra = jnp.pad(extra, ((0, 0), (0, 128 - extra.shape[1])))
    attn_shard = jnp.concatenate([query_weight, key_weight, value_weight, extra, output_weight.T], 1)
    down_shard = down_weight.transpose(0, 2, 1)
    routes_all = lax.all_gather(routes, "fsdp", axis=0, tiled=True)
    if lax.axis_size("ctx") == 4:
        attn_full, expert_full, outer_all = gather_all(
            attn_shard, gate_weight, up_weight, down_shard, cotangent
        )
    else:
        attn_full = lax.all_gather(attn_shard, both, axis=0, tiled=True)
        packed = jnp.concatenate([gate_weight, up_weight, down_shard], -1)
        expert_full = spread_experts(packed)
        expert_full = expert_full.reshape(D, local, 3, hidden_width).transpose(0, 2, 1, 3)
        expert_full = expert_full.reshape(D, 3 * span)
        outer_all = lax.all_gather(cotangent, "fsdp", axis=0, tiled=True)
    qkv_full = attn_full[:, :qkv_width]
    router_full = attn_full[:, qkv_width : qkv_width + EXPERTS]
    gain_one = attn_full[:, qkv_width + EXPERTS]
    gain_two = attn_full[:, qkv_width + EXPERTS + 1]
    output_turned = attn_full[:, qkv_width + 128 :]
    gate_up = expert_full[:, : 2 * span]
    down_turned = expert_full[:, 2 * span :]

    begin = lax.axis_index("ctx") * tokens
    segment_row = segments[0]
    place = lax.dynamic_slice_in_dim(document_place(segment_row), begin, tokens)
    query_doc = lax.dynamic_slice_in_dim(segment_row, begin, tokens)
    query_order = begin + jnp.arange(tokens, dtype=jnp.int32)
    scale = HD ** (-0.5)
    inputs = layer_input.astype(jnp.float32)
    first_norm, first_inverse = normalize(inputs, gain_one)
    normed1 = first_norm.astype(low)
    projected = jnp.dot(normed1, qkv_full, preferred_element_type=jnp.float32)
    query = rotate(projected[:, :width], place, 1.0).astype(low)
    key = rotate(projected[:, width : width + kv_width], place, 1.0).astype(low)
    value = projected[:, width + kv_width :].astype(low)
    key_groups = kv_width // HD
    groups = width // kv_width
    grouped = query.reshape(tokens, key_groups, groups, HD)
    pair_all = lax.all_gather(jnp.concatenate([key, value], 1), "ctx", axis=0, tiled=True)
    key_all = pair_all[:, :kv_width]
    value_all = pair_all[:, kv_width:]

    def block_scores(key_piece, offset):
        count = key_piece.shape[0]
        key_heads = key_piece.reshape(count, key_groups, HD)
        scores = (
            jnp.einsum("qkgd,nkd->qkgn", grouped, key_heads, preferred_element_type=jnp.float32)
            * scale
        )
        key_doc = lax.dynamic_slice_in_dim(segment_row, offset, count)
        key_order = offset + jnp.arange(count, dtype=jnp.int32)
        seen = (key_doc[None, :] == query_doc[:, None]) & (
            key_order[None, :] <= query_order[:, None]
        )
        return (scores, seen[:, None, None, :], key_heads)

    def masked_away(offset, count):
        last_doc = lax.dynamic_index_in_dim(segment_row, offset + count - 1, keepdims=False)
        return (offset > query_order[tokens - 1]) | (last_doc < query_doc[0])

    scores, seen, key_heads = block_scores(key_all, jnp.int32(0))
    scores = jnp.where(seen, scores, MASKED_SCORE)
    running = jnp.max(scores, -1)
    weights = jnp.where(seen, jnp.exp(scores - running[..., None]), 0.0)
    summed = jnp.einsum(
        "qkgn,nkd->qkgd",
        weights.astype(low),
        value_all.reshape(seq_len, key_groups, HD),
        preferred_element_type=jnp.float32,
    )
    totals = jnp.sum(weights, -1)
    mixed = summed / totals[..., None]
    log_total = running + jnp.log(totals)
    mixed_low = mixed.reshape(tokens, -1).astype(low)
    attention = add_pair(times_transpose(mixed_low, output_turned).astype(low), 3)
    middle = inputs + attention
    second_norm, second_inverse = normalize(middle, gain_two)
    normed2 = second_norm.astype(low)

    normed2_all = along_z(normed2)
    logits_all = jnp.dot(normed2_all, router_full, preferred_element_type=jnp.float32)
    expert_ids = jnp.arange(EXPERTS, dtype=jnp.int32)
    chosen_all = jnp.any(routes_all[:, :, None] == expert_ids[None, None, :], 1)
    masked_logits = jnp.where(chosen_all, logits_all, MASKED_SCORE)
    top = jnp.max(masked_logits, -1, keepdims=True)
    lifted = jnp.where(chosen_all, jnp.exp(masked_logits - top), 0.0)
    gates_all = lifted / jnp.sum(lifted, -1, keepdims=True)
    place_z = lax.axis_index("fsdp")
    gates_here = lax.dynamic_slice_in_dim(gates_all, place_z * local, local, 1)
    chosen_here = lax.dynamic_slice_in_dim(chosen_all, place_z * local, local, 1)
    chosen = lax.dynamic_slice_in_dim(chosen_all, place_z * tokens, tokens, 0)
    gates = lax.dynamic_slice_in_dim(gates_all, place_z * tokens, tokens, 0)

    reach = normed2_all.shape[0]
    both_sides = jnp.dot(normed2_all, gate_up, preferred_element_type=jnp.float32)
    former = both_sides[:, :span]
    latter = both_sides[:, span:]
    hidden_grad = jnp.dot(outer_all, down_turned, preferred_element_type=jnp.float32)
    gate_wide = jnp.broadcast_to(gates_here[:, :, None], (reach, local, hidden_width)).reshape(reach, span)
    logistic = jax.nn.sigmoid(former)
    active = former * logistic
    hidden = (active * latter).astype(low).astype(jnp.float32)
    gated = (hidden * gate_wide).astype(low)
    dgates = jnp.sum((hidden * hidden_grad).reshape(reach, local, hidden_width), -1)
    scaled_grad = hidden_grad * gate_wide
    former_grad = (scaled_grad * latter * logistic * (1.0 + former * (1.0 - logistic))).astype(low)
    latter_grad = (scaled_grad * active).astype(low)
    side_grads = jnp.concatenate([former_grad, latter_grad], 1)
    mixture_part = times_transpose(gated, down_turned)
    input_part = times_transpose(side_grads, gate_up)
    side_sums = contract_rows(normed2_all, side_grads)
    down_sums = contract_rows(outer_all, gated)
    dgates = jnp.where(chosen_here, dgates, 0.0)
    dgates_wide = lax.dynamic_update_slice_in_dim(
        jnp.zeros((reach, EXPERTS), jnp.float32), dgates, place_z * local, 1
    )
    dgates_high = dgates_wide.astype(low)
    dgates_rest = (dgates_wide - dgates_high.astype(jnp.float32)).astype(low)
    dgates_sent = jnp.concatenate([dgates_high, dgates_rest], 1)
    dgates_sent = jnp.pad(dgates_sent, ((0, 0), (0, 128 - 2 * EXPERTS)))
    returned = sum_z(jnp.concatenate([input_part.astype(low), dgates_sent], 1), 4)
    mixture = lax.psum_scatter(
        lax.psum(mixture_part.astype(low), "tp"), "fsdp", scatter_dimension=0, tiled=True
    ).astype(jnp.float32)
    layer_output = (middle + mixture).astype(low)
    side_out = collect_experts(side_sums.astype(low), rows).reshape(ep, rows, 2, local, hidden_width)
    side_out = side_out.transpose(2, 0, 3, 1, 4).reshape(2, EXPERTS, rows, hidden_width).astype(jnp.float32)
    down_out = collect_experts(down_sums.astype(low), rows).reshape(ep, rows, local, hidden_width)
    down_out = down_out.transpose(0, 2, 3, 1).reshape(EXPERTS, hidden_width, rows).astype(jnp.float32)

    outer_grad = cotangent.astype(jnp.float32)
    input_grad_part = returned[:, :D]
    picked = returned[:, D : D + EXPERTS] + returned[:, D + EXPERTS : D + 2 * EXPERTS]
    logit_grad = (gates * (picked - jnp.sum(gates * picked, -1, keepdims=True))).astype(low)
    router_sums = contract_rows(normed2, logit_grad)
    second_grad = input_grad_part + times_transpose(logit_grad, router_full)
    middle_back, gain_two_sums = norm_back(second_grad, middle, second_inverse, gain_two)
    middle_grad = outer_grad + middle_back
    attention_grad = middle_grad.astype(low)
    output_sums = contract_rows(attention_grad, mixed_low)
    mixed_grad = jnp.dot(attention_grad, output_turned, preferred_element_type=jnp.float32).astype(low)
    mixed_heads = mixed_grad.reshape(tokens, key_groups, groups, HD)
    delta = jnp.sum(mixed_heads.astype(jnp.float32) * mixed, -1)

    def back_two(number, state):
        offset = number * tokens
        key_piece = lax.dynamic_slice_in_dim(key_all, offset, tokens, 0)
        value_piece = lax.dynamic_slice_in_dim(value_all, offset, tokens, 0)

        def back_compute(inner):
            query_sum, pair_sum = inner
            scores, seen, key_heads = block_scores(key_piece, offset)
            probs = jnp.where(seen, jnp.exp(scores - log_total[..., None]), 0.0)
            value_heads = value_piece.reshape(tokens, key_groups, HD)
            prob_grad = jnp.einsum(
                "qkgd,nkd->qkgn", mixed_heads, value_heads, preferred_element_type=jnp.float32
            )
            score_grad = (probs * (prob_grad - delta[..., None])).astype(low)
            query_sum = (
                query_sum
                + jnp.einsum(
                    "qkgn,nkd->qkgd", score_grad, key_heads, preferred_element_type=jnp.float32
                )
                * scale
            )
            key_block = (
                jnp.einsum(
                    "qkgn,qkgd->nkd", score_grad, grouped, preferred_element_type=jnp.float32
                )
                * scale
            )
            value_block = jnp.einsum(
                "qkgn,qkgd->nkd", probs.astype(low), mixed_heads, preferred_element_type=jnp.float32
            )
            pair = jnp.concatenate([key_block.reshape(tokens, -1), value_block.reshape(tokens, -1)], 1)
            return (query_sum, lax.dynamic_update_slice_in_dim(pair_sum, pair, offset, 0))

        return lax.cond(masked_away(offset, tokens), lambda inner: inner, back_compute, state)

    back_state = (
        jnp.zeros((tokens, key_groups, groups, HD), jnp.float32),
        jnp.zeros((seq_len, 2 * kv_width), jnp.float32),
    )
    query_sum, pair_sum = lax.fori_loop(0, seq_len // tokens, back_two, back_state)
    pair_local = lax.psum_scatter(
        pair_sum.astype(low), "ctx", scatter_dimension=0, tiled=True
    ).astype(jnp.float32)
    query_back = rotate(query_sum.reshape(tokens, -1), place, -1.0)
    key_back = rotate(pair_local[:, :kv_width], place, -1.0)
    qkv_back = jnp.concatenate([query_back, key_back, pair_local[:, kv_width:]], 1).astype(low)
    qkv_sums = contract_rows(normed1, qkv_back)
    first_part = times_transpose(qkv_back, qkv_full)
    first_grad = add_pair(first_part.astype(low), 5)
    input_back, gain_one_sums = norm_back(first_grad, inputs, first_inverse, gain_one)
    input_grad = middle_grad + input_back
    small_sums = jnp.concatenate([router_sums, gain_one_sums[:, None], gain_two_sums[:, None]], 1)
    small_sums = jnp.pad(small_sums, ((0, 0), (0, 128 - small_sums.shape[1])))
    attn_sums = jnp.concatenate([qkv_sums.astype(low), small_sums.astype(low), output_sums.astype(low)], 1)
    if lax.axis_size("ctx") == 4:
        attn_out = scatter_sums(attn_sums, 6)
    else:
        attn_out = lax.psum_scatter(attn_sums, both, scatter_dimension=0, tiled=True).astype(jnp.float32)
    small_out = attn_out[:, qkv_width : qkv_width + 128]
    return (
        layer_output,
        input_grad,
        small_out[:, EXPERTS],
        attn_out[:, :width],
        attn_out[:, width : width + kv_width],
        attn_out[:, width + kv_width : qkv_width],
        attn_out[:, qkv_width + 128 :].T,
        small_out[:, EXPERTS + 1],
        small_out[:, :EXPERTS],
        side_out[0],
        side_out[1],
        down_out,
    )


def solution(mesh):
    in_specs = (
        P(("fsdp", "ctx"), None),
        P("fsdp", None),
        P(("fsdp", "ctx"), None),
        P(("fsdp", "ctx")),
        P(("fsdp", "ctx"), "tp"),
        P(("fsdp", "ctx"), "tp"),
        P(("fsdp", "ctx"), "tp"),
        P("tp", ("fsdp", "ctx")),
        P(("fsdp", "ctx")),
        P(("fsdp", "ctx"), None),
        P(None, ("fsdp", "ctx"), "tp"),
        P(None, ("fsdp", "ctx"), "tp"),
        P(None, "tp", ("fsdp", "ctx")),
        P(("fsdp", "ctx"), None),
    )
    out_specs = (
        P(("fsdp", "ctx"), None),
        P(("fsdp", "ctx"), None),
        P(("fsdp", "ctx")),
        P(("fsdp", "ctx"), "tp"),
        P(("fsdp", "ctx"), "tp"),
        P(("fsdp", "ctx"), "tp"),
        P("tp", ("fsdp", "ctx")),
        P(("fsdp", "ctx")),
        P(("fsdp", "ctx"), None),
        P(None, ("fsdp", "ctx"), "tp"),
        P(None, ("fsdp", "ctx"), "tp"),
        P(None, "tp", ("fsdp", "ctx")),
    )
    return jax.shard_map(shards, mesh=mesh, in_specs=in_specs, out_specs=out_specs, check_vma=False)
```

time: 2810 us -> 718 us (0.26)
  waiting for transfers between devices: 2100 us -> 150 us
  Pallas kernels: 0 us -> 334 us
  blocking collectives: 216 us -> 9.83 us
  other arithmetic: 130 us -> 34.4 us
  matrix products: 182 us -> 90.7 us
  local copies, waits for them, and re-layouts: 140 us -> 59 us
    reduce_scatter x9 -> x4, waiting for transfers between devices: 1610 us -> 123 us  [the longest x2 61.5 us: collect_experts(): mine = lax.psum_scatter(turned, 'ctx', scatter_dimension=0, tiled=True)]
    all_gather x5 -> x1, waiting for transfers between devices: 375 us -> 14.7 us  [shards(): lax.all_gather(jnp.concatenate([key, value], 1), 'ctx', axis=0, tiled=True)]
    pallas_call x0 -> x6, Pallas kernels: none -> 334 us  [the longest x1 158 us: gather_all(): pl.pallas_call(gather_kernel, out_shape=(jax.ShapeDtypeStruct((total, att...]
    all_gather x5 -> x1, blocking collectives: 126 us -> 9.83 us  [shards(): routes_all = lax.all_gather(routes, 'fsdp', axis=0, tiled=True)]
    dot_general x16 -> x7, matrix products: 149 us -> 36.8 us  [the longest x1 12.5 us: shards(): jnp.dot(normed2_all, gate_up, preferred_element_type=jnp.float32)]
    unnamed x2 -> x0, blocking collectives: 87.3 us -> none
    gather x12 -> x0, local copies, waits for them, and re-layouts: 85 us -> none  [the longest x2 20.2 us: shards(): jnp.concatenate([gate_table, jnp.zeros((1, EXPERTS), jnp.float32)], 0)]
    unnamed x19 -> x6, waiting for transfers between devices: 72.2 us -> 0.1 us
  transfers between devices with their start and end apart: 18 -> 8, of which waited for: 14 -> 5; matrix products, arithmetic and copies ran while one was open for 9% -> 15% of each run, Pallas kernels for 0% -> 19%
where the time goes in v1:
time: 718 us; the launch traced here: 711 us
  Pallas kernels  334 us (47%)
  waiting for transfers between devices  150 us (21%)
  matrix products  90.7 us (13%)
  local copies, waits for them, and re-layouts  59 us (8%)
  other arithmetic  34.4 us (5%)
  between operations  15.1 us (2%)
  blocking collectives  9.83 us (1%)
  starting transfers between devices  9.38 us (1%)
  loops' own time  8.07 us (1%)
    pallas_call x1, Pallas kernels, gather_all(): pl.pallas_call(gather_kernel, out_shape=(jax.ShapeDtypeStruct((total, att...  158 us
    pallas_call x1, Pallas kernels, scatter_sums(): pl.pallas_call(scatter_kernel, out_shape=jax.ShapeDtypeStruct((rows, widt...  85.7 us
    reduce_scatter x2, waiting for transfers between devices, collect_experts(): mine = lax.psum_scatter(turned, 'ctx', scatter_dimension=0, tiled=True)  61.5 us
    reduce_scatter x1, waiting for transfers between devices, shards(): lax.psum_scatter(lax.psum(mixture_part.astype(low), 'tp'), 'fsdp', scatte...  59.9 us
    pallas_call x1, Pallas kernels, sum_z(): pl.pallas_call(sum_z_kernel, out_shape=jax.ShapeDtypeStruct((tokens, widt...  44.9 us
    pallas_call x1, Pallas kernels, along_z(): pl.pallas_call(along_z_kernel, out_shape=jax.ShapeDtypeStruct((ep * mine....  39.8 us
    dot_general x5, matrix products, contract_rows(): lax.dot_general(left, right, (((0,), (0,)), ((), ())), preferred_element_...  25.1 us
    dot_general x5, matrix products, times_transpose(): lax.dot_general(left, right, (((1,), (1,)), ((), ())), preferred_element_...  24.2 us
  transfers between devices with their start and end apart: 8, of which 5 were waited for; matrix products, arithmetic and copies ran while one was open for 15% of the time, Pallas kernels for 19%

profile of v1, /device:TPU:9, one launch (start us, length us, event | category | flops | bytes accessed | tf_op | source)
XLA Modules:
  0.0 710.9 jit_solution(11462327924831420903)
XLA Ops:
  7.3 1.0 constant_dynamic-update-slice_fusion.2
  12.4 158.4 %gather_all.1 = (bf16[1536,2176]{1,0:T(8,128)(2,1)}, bf16[1536,3072]{1,0:T(8,128)(2,1)}, bf16[1024,1536]{1,0:T(8,128)(2,1)}) custom-call(bf16[96,2176]{1,0:T(8,128)(2,1)} %copy-done.13, bf16[16,96,256]{2,1,0:T(8,128)(2,1)} %gate_ref.1, bf16[16,96,256]{2,1,0:T(8,128)(2,1)} %up_ref.1, bf16[16,96,256]{2,1,0:T(8,128)(2,1)} %bitcast.177, bf16[256,1536]{1,0:T(8,128)(2,1)} %outer_ref.1), custom_call_target="tpu_custom_call" | custom-call | tf_op jit(solution)/shard_map/gather_all/pallas_call | solution.py:258
  170.8 1.7 convert_reduce_fusion
  173.4 3.4 fusion.34
  176.8 1.0 copy-done.8
  180.6 1.2 slice.205
  182.1 9.8 %all_gather.7 = s32[1024,8]{0,1:T(8,128)S(1)} all-gather(s32[256,8]{0,1:T(8,128)S(1)} %copy-done.26), channel_id=1, replica_groups=mesh['fsdp'=4,'ctx'=4,'tp'=2] {'fsdp'}, dimensions={0}, use_global_device_ids=true | all-gather | bytes 40960 | tf_op jit(solution)/shard_map/all_gather | solution.py:591
  192.7 14.7 %all-gather.2.cloned.1.call-done = bf16[1024,512]{1,0:T(8,128)(2,1)} async-done(((bf16[256,512]{1,0:T(8,128)(2,1)}), bf16[1024,512]{1,0:T(8,128)(2,1)}) %all-gather.2.cloned.1.call-update) | async-done | bytes 1048592 | tf_op jit(solution)/shard_map/all_gather | solution.py:627
  207.3 1.3 fusion.86
  209.0 2.0 fusion.15
  211.0 3.4 fusion.16
  214.4 4.2 fusion.89
  218.6 2.6 convolution_convert_fusion.5.part_ref
  221.3 2.8 add_pair.2
  224.4 1.1 multiply_convert_fusion.3.mine_ref
  225.5 39.8 %along_z.1 = bf16[1024,1536]{1,0:T(8,128)(2,1)} custom-call(bf16[256,1536]{1,0:T(8,128)(2,1)} %multiply_convert_fusion.3.mine_ref), custom_call_target="tpu_custom_call" | custom-call | tf_op jit(solution)/shard_map/along_z/pallas_call | solution.py:327
  265.3 3.0 fusion.90
  270.0 1.2 broadcast_in_dim.129
  271.3 1.0 copy.208
  273.2 12.5 %fusion.25 = f32[1024,2048]{1,0:T(8,128)} fusion(bf16[1024,1536]{1,0:T(8,128)(2,1)S(1)} %copy-done.6, bf16[1536,3072]{1,0:T(8,128)(2,1)} %get-tuple-element.550), kind=kOutput, calls=%fused_computation.38 | convolution fusion | flops 6442450944 | bytes 17825792 | tf_op jit(solution)/shard_map/dot_general | solution.py:683
  285.7 9.7 %multiply_convert_fusion.1 = (bf16[1024,1024]{1,0:T(8,128)(2,1)}, bf16[1024,1024]{1,0:T(8,128)(2,1)}, f32[1024,1024]{1,0:T(8,128)}, bf16[1024,1024]{1,0:T(8,128)(2,1)S(1)}) fusion(f32[1024,2048]{1,0:T(8,128)} %fusion.25, f32[1024,1024]{1,0:T(8,128)S(1)} %bitcast.160, bf16[1024,1536]{1,0:T(8,128)(2,1)S(1)} %copy-done.28, bf16[1536,3072]{1,0:T(8,128)(2,1)S(1)} %bitcast.192), kind=kOutput, calls=%fused_computation.45 | convolution fusion | flops 3240099840 | bytes 29360128 | tf_op jit(solution)/shard_map/dot_general | solution.py:686
  295.5 1.3 copy-done.29
  296.8 5.4 convolution_convert_fusion.3
  302.2 59.9 %reduce-scatter.11.cloned.1.call-done = bf16[256,1536]{1,0:T(8,128)(2,1)} async-done(((bf16[1024,1536]{1,0:T(8,128)(2,1)}), bf16[256,1536]{1,0:T(8,128)(2,1)}) %reduce-scatter.11.cloned.1.call-update) | async-done | bytes 786448 | tf_op jit(solution)/shard_map/reduce_scatter | solution.py:710
  362.1 7.2 %convolution_convert_fusion.2 = bf16[1536,1024]{1,0:T(8,128)(2,1)S(1)} fusion(bf16[1024,1536]{1,0:T(8,128)(2,1)} %get-tuple-element.551, f32[1024,1024]{1,0:T(8,128)} %bitcast.162, bf16[1024,1024]{1,0:T(8,128)(2,1)} %copy-done.29), kind=kOutput, calls=%fused_computation.50 | convolution fusion | flops 3225944064 | bytes 12582912 | tf_op jit(solution)/shard_map/dot_general | solution.py:54
  369.4 2.1 copy.191
  371.5 5.6 reshape.383
  377.1 4.2 reduce_sum.103
  381.3 2.1 dynamic-slice_select_fusion
  384.2 3.4 dynamic_update_slice.9
  387.6 1.4 subtract_convert_fusion
  389.2 10.1 %fusion.29 = bf16[1024,1536]{1,0:T(8,128)(2,1)S(1)} fusion(bf16[1536,3072]{1,0:T(8,128)(2,1)} %get-tuple-element.550, bf16[1024,1024]{1,0:T(8,128)(2,1)} %get-tuple-element.739, bf16[1024,1024]{1,0:T(8,128)(2,1)} %get-tuple-element.738), kind=kOutput, calls=%fused_computation.49 | convolution fusion | flops 6452412416 | bytes 13631488 | tf_op jit(solution)/shard_map/dot_general | solution.py:60
  399.6 44.9 %sum_z.1 = f32[256,1664]{1,0:T(8,128)S(1)} custom-call(bf16[1024,1664]{1,0:T(8,128)(2,1)S(1)} %pad_maximum_fusion.1.part_ref), custom_call_target="tpu_custom_call" | custom-call | tf_op jit(solution)/shard_map/sum_z/pallas_call | solution.py:394
  444.9 2.7 multiply_reduce_fusion
  447.6 3.2 subtract_add_fusion
  450.9 1.1 copy-done.1
  452.0 3.2 fusion.57
  455.2 1.2 copy.182
  456.5 1.1 broadcast_in_dim.132
  457.7 20.1 %while.19 = (s32[]{:T(128)}, f32[256,4,3,64]{0,3,2,1:T(8,128)S(1)}, bf16[1024,512]{0,1:T(8,128)(2,1)}, s32[256]{0:T(256)S(1)}, s32[1024]{0:T(1024)S(1)}, /*index...) while((s32[]{:T(128)}, f32[256,4,3,64]{0,3,2,1:T(8,128)S(1)}, ...), condition=%wide.region_18.19_spmd, body=%wide.region_15.18_spmd.sunk | while | flops 512426240 | bytes 19246536 | solution.py:772
  461.3 5.3 conditional.2
  463.1 1.1 fusion.1
  477.8 9.9 %convolution_convert_fusion = bf16[1536,2048]{1,0:T(8,128)(2,1)S(1)} fusion(bf16[1024,1536]{1,0:T(8,128)(2,1)} %along_z.1, bf16[1024,1024]{1,0:T(8,128)(2,1)} %get-tuple-element.739, bf16[1024,1024]{1,0:T(8,128)(2,1)} %get-tuple-element.738), kind=kOutput, calls=%fused_computation.30 | convolution fusion | flops 6453985280 | bytes 13631488 | tf_op jit(solution)/shard_map/dot_general | solution.py:54
  487.7 3.3 copy.188
  491.1 4.4 all-to-all-start.1
  495.5 2.1 convolution_convert_fusion.6
  497.7 2.3 convolution_convert_fusion.4
  500.0 12.5 %all-to-all-done.1 = bf16[4,96,1024]{2,1,0:T(8,128)(2,1)} async-done(((bf16[4,96,1024]{2,1,0:T(8,128)(2,1)}), bf16[4,96,1024]{2,1,0:T(8,128)(2,1)}, u32[]{:S(2)}, u32[]{:S(2)}) %all-to-all-start.1) | async-done | bytes 786464 | tf_op jit(solution)/shard_map/all_to_all | solution.py:80
  512.6 1.9 reshape.399
  514.5 1.4 copy.192
  515.9 1.3 reduce-scatter.5.cloned.1.call-done
  517.2 1.0 fusion.88
  518.4 3.3 fusion.39.part_ref
  521.7 2.8 add_pair.3
  525.3 3.6 convolution_convert_fusion.1
  528.8 61.5 %reduce-scatter.7.cloned.1.call-done = bf16[384,2048]{1,0:T(8,128)(2,1)} async-done(((bf16[1536,2048]{1,0:T(8,128)(2,1)}), bf16[384,2048]{1,0:T(8,128)(2,1)}) %reduce-scatter.7.cloned.1.call-update) | async-done | bytes 1572880 | tf_op jit(solution)/shard_map/reduce_scatter | solution.py:79
  590.3 4.8 all-to-all-start
  595.1 6.5 fusion.19.part_ref
  601.6 85.7 %scatter_sums.1 = f32[96,2176]{1,0:T(8,128)S(1)} custom-call(bf16[1536,2176]{1,0:T(8,128)(2,1)} %fusion.19.part_ref), custom_call_target="tpu_custom_call" | custom-call | tf_op jit(solution)/shard_map/scatter_sums/pallas_call | solution.py:530
  690.2 3.2 fusion.50
  693.4 5.1 reshape.398
  698.5 2.4 fusion.85
  700.9 1.4 copy.189
  702.4 1.4 copy.190
  (168 shorter events, 28.9 us)
Async XLA Ops:
  7.2 165.4 %copy-start = (bf16[256,1536]{1,0:T(8,128)(2,1)S(1)}, bf16[256,1536]{1,0:T(8,128)(2,1)}, u32[]{:S(2)}) copy-start(bf16[256,1536]{1,0:T(8,128)(2,1)} %param.18) | copy-start | bytes 2359300
  7.2 200.1 %all-gather.2.cloned.1.call-start = ((), (), s32[]{:S(2)}) async-start(), calls=%async_computation.6 | async-start | bytes 1310720 | tf_op jit(solution)/shard_map/all_gather | solution.py:627
  11.6 0.8 copy-start.13
  172.5 4.2 copy-start.20
  173.4 3.4 copy-start.24
  173.4 4.6 copy-start.23
  176.8 1.1 copy-start.8
  176.8 5.3 copy-start.26
  179.7 12.7 %copy-start.9 = (f32[256,32]{0,1:T(8,128)}, f32[256,32]{0,1:T(8,128)S(1)}, u32[]{:S(2)}) copy-start(f32[256,32]{0,1:T(8,128)S(1)} %get-tuple-element.764) | copy-start | bytes 98308
  180.6 181.5 %reduce-scatter.11.cloned.1.call-start = ((), (), s32[]{:S(2)}) async-start(), calls=%async_computation.10 | async-start | bytes 3932160 | tf_op jit(solution)/shard_map/reduce_scatter | solution.py:710
  209.0 5.4 copy-start.7
  218.6 2.6 copy-start.16
  269.0 0.8 copy-start.4
  271.3 1.9 copy-start.6
  271.3 14.4 %slice-start = ((s8[9437184]{0:T(1024)(128)(4,1)}), s8[4194304]{0:T(1024)(128)(4,1)S(1)}, s32[]{:S(2)}) async-start(s8[9437184]{0:T(1024)(128)(4,1)} %bitcast.191), calls=%async_computation.12 | async-start | bytes 8388608
  272.3 23.1 %copy-start.3 = (f32[128,8,4,256]{3,1,2,0:T(8,128)}, f32[128,8,4,256]{3,1,2,0:T(8,128)S(1)}, u32[]{:S(2)}) copy-start(f32[128,8,4,256]{3,1,2,0:T(8,128)S(1)} %copy.208) | copy-start | bytes 12582916
  273.2 12.5 %slice-start.1 = ((s8[9437184]{0:T(1024)(128)(4,1)}), s8[4194304]{0:T(1024)(128)(4,1)S(1)}, s32[]{:S(2)}) async-start(s8[9437184]{0:T(1024)(128)(4,1)} %bitcast.191), calls=%async_computation.13 | async-start | bytes 8388608
  273.2 12.5 %slice-start.2 = ((s8[9437184]{0:T(1024)(128)(4,1)}), s8[1048576]{0:T(1024)(128)(4,1)S(1)}, s32[]{:S(2)}) async-start(s8[9437184]{0:T(1024)(128)(4,1)} %bitcast.191), calls=%async_computation.14 | async-start | bytes 2097152
  273.2 12.5 %copy-start.28 = (bf16[1024,1536]{1,0:T(8,128)(2,1)S(1)}, bf16[1024,1536]{1,0:T(8,128)(2,1)}, u32[]{:S(2)}) copy-start(bf16[1024,1536]{1,0:T(8,128)(2,1)} %get-tuple-element.551) | copy-start | bytes 9437188
  295.4 1.3 copy-start.29
  302.2 145.5 %all-reduce.5.cloned.1.call-start = ((), (), s32[]{:S(2)}) async-start(), calls=%async_computation.11 | async-start | bytes 1572864 | tf_op jit(solution)/shard_map/psum | solution.py:711
  362.1 129.0 %reduce-scatter.9.cloned.1.call-start = ((), (), s32[]{:S(2)}) async-start(), calls=%async_computation.9 | async-start | bytes 3932160 | tf_op jit(solution)/shard_map/reduce_scatter | solution.py:79
  371.5 145.8 %reduce-scatter.5.cloned.1.call-start = ((), (), s32[]{:S(2)}) async-start(), calls=%async_computation.7 | async-start | bytes 1310720 | tf_op jit(solution)/shard_map/reduce_scatter | solution.py:773
  399.5 45.0 %copy-start.5 = (f32[1024,16]{1,0:T(8,128)S(1)}, f32[1024,16]{1,0:T(8,128)}, u32[]{:S(2)}) copy-start(f32[1024,16]{1,0:T(8,128)} %copy-done.4) | copy-start | bytes 196612
  444.8 2.7 copy-start.14
  450.9 1.1 copy-start.1
  450.9 5.5 copy-start.12
  477.8 112.5 %reduce-scatter.7.cloned.1.call-start = ((), (), s32[]{:S(2)}) async-start(), calls=%async_computation.8 | async-start | bytes 7864320 | tf_op jit(solution)/shard_map/reduce_scatter | solution.py:79
  491.0 4.5 copy-start.15
  491.0 6.5 copy-start.10
  491.0 6.5 copy-start.18
  491.0 6.7 copy-start.2
  491.1 21.5 %all-to-all-start.1 = ((bf16[4,96,1024]{2,1,0:T(8,128)(2,1)}), bf16[4,96,1024]{2,1,0:T(8,128)(2,1)}, u32[]{:S(2)}, u32[]{:S(2)}) async-start(bf16[4,96,1024]{2,1,0:T(8,128)(2,1)} %bitcast.178), calls=%async_computation.4 | async-start | bytes 1572864 | tf_op jit(solution)/shard_map/all_to_all | solution.py:80
  495.4 2.3 copy-start.17
  500.0 18.2 %copy-start.11 = (f32[256,32]{0,1:T(8,128)S(1)}, f32[256,32]{0,1:T(8,128)}, u32[]{:S(2)}) copy-start(f32[256,32]{0,1:T(8,128)} %copy-done.9) | copy-start | bytes 98308
  500.0 18.2 %copy-start.19 = (f32[256,32]{0,1:T(8,128)S(1)}, f32[256,32]{0,1:T(8,128)}, u32[]{:S(2)}) copy-start(f32[256,32]{0,1:T(8,128)} %get-tuple-element.762) | copy-start | bytes 98308
  518.3 6.2 copy-start.21
  518.4 6.2 copy-start.25
  521.7 3.3 copy-start.22
  590.3 103.1 %all-to-all-start = ((bf16[4,96,2048]{2,1,0:T(8,128)(2,1)}), bf16[4,96,2048]{2,1,0:T(8,128)(2,1)}, u32[]{:S(2)}, u32[]{:S(2)}) async-start(bf16[4,96,2048]{2,1,0:T(8,128)(2,1)} %bitcast.170), calls=%async_computation.2 | async-start | bytes 3145728 | tf_op jit(solution)/shard_map/all_to_all | solution.py:80
  601.6 88.7 %copy-start.27 = (f32[256]{0:T(256)S(1)}, f32[256]{0:T(256)}, u32[]{:S(2)}) copy-start(f32[256]{0:T(256)} %get-tuple-element.765) | copy-start | bytes 3076
Sparse Core Ops, SparseCore 0:
  180.7 26.5 all-gather.1
  302.3 59.7 reduce-scatter.10
  364.4 20.4 all-reduce.4
  388.0 44.4 reduce-scatter.8
  477.9 39.3 reduce-scatter.4
  520.1 70.1 reduce-scatter.6

commit v2 on v1

v2 whole, which is shorter than its diff:
```python
import jax
import jax.numpy as jnp
from jax import lax
from jax.experimental import pallas as pl
from jax.experimental.pallas import tpu as pltpu
from jax.sharding import PartitionSpec as P

MESH = pl.DeviceIdType.MESH

D = 1536
HD = 64
EXPERTS = 16


EPSILON = 1e-05
MASKED_SCORE = -1e30


def rotate(values, cosine, sine):
    rows = values.shape[0]
    shaped = values.reshape(rows, -1, HD)
    half = HD // 2
    cosine, sine = cosine[:, None, :], sine[:, None, :]
    former = shaped[..., :half]
    latter = shaped[..., half:]
    turned = jnp.concatenate([former * cosine - latter * sine, latter * cosine + former * sine], -1)
    return turned.reshape(rows, -1)


def normalize(values, gain):
    inverse = lax.rsqrt(jnp.mean(values * values, -1, keepdims=True) + EPSILON)
    return (values * inverse * gain.astype(jnp.float32), inverse)


def norm_back(grad, values, inverse, gain):
    scaled = grad * gain.astype(jnp.float32)
    gain_grad = jnp.sum(grad * values * inverse, 0)
    mean_term = jnp.mean(scaled * values, -1, keepdims=True)
    return (inverse * scaled - values * inverse**3 * mean_term, gain_grad)


def document_place(segment_row):
    length = segment_row.shape[0]
    order = jnp.arange(length, dtype=jnp.int32)
    fresh = jnp.concatenate([jnp.ones((1,), jnp.bool_), segment_row[1:] != segment_row[:-1]])
    starts = lax.cummax(jnp.where(fresh, order, 0), axis=0)
    return order - starts


def contract_rows(left, right):
    return lax.dot_general(
        left, right, (((0,), (0,)), ((), ())), preferred_element_type=jnp.float32
    )


def times_transpose(left, right):
    return lax.dot_general(
        left, right, (((1,), (1,)), ((), ())), preferred_element_type=jnp.float32
    )


def spread_experts(packed):
    ep = lax.axis_size("fsdp")
    local = packed.shape[0] // ep
    rows = packed.shape[1]
    swapped = lax.all_to_all(packed, "fsdp", 0, 0, tiled=True)
    swapped = swapped.reshape(ep, local, rows, -1).transpose(0, 2, 1, 3)
    swapped = swapped.reshape(ep, rows, -1)
    whole = lax.all_gather(swapped, "ctx", axis=1)
    return whole.reshape(ep * lax.axis_size("ctx") * rows, -1)


def collect_experts(sums, rows):
    ep, ring = lax.axis_size("fsdp"), lax.axis_size("ctx")
    turned = sums.reshape(ep, ring, rows, -1).transpose(1, 0, 2, 3).reshape(sums.shape)
    mine = lax.psum_scatter(turned, "ctx", scatter_dimension=0, tiled=True)
    return lax.all_to_all(mine, "fsdp", 0, 0, tiled=True)


def at_device(fsdp, ctx, tp):
    return {"fsdp": fsdp, "ctx": ctx, "tp": tp}


def greet(partners):
    barrier = pltpu.get_barrier_semaphore()
    for device in partners:
        pl.semaphore_signal(barrier, inc=1, device_id=device, device_id_type=MESH)
    pl.semaphore_wait(barrier, len(partners))


def remote(source, target, send, recv, device):
    return pltpu.make_async_remote_copy(
        src_ref=source, dst_ref=target, send_sem=send, recv_sem=recv, device_id=device, device_id_type=MESH
    )


def lasting(us):
    return pl.CostEstimate(flops=0, bytes_accessed=us * 3690000, transcendentals=0)


def front_kernel(
    attn_ref, gate_ref, up_ref, down_ref, outer_ref, routes_ref, input_ref, segment_ref, freq_ref,
    expert_out, outer_out, routes_out, normed2_out,
    attn_out, normed1_out, query_out, pair_out, mixed_out, log_out, middle_out, cos_out, sin_out,
    query_s, key_s, value_s, mixed_s, bias_s, part_s, other_s, normed2_s,
    local_sem, z_send, z_recv, plane_send, plane_recv, relay_send, relay_recv, core_send, core_recv,
    key_send, key_recv, pair_send, pair_recv,
):
    ep = z_send.shape[1] + 1
    f, c, t = lax.axis_index("fsdp"), lax.axis_index("ctx"), lax.axis_index("tp")
    low = jnp.bfloat16
    rows = attn_ref.shape[0]
    local = gate_ref.shape[0] // ep
    hidden = gate_ref.shape[2]
    tokens = outer_ref.shape[0]
    half = tokens // 2
    heads = query_s.shape[0]
    key_heads = key_s.shape[0]
    width, kv_width = heads * HD, key_heads * HD
    qkv_width = width + 2 * kv_width
    outs = (attn_out, expert_out)
    cuts = [(out.shape[1] // 256) * 128 for out in outs]

    def peer(distance):
        return lax.rem(f + distance, ep)

    def shard_rows(fsdp, ctx):
        return pl.ds(pl.multiple_of((fsdp * 4 + ctx) * rows, 16), rows)

    def columns(kind, side):
        cut, full = cuts[kind], outs[kind].shape[1]
        return pl.ds(0, cut) if side == 0 else pl.ds(cut, full - cut)

    line = [at_device(peer(d), c, t) for d in range(1, ep)]
    plane = [at_device(f, c ^ k, t) for k in range(1, 4)]
    x_device, y_device = plane[0], plane[1]
    core = at_device(f, c, 1 - t)
    greet(line + plane + [core])

    mine = shard_rows(f, c)
    sent = []

    def send(copy):
        copy.start()
        sent.append(copy)

    def z_arrival(kind, d):
        place = shard_rows(peer(ep - d), c)
        remote(
            outs[kind].at[place], outs[kind].at[place], z_send.at[kind, d - 1], z_recv.at[kind, d - 1], x_device
        ).wait_recv()

    def spread(kind, d):
        place = shard_rows(peer(ep - d), c)
        for step in range(2):
            for way, device in enumerate((x_device, y_device)):
                side = step ^ way
                block = outs[kind].at[place, columns(kind, side)]
                send(
                    remote(
                        block, block, plane_send.at[kind, d, way, side], plane_recv.at[kind, d, way, side], device
                    )
                )

    def pass_on(kind, d):
        for way, device in enumerate((y_device, x_device)):
            place = shard_rows(peer(ep - d), c ^ (1 << way))
            block = outs[kind].at[place, columns(kind, way)]
            remote(
                block, block, plane_send.at[kind, d, way, way], plane_recv.at[kind, d, way, way], device
            ).wait_recv()
            send(remote(block, block, relay_send.at[kind, d, way], relay_recv.at[kind, d, way], device))

    def settle(kind):
        for d in range(ep):
            back = peer(ep - d)
            for way, device in enumerate((x_device, y_device)):
                side = 1 - way
                block = outs[kind].at[shard_rows(back, c ^ (1 << way)), columns(kind, side)]
                remote(
                    block, block, plane_send.at[kind, d, way, side], plane_recv.at[kind, d, way, side], device
                ).wait_recv()
                block = outs[kind].at[shard_rows(back, c ^ 3), columns(kind, way)]
                remote(
                    block, block, relay_send.at[kind, d, way], relay_recv.at[kind, d, way], device
                ).wait_recv()

    def line_place(fsdp, part):
        return pl.ds(pl.multiple_of(fsdp * tokens + part * half, 16), half)

    own_tokens = pl.ds(pl.multiple_of(f * tokens, 16), tokens)
    my_half = pl.ds(pl.multiple_of(t * half, 16), half)

    def line_send(kind, source, target):
        for d in range(1, ep):
            send(
                remote(
                    source, target.at[line_place(f, t)], z_send.at[kind, d - 1], z_recv.at[kind, d - 1], line[d - 1]
                )
            )

    def line_forward(kind, target):
        for d in range(1, ep):
            block = target.at[line_place(peer(ep - d), t)]
            remote(block, block, z_send.at[kind, d - 1], z_recv.at[kind, d - 1], core).wait_recv()
            send(remote(block, block, core_send.at[kind - 2, d - 1], core_recv.at[kind - 2, d - 1], core))

    def line_settle(kind, target):
        for d in range(1, ep):
            block = target.at[line_place(peer(ep - d), 1 - t)]
            remote(block, block, core_send.at[kind - 2, d - 1], core_recv.at[kind - 2, d - 1], core).wait_recv()

    for d in range(1, ep):
        send(remote(attn_ref, attn_out.at[mine], z_send.at[0, d - 1], z_recv.at[0, d - 1], line[d - 1]))
    own_attn = pltpu.make_async_copy(attn_ref, attn_out.at[mine], local_sem.at[0])
    own_attn.start()
    own_outer = pltpu.make_async_copy(outer_ref, outer_out.at[own_tokens], local_sem.at[2])
    own_outer.start()
    own_routes = pltpu.make_async_copy(routes_ref, routes_out.at[own_tokens], local_sem.at[3])
    own_routes.start()
    for d in range(1, ep):
        send(
            remote(
                routes_ref, routes_out.at[own_tokens], z_send.at[4, d - 1], z_recv.at[4, d - 1], line[d - 1]
            )
        )
    for kind, ref in enumerate((gate_ref, up_ref, down_ref)):
        for e in range(local):
            target = expert_out.at[mine, pl.ds((kind * local + e) * hidden, hidden)]
            pltpu.make_async_copy(ref.at[f * local + e], target, local_sem.at[1]).start()
    own_attn.wait()
    spread(0, 0)

    length = segment_ref.shape[1]
    seg_keys = segment_ref[...].astype(jnp.float32)
    seg_here = segment_ref[:, pl.ds(pl.multiple_of(c * tokens, 128), tokens)].astype(jnp.float32)
    seg_queries = jnp.broadcast_to(seg_here, (128, tokens)).T[:, :1]
    key_order = lax.broadcasted_iota(jnp.int32, (tokens, length), 1)
    query_order = lax.broadcasted_iota(jnp.int32, (tokens, length), 0) + c * tokens
    same = seg_keys == seg_queries
    seen = same & (key_order <= query_order)
    bias_s[...] = jnp.where(seen, 0.0, MASKED_SCORE)
    place = jnp.sum(jnp.where(same & (key_order < query_order), 1.0, 0.0), -1, keepdims=True)
    angle = place * freq_ref[...]
    lane = lax.broadcasted_iota(jnp.int32, (tokens, 128), 1)
    first_half = lax.rem(lane, HD) < HD // 2
    cosine = jnp.cos(angle)
    sine = jnp.where(first_half, -jnp.sin(angle), jnp.sin(angle))
    cos_out[...] = cosine
    sin_out[...] = sine
    inputs = input_ref[...].astype(jnp.float32)
    inverse = lax.rsqrt(jnp.mean(inputs * inputs, -1, keepdims=True) + EPSILON)

    for d in range(1, ep):
        z_arrival(0, d)
        spread(0, d)
        pass_on(0, d - 1)
    for d in range(1, ep):
        for kind, ref in enumerate((gate_ref, up_ref, down_ref)):
            for e in range(local):
                target = expert_out.at[mine, pl.ds((kind * local + e) * hidden, hidden)]
                remote(
                    ref.at[peer(d) * local + e], target, z_send.at[1, d - 1], z_recv.at[1, d - 1], line[d - 1]
                ).start()
    pass_on(0, ep - 1)
    settle(0)

    gains = attn_out[:, qkv_width : qkv_width + 128].astype(jnp.float32).T
    normed1_out[...] = (inputs * inverse * gains[EXPERTS : EXPERTS + 1, :]).astype(low)

    def project(start):
        return jnp.dot(
            normed1_out[...], attn_out[:, start : start + 256], preferred_element_type=jnp.float32
        )

    def turned(tile):
        swapped = jnp.where(first_half, pltpu.roll(tile, 128 - HD // 2, 1), pltpu.roll(tile, HD // 2, 1))
        return tile * cos_out[...] + swapped * sin_out[...]

    here = pl.ds(pl.multiple_of(c * tokens, 16), tokens)
    for start in range(0, kv_width, 256):
        tile = project(width + start)
        for side in (0, 128):
            pair_out[here, start + side : start + side + 128] = turned(tile[:, side : side + 128]).astype(low)
    for start in range(0, kv_width, 256):
        pair_out[here, kv_width + start : kv_width + start + 256] = project(width + kv_width + start).astype(low)
    for k in (3, 1, 2):
        send(remote(pair_out.at[here], pair_out.at[here], key_send.at[k - 1], key_recv.at[k - 1], plane[k - 1]))
    for start in range(0, width, 256):
        tile = project(start)
        for side in (0, 128):
            query_out[:, start + side : start + side + 128] = turned(tile[:, side : side + 128]).astype(low)
    for h in range(heads):
        query_s[h] = query_out[:, h * HD : (h + 1) * HD]
    pltpu.make_async_copy(expert_out.at[mine], expert_out.at[mine], local_sem.at[1]).wait()
    for k in range(1, 4):
        block = pair_out.at[pl.ds(pl.multiple_of((c ^ k) * tokens, 16), tokens)]
        remote(block, block, key_send.at[k - 1], key_recv.at[k - 1], plane[k - 1]).wait_recv()
    spread(1, 0)
    for g in range(key_heads):
        key_s[g] = pair_out[:, g * HD : (g + 1) * HD]
        value_s[g] = pair_out[:, kv_width + g * HD : kv_width + (g + 1) * HD]
    pass_on(1, 0)

    def attend(h, carry):
        g = lax.div(h, heads // key_heads)
        query = query_s[h] * jnp.asarray(HD**-0.5, low)
        scores = lax.dot_general(
            query, key_s[g], (((1,), (1,)), ((), ())), preferred_element_type=jnp.float32
        ) + bias_s[...]
        top = jnp.max(scores, -1, keepdims=True)
        weights = jnp.exp(scores - top)
        total = jnp.sum(weights, -1, keepdims=True)
        summed = jnp.dot(weights.astype(low), value_s[g], preferred_element_type=jnp.float32)
        mixed_s[h] = (summed / total).astype(low)
        log_out[h] = top + jnp.log(total)
        return carry

    lax.fori_loop(0, heads, attend, 0)
    for h in range(heads):
        mixed_out[:, h * HD : (h + 1) * HD] = mixed_s[h]
    z_arrival(1, 1)
    spread(1, 1)
    line_send(2, outer_ref.at[my_half], outer_out)

    model = input_ref.shape[1]
    for start in range(0, model, 256):
        part_s[:, start : start + 256] = lax.dot_general(
            mixed_out[...], attn_out[start : start + 256, qkv_width + 128 :],
            (((1,), (1,)), ((), ())), preferred_element_type=jnp.float32,
        ).astype(low)
    exchange = remote(part_s, other_s, pair_send, pair_recv, core)
    send(exchange)
    for d in range(2, ep):
        z_arrival(1, d)
        spread(1, d)
        pass_on(1, d - 1)
    exchange.wait_recv()
    middle = input_ref[...].astype(jnp.float32) + (
        part_s[...].astype(jnp.float32) + other_s[...].astype(jnp.float32)
    )
    middle_out[...] = middle
    inverse = lax.rsqrt(jnp.mean(middle * middle, -1, keepdims=True) + EPSILON)
    gains = attn_out[:, qkv_width : qkv_width + 128].astype(jnp.float32).T
    normed2_s[...] = (middle * inverse * gains[EXPERTS + 1 : EXPERTS + 2, :]).astype(low)
    line_send(3, normed2_s.at[my_half], normed2_out)
    own_normed2 = pltpu.make_async_copy(normed2_s, normed2_out.at[own_tokens], local_sem.at[4])
    own_normed2.start()
    pass_on(1, ep - 1)
    line_forward(2, outer_out)
    line_forward(3, normed2_out)
    settle(1)
    line_settle(2, outer_out)
    line_settle(3, normed2_out)
    for d in range(1, ep):
        place = pl.ds(pl.multiple_of(peer(ep - d) * tokens, 16), tokens)
        remote(
            routes_out.at[place], routes_out.at[place], z_send.at[4, d - 1], z_recv.at[4, d - 1], core
        ).wait_recv()
        remote(
            expert_out.at[mine], expert_out.at[mine], z_send.at[1, d - 1], z_recv.at[1, d - 1], core
        ).wait_send()
    own_outer.wait()
    own_routes.wait()
    own_normed2.wait()
    for copy in sent:
        copy.wait_send()


def front(attn, gate, up, down, outer, routes, inputs, segments, freq, heads, key_heads):
    ep = lax.axis_size("fsdp")
    rows = attn.shape[0]
    total = rows * ep * lax.axis_size("ctx")
    local = gate.shape[0] // ep
    tokens, model = inputs.shape
    length = segments.shape[1]
    low = jnp.bfloat16
    dma = pltpu.SemaphoreType.DMA
    anywhere = pl.BlockSpec(memory_space=pl.ANY)
    vmem = pl.BlockSpec(memory_space=pltpu.VMEM)
    shape = jax.ShapeDtypeStruct
    return pl.pallas_call(
        front_kernel,
        out_shape=(
            shape((total, 3 * local * gate.shape[2]), low),
            shape((ep * tokens, model), low),
            shape((ep * tokens, routes.shape[1]), routes.dtype),
            shape((ep * tokens, model), low),
            shape((total, attn.shape[1]), low),
            shape((tokens, model), low),
            shape((tokens, heads * HD), low),
            shape((length, 2 * key_heads * HD), low),
            shape((tokens, heads * HD), low),
            shape((heads, tokens, 1), jnp.float32),
            shape((tokens, model), jnp.float32),
            shape((tokens, 128), jnp.float32),
            shape((tokens, 128), jnp.float32),
        ),
        in_specs=[anywhere] * 6 + [vmem] * 3,
        out_specs=(anywhere,) * 4 + (vmem,) * 9,
        scratch_shapes=[
            pltpu.VMEM((heads, tokens, HD), low),
            pltpu.VMEM((key_heads, length, HD), low),
            pltpu.VMEM((key_heads, length, HD), low),
            pltpu.VMEM((heads, tokens, HD), low),
            pltpu.VMEM((tokens, length), jnp.float32),
            pltpu.VMEM((tokens, model), low),
            pltpu.VMEM((tokens, model), low),
            pltpu.VMEM((tokens, model), low),
            dma((5,)),
            dma((5, ep - 1)),
            dma((5, ep - 1)),
            dma((2, ep, 2, 2)),
            dma((2, ep, 2, 2)),
            dma((2, ep, 2)),
            dma((2, ep, 2)),
            dma((2, ep - 1)),
            dma((2, ep - 1)),
            dma((3,)),
            dma((3,)),
            dma,
            dma,
        ],
        compiler_params=pltpu.CompilerParams(
            collective_id=1, has_side_effects=True, vmem_limit_bytes=56 * 1024 * 1024
        ),
        cost_estimate=lasting(180),
        name="front",
    )(attn, gate, up, down, outer, routes, inputs, segments, freq)


def z_sum_scratch(ep, tokens, width, low):
    dma = pltpu.SemaphoreType.DMA
    return [
        pltpu.VMEM((ep, tokens // 2, width), low),
        pltpu.VMEM((ep - 1, tokens // 2, width), low),
        pltpu.VMEM((ep - 1, tokens // 2, width), low),
        dma((ep,)),
        dma((ep,)),
        dma((ep - 1,)),
        dma((ep - 1,)),
        dma,
        dma,
    ]


class ZSum:
    size = 9

    def __init__(self, part, out, scratch, sent):
        self.part, self.out, self.sent = part, out, sent
        (
            self.core_in, self.z_out, self.z_in, self.core_send, self.core_recv,
            self.z_send, self.z_recv, self.back_send, self.back_recv,
        ) = scratch
        self.ep = self.core_in.shape[0]
        self.f, self.c, self.t = lax.axis_index("fsdp"), lax.axis_index("ctx"), lax.axis_index("tp")
        self.half = out.shape[0] // 2
        self.core = at_device(self.f, self.c, 1 - self.t)

    def peer(self, distance):
        return lax.rem(self.f + distance, self.ep)

    def place(self, fsdp, part):
        return pl.ds(pl.multiple_of(fsdp * 2 * self.half + part * self.half, 16), self.half)

    def send(self, copy):
        copy.start()
        self.sent.append(copy)

    def to_core(self):
        for d in list(range(1, self.ep)) + [0]:
            self.send(
                remote(
                    self.part.at[self.place(self.peer(d), 1 - self.t)], self.core_in.at[d],
                    self.core_send.at[d], self.core_recv.at[d], self.core,
                )
            )

    def added(self, d):
        landing = self.core_in.at[d]
        remote(landing, landing, self.core_send.at[d], self.core_recv.at[d], self.core).wait_recv()
        mine = self.part[self.place(self.peer(d), self.t), :]
        return mine.astype(jnp.float32) + self.core_in[d].astype(jnp.float32)

    def to_z(self):
        for d in range(1, self.ep):
            self.z_out[d - 1] = self.added(d).astype(self.z_out.dtype)
            self.send(
                remote(
                    self.z_out.at[d - 1], self.z_in.at[d - 1], self.z_send.at[d - 1], self.z_recv.at[d - 1],
                    at_device(self.peer(d), self.c, self.t),
                )
            )

    def from_z(self):
        rows = pl.ds(pl.multiple_of(self.t * self.half, 16), self.half)
        self.out[rows, :] = self.added(0)
        for d in range(1, self.ep):
            landing = self.z_in.at[d - 1]
            remote(landing, landing, self.z_send.at[d - 1], self.z_recv.at[d - 1], self.core).wait_recv()
            self.out[rows, :] += self.z_in[d - 1].astype(jnp.float32)
        mine = self.out.at[rows]
        self.send(remote(mine, mine, self.back_send, self.back_recv, self.core))

    def finish(self):
        other = self.out.at[pl.ds(pl.multiple_of((1 - self.t) * self.half, 16), self.half)]
        remote(other, other, self.back_send, self.back_recv, self.core).wait_recv()


def plane_sum_scratch(ep, rows, width, low):
    cut = -(-width // 256) * 128
    dma = pltpu.SemaphoreType.DMA
    return [
        pltpu.VMEM((ep, 2, rows, cut), low),
        pltpu.VMEM((ep, 2, rows, width - cut), low),
        pltpu.VMEM((ep, rows, cut), low),
        pltpu.VMEM((ep, rows, width - cut), low),
        pltpu.VMEM((ep, rows, cut), low),
        pltpu.VMEM((ep, rows, width - cut), low),
        dma((2, ep, 2)),
        dma((2, ep, 2)),
        dma((2, ep)),
        dma((2, ep)),
    ]


class PlaneSum:
    size = 10

    def __init__(self, part, rows, scratch, sent):
        self.part, self.rows, self.sent = part, rows, sent
        self.first_in, self.second_out, self.second_in = scratch[0:2], scratch[2:4], scratch[4:6]
        self.first_send, self.first_recv, self.second_send, self.second_recv = scratch[6:10]
        self.ep = self.first_in[0].shape[0]
        self.f, self.c, self.t = lax.axis_index("fsdp"), lax.axis_index("ctx"), lax.axis_index("tp")
        cut = self.first_in[0].shape[-1]
        self.columns = (pl.ds(0, cut), pl.ds(cut, part.shape[1] - cut))
        self.neighbours = (at_device(self.f, self.c ^ 1, self.t), at_device(self.f, self.c ^ 2, self.t))
        self.order = list(range(1, self.ep)) + [0]

    def block(self, distance, ctx, way):
        start = (lax.rem(self.f + distance, self.ep) * 4 + ctx) * self.rows
        return pl.ds(pl.multiple_of(start, 16), self.rows), self.columns[way]

    def send(self, copy):
        copy.start()
        self.sent.append(copy)

    def first(self):
        for d in self.order:
            for number in range(2):
                for way in range(2):
                    target = self.c ^ 3 if number == 0 else self.c ^ (1 << way)
                    self.send(
                        remote(
                            self.part.at[self.block(d, target, way)], self.first_in[way].at[d, number],
                            self.first_send.at[way, d, number], self.first_recv.at[way, d, number],
                            self.neighbours[way],
                        )
                    )

    def second(self):
        for d in self.order:
            for way in range(2):
                for number in range(2):
                    landing = self.first_in[way].at[d, number]
                    remote(
                        landing, landing, self.first_send.at[way, d, number],
                        self.first_recv.at[way, d, number], self.neighbours[way],
                    ).wait_recv()
                own = self.part[self.block(d, self.c ^ (2 >> way), way)]
                added = own.astype(jnp.float32) + self.first_in[way][d, 0].astype(jnp.float32)
                self.second_out[way][d] = added.astype(self.part.dtype)
                self.send(
                    remote(
                        self.second_out[way].at[d], self.second_in[way].at[d],
                        self.second_send.at[way, d], self.second_recv.at[way, d], self.neighbours[1 - way],
                    )
                )

    def total(self, d, way):
        landing = self.second_in[way].at[d]
        remote(
            landing, landing, self.second_send.at[way, d], self.second_recv.at[way, d], self.neighbours[1 - way]
        ).wait_recv()
        return (
            self.part[self.block(d, self.c, way)].astype(jnp.float32)
            + self.first_in[way][d, 1].astype(jnp.float32)
            + self.second_in[way][d].astype(jnp.float32)
        )


def all_partners(ep):
    f, c, t = lax.axis_index("fsdp"), lax.axis_index("ctx"), lax.axis_index("tp")
    line = [at_device(lax.rem(f + d, ep), c, t) for d in range(1, ep)]
    return line + [at_device(f, c ^ 1, t), at_device(f, c ^ 2, t), at_device(f, c, 1 - t)]


def back_kernel(part_ref, down_ref, sum_ref, down_out, *scratch):
    ep, rows = down_out.shape[0], down_out.shape[1]
    sent = []
    tokens = ZSum(part_ref, sum_ref, scratch[: ZSum.size], sent)
    plane = PlaneSum(down_ref, rows, scratch[ZSum.size :], sent)
    greet(all_partners(ep))
    tokens.to_core()
    plane.first()
    tokens.to_z()
    plane.second()
    tokens.from_z()
    for d in plane.order:
        for way in range(2):
            down_out[plane_row(d, ep), :, plane.columns[way]] = plane.total(d, way).astype(down_out.dtype)
    tokens.finish()
    for copy in sent:
        copy.wait_send()


def plane_row(distance, ep):
    return lax.rem(lax.axis_index("fsdp") + distance, ep)


def sum_back(part, down, collective_id):
    ep = lax.axis_size("fsdp")
    rows = down.shape[0] // (4 * ep)
    tokens, width = part.shape[0] // ep, part.shape[1]
    vmem = pl.BlockSpec(memory_space=pltpu.VMEM)
    return pl.pallas_call(
        back_kernel,
        out_shape=(
            jax.ShapeDtypeStruct((tokens, width), jnp.float32),
            jax.ShapeDtypeStruct((ep, rows, down.shape[1]), down.dtype),
        ),
        in_specs=[vmem] * 2,
        out_specs=(vmem,) * 2,
        scratch_shapes=z_sum_scratch(ep, tokens, width, part.dtype)
        + plane_sum_scratch(ep, rows, down.shape[1], down.dtype),
        compiler_params=pltpu.CompilerParams(
            collective_id=collective_id, has_side_effects=True, vmem_limit_bytes=48 * 1024 * 1024
        ),
        cost_estimate=lasting(45),
        name="sum_back",
    )(part, down)


def keys_kernel(part_ref, down_ref, sum_ref, down_out, landing, send, recv, z_send, z_recv):
    ep = down_ref.shape[0]
    f, c, t = lax.axis_index("fsdp"), lax.axis_index("ctx"), lax.axis_index("tp")
    tokens = sum_ref.shape[0]

    def peer(distance):
        return lax.rem(f + distance, ep)

    plane = [at_device(f, c ^ k, t) for k in range(1, 4)]
    greet([at_device(peer(d), c, t) for d in range(1, ep)] + plane)
    sent = []
    for k in (3, 1, 2):
        place = pl.ds(pl.multiple_of((c ^ k) * tokens, 16), tokens)
        copy = remote(part_ref.at[place], landing.at[k - 1], send.at[k - 1], recv.at[k - 1], plane[k - 1])
        copy.start()
        sent.append(copy)
    for d in range(1, ep):
        copy = remote(
            down_ref.at[peer(d)], down_out.at[f], z_send.at[d - 1], z_recv.at[d - 1], at_device(peer(d), c, t)
        )
        copy.start()
        sent.append(copy)
    down_out[f] = down_ref[f]
    sum_ref[...] = part_ref[pl.ds(pl.multiple_of(c * tokens, 16), tokens), :].astype(jnp.float32)
    for k in (1, 2, 3):
        block = landing.at[k - 1]
        remote(block, block, send.at[k - 1], recv.at[k - 1], plane[k - 1]).wait_recv()
        sum_ref[...] += landing[k - 1].astype(jnp.float32)
    for d in range(1, ep):
        block = down_out.at[peer(ep - d)]
        remote(block, block, z_send.at[d - 1], z_recv.at[d - 1], plane[0]).wait_recv()
    for copy in sent:
        copy.wait_send()


def sum_keys(part, down, collective_id):
    ep = lax.axis_size("fsdp")
    tokens, width = part.shape[0] // 4, part.shape[1]
    dma = pltpu.SemaphoreType.DMA
    vmem = pl.BlockSpec(memory_space=pltpu.VMEM)
    return pl.pallas_call(
        keys_kernel,
        out_shape=(
            jax.ShapeDtypeStruct((tokens, width), jnp.float32),
            jax.ShapeDtypeStruct(down.shape, down.dtype),
        ),
        in_specs=[vmem] * 2,
        out_specs=(vmem,) * 2,
        scratch_shapes=[
            pltpu.VMEM((3, tokens, width), part.dtype), dma((3,)), dma((3,)), dma((ep - 1,)), dma((ep - 1,))
        ],
        compiler_params=pltpu.CompilerParams(
            collective_id=collective_id, has_side_effects=True, vmem_limit_bytes=32 * 1024 * 1024
        ),
        cost_estimate=lasting(20),
        name="sum_keys",
    )(part, down)


def pair_kernel(part_ref, sum_ref, other, send, recv):
    f, c, t = lax.axis_index("fsdp"), lax.axis_index("ctx"), lax.axis_index("tp")
    core = at_device(f, c, 1 - t)
    greet([core])
    copy = remote(part_ref, other, send, recv, core)
    copy.start()
    copy.wait()
    sum_ref[...] = part_ref[...].astype(jnp.float32) + other[...].astype(jnp.float32)


def add_pair(part, collective_id):
    dma = pltpu.SemaphoreType.DMA
    vmem = pl.BlockSpec(memory_space=pltpu.VMEM)
    return pl.pallas_call(
        pair_kernel,
        out_shape=jax.ShapeDtypeStruct(part.shape, jnp.float32),
        in_specs=[vmem],
        out_specs=vmem,
        scratch_shapes=[pltpu.VMEM(part.shape, part.dtype), dma, dma],
        compiler_params=pltpu.CompilerParams(
            collective_id=collective_id, has_side_effects=True, vmem_limit_bytes=32 * 1024 * 1024
        ),
        cost_estimate=lasting(5),
        name="add_pair",
    )(part)


def last_kernel(part_ref, mixture_ref, sum_ref, mixed_ref, *scratch):
    ep = lax.axis_size("fsdp")
    rows = sum_ref.shape[0]
    sent = []
    tokens = ZSum(mixture_ref, mixed_ref, scratch[: ZSum.size], sent)
    plane = PlaneSum(part_ref, rows, scratch[ZSum.size : ZSum.size + PlaneSum.size], sent)
    z_out, z_in, z_send, z_recv = scratch[ZSum.size + PlaneSum.size :]
    partners = all_partners(ep)
    greet(partners)
    plane.first()
    tokens.to_core()
    tokens.to_z()
    plane.second()
    for d in plane.order:
        for way in range(2):
            total = plane.total(d, way)
            if d == 0:
                sum_ref[:, plane.columns[way]] = total
            else:
                z_out[d - 1, :, plane.columns[way]] = total.astype(z_out.dtype)
        if d > 0:
            copy = remote(z_out.at[d - 1], z_in.at[d - 1], z_send.at[d - 1], z_recv.at[d - 1], partners[d - 1])
            copy.start()
            sent.append(copy)
    tokens.from_z()
    for d in range(1, ep):
        landing = z_in.at[d - 1]
        remote(landing, landing, z_send.at[d - 1], z_recv.at[d - 1], partners[d - 1]).wait_recv()
        sum_ref[...] += z_in[d - 1].astype(jnp.float32)
    tokens.finish()
    for copy in sent:
        copy.wait_send()


def sum_last(part, mixture, collective_id):
    ep = lax.axis_size("fsdp")
    rows = part.shape[0] // (4 * ep)
    width, low = part.shape[1], part.dtype
    tokens = mixture.shape[0] // ep
    dma = pltpu.SemaphoreType.DMA
    vmem = pl.BlockSpec(memory_space=pltpu.VMEM)
    return pl.pallas_call(
        last_kernel,
        out_shape=(
            jax.ShapeDtypeStruct((rows, width), jnp.float32),
            jax.ShapeDtypeStruct((tokens, mixture.shape[1]), jnp.float32),
        ),
        in_specs=[vmem] * 2,
        out_specs=(vmem,) * 2,
        scratch_shapes=z_sum_scratch(ep, tokens, mixture.shape[1], low)
        + plane_sum_scratch(ep, rows, width, low)
        + [
            pltpu.VMEM((ep - 1, rows, width), low),
            pltpu.VMEM((ep - 1, rows, width), low),
            dma((ep - 1,)),
            dma((ep - 1,)),
        ],
        compiler_params=pltpu.CompilerParams(
            collective_id=collective_id, has_side_effects=True, vmem_limit_bytes=48 * 1024 * 1024
        ),
        cost_estimate=lasting(75),
        name="sum_last",
    )(part, mixture)


def shards(
    layer_input,
    segments,
    routes,
    norm_gain,
    query_weight,
    key_weight,
    value_weight,
    output_weight,
    ffn_gain,
    router_weight,
    gate_weight,
    up_weight,
    down_weight,
    cotangent,
):
    low = jnp.bfloat16
    both = ("fsdp", "ctx")
    ep = lax.axis_size("fsdp")
    tokens = layer_input.shape[0]
    seq_len = segments.shape[1]
    rows = query_weight.shape[0]
    width = query_weight.shape[1]
    kv_width = key_weight.shape[1]
    hidden_width = gate_weight.shape[2]
    local = EXPERTS // ep
    span = local * hidden_width

    qkv_width = width + 2 * kv_width
    extra = jnp.concatenate([router_weight, norm_gain[:, None], ffn_gain[:, None]], 1)
    extra = jnp.pad(extra, ((0, 0), (0, 128 - extra.shape[1])))
    attn_shard = jnp.concatenate([query_weight, key_weight, value_weight, extra, output_weight.T], 1)
    down_shard = down_weight.transpose(0, 2, 1)
    begin = lax.axis_index("ctx") * tokens
    segment_row = segments[0]
    query_doc = lax.dynamic_slice_in_dim(segment_row, begin, tokens)
    query_order = begin + jnp.arange(tokens, dtype=jnp.int32)
    scale = HD ** (-0.5)
    inputs = layer_input.astype(jnp.float32)
    key_groups = kv_width // HD
    groups = width // kv_width
    freq = 10000.0 ** (-2.0 * jnp.arange(HD // 2, dtype=jnp.float32) / HD)

    def unpack(attn_full):
        return (
            attn_full[:, :qkv_width],
            attn_full[:, qkv_width : qkv_width + EXPERTS],
            attn_full[:, qkv_width + EXPERTS],
            attn_full[:, qkv_width + EXPERTS + 1],
            attn_full[:, qkv_width + 128 :],
        )

    if lax.axis_size("ctx") == 4:
        (
            expert_full, outer_all, routes_all, normed2_all,
            attn_full, normed1, query, pair_all, mixed_low, log_total, middle, cosine, sine,
        ) = front(
            attn_shard, gate_weight, up_weight, down_shard, cotangent, routes, layer_input, segments,
            jnp.tile(freq, 4)[None, :], width // HD, key_groups,
        )
        qkv_full, router_full, gain_one, gain_two, output_turned = unpack(attn_full)
        log_total = log_total[:, :, 0].T.reshape(tokens, key_groups, groups)
        cosine, sine = cosine[:, : HD // 2], sine[:, HD // 2 : HD]
        first_inverse = lax.rsqrt(jnp.mean(inputs * inputs, -1, keepdims=True) + EPSILON)
        second_inverse = lax.rsqrt(jnp.mean(middle * middle, -1, keepdims=True) + EPSILON)
        normed2 = lax.dynamic_slice_in_dim(normed2_all, lax.axis_index("fsdp") * tokens, tokens)
    else:
        attn_full = lax.all_gather(attn_shard, both, axis=0, tiled=True)
        qkv_full, router_full, gain_one, gain_two, output_turned = unpack(attn_full)
        packed = jnp.concatenate([gate_weight, up_weight, down_shard], -1)
        expert_full = spread_experts(packed)
        expert_full = expert_full.reshape(D, local, 3, hidden_width).transpose(0, 2, 1, 3)
        expert_full = expert_full.reshape(D, 3 * span)
        outer_all = lax.all_gather(cotangent, "fsdp", axis=0, tiled=True)
        routes_all = lax.all_gather(routes, "fsdp", axis=0, tiled=True)
        place = lax.dynamic_slice_in_dim(document_place(segment_row), begin, tokens)
        angle = place.astype(jnp.float32)[:, None] * freq[None, :]
        cosine, sine = jnp.cos(angle), jnp.sin(angle)
        first_norm, first_inverse = normalize(inputs, gain_one)
        normed1 = first_norm.astype(low)
        projected = jnp.dot(normed1, qkv_full, preferred_element_type=jnp.float32)
        query = rotate(projected[:, :width], cosine, sine).astype(low)
        key = rotate(projected[:, width : width + kv_width], cosine, sine).astype(low)
        value = projected[:, width + kv_width :].astype(low)
        pair_all = lax.all_gather(jnp.concatenate([key, value], 1), "ctx", axis=0, tiled=True)
        heads = query.reshape(tokens, key_groups, groups, HD)
        key_heads = pair_all[:, :kv_width].reshape(seq_len, key_groups, HD)
        value_heads = pair_all[:, kv_width:].reshape(seq_len, key_groups, HD)
        scores = jnp.einsum("qkgd,nkd->qkgn", heads, key_heads, preferred_element_type=jnp.float32) * scale
        seen = (segment_row[None, :] == query_doc[:, None]) & (
            jnp.arange(seq_len, dtype=jnp.int32)[None, :] <= query_order[:, None]
        )
        scores = jnp.where(seen[:, None, None, :], scores, MASKED_SCORE)
        running = jnp.max(scores, -1)
        weights = jnp.exp(scores - running[..., None])
        summed = jnp.einsum(
            "qkgn,nkd->qkgd", weights.astype(low), value_heads, preferred_element_type=jnp.float32
        )
        totals = jnp.sum(weights, -1)
        log_total = running + jnp.log(totals)
        mixed_low = (summed / totals[..., None]).reshape(tokens, -1).astype(low)
        attention = add_pair(times_transpose(mixed_low, output_turned).astype(low), 3)
        middle = inputs + attention
        second_norm, second_inverse = normalize(middle, gain_two)
        normed2 = second_norm.astype(low)
        normed2_all = lax.all_gather(normed2, "fsdp", axis=0, tiled=True)
    gate_up = expert_full[:, : 2 * span]
    down_turned = expert_full[:, 2 * span :]
    key_all = pair_all[:, :kv_width]
    value_all = pair_all[:, kv_width:]
    grouped = query.reshape(tokens, key_groups, groups, HD)

    def block_scores(key_piece, offset):
        count = key_piece.shape[0]
        key_heads = key_piece.reshape(count, key_groups, HD)
        scores = (
            jnp.einsum("qkgd,nkd->qkgn", grouped, key_heads, preferred_element_type=jnp.float32)
            * scale
        )
        key_doc = lax.dynamic_slice_in_dim(segment_row, offset, count)
        key_order = offset + jnp.arange(count, dtype=jnp.int32)
        seen = (key_doc[None, :] == query_doc[:, None]) & (
            key_order[None, :] <= query_order[:, None]
        )
        return (scores, seen[:, None, None, :], key_heads)

    def masked_away(offset, count):
        last_doc = lax.dynamic_index_in_dim(segment_row, offset + count - 1, keepdims=False)
        return (offset > query_order[tokens - 1]) | (last_doc < query_doc[0])

    logits_all = jnp.dot(normed2_all, router_full, preferred_element_type=jnp.float32)
    expert_ids = jnp.arange(EXPERTS, dtype=jnp.int32)
    chosen_all = jnp.any(routes_all[:, :, None] == expert_ids[None, None, :], 1)
    masked_logits = jnp.where(chosen_all, logits_all, MASKED_SCORE)
    top = jnp.max(masked_logits, -1, keepdims=True)
    lifted = jnp.where(chosen_all, jnp.exp(masked_logits - top), 0.0)
    gates_all = lifted / jnp.sum(lifted, -1, keepdims=True)
    place_z = lax.axis_index("fsdp")
    gates_here = lax.dynamic_slice_in_dim(gates_all, place_z * local, local, 1)
    chosen_here = lax.dynamic_slice_in_dim(chosen_all, place_z * local, local, 1)
    chosen = lax.dynamic_slice_in_dim(chosen_all, place_z * tokens, tokens, 0)
    gates = lax.dynamic_slice_in_dim(gates_all, place_z * tokens, tokens, 0)

    reach = normed2_all.shape[0]
    both_sides = jnp.dot(normed2_all, gate_up, preferred_element_type=jnp.float32)
    former = both_sides[:, :span]
    latter = both_sides[:, span:]
    hidden_grad = jnp.dot(outer_all, down_turned, preferred_element_type=jnp.float32)
    gate_wide = jnp.concatenate(
        [jnp.broadcast_to(gates_here[:, e : e + 1], (reach, hidden_width)) for e in range(local)], 1
    )
    logistic = jax.nn.sigmoid(former)
    active = former * logistic
    hidden = (active * latter).astype(low).astype(jnp.float32)
    gated = (hidden * gate_wide).astype(low)
    parts = [slice(e * hidden_width, (e + 1) * hidden_width) for e in range(local)]
    dgates = jnp.stack([jnp.sum(hidden[:, part] * hidden_grad[:, part], -1) for part in parts], 1)
    scaled_grad = hidden_grad * gate_wide
    former_grad = (scaled_grad * latter * logistic * (1.0 + former * (1.0 - logistic))).astype(low)
    latter_grad = (scaled_grad * active).astype(low)
    side_grads = jnp.concatenate([former_grad, latter_grad], 1)
    mixture_part = times_transpose(gated, down_turned)
    input_part = times_transpose(side_grads, gate_up)
    side_sums = contract_rows(normed2_all, side_grads)
    down_sums = contract_rows(outer_all, gated)
    dgates = jnp.where(chosen_here, dgates, 0.0)
    dgates_wide = lax.dynamic_update_slice_in_dim(
        jnp.zeros((reach, EXPERTS), jnp.float32), dgates, place_z * local, 1
    )
    dgates_high = dgates_wide.astype(low)
    dgates_rest = (dgates_wide - dgates_high.astype(jnp.float32)).astype(low)
    dgates_sent = jnp.concatenate([dgates_high, dgates_rest], 1)
    dgates_sent = jnp.pad(dgates_sent, ((0, 0), (0, 128 - 2 * EXPERTS)))
    back_part = jnp.concatenate([input_part.astype(low), dgates_sent], 1)
    if lax.axis_size("ctx") == 4:
        returned, down_mine = sum_back(back_part, down_sums.astype(low), 4)
    else:
        returned = lax.psum_scatter(
            lax.psum(back_part, "tp"), "fsdp", scatter_dimension=0, tiled=True
        ).astype(jnp.float32)
    side_out = collect_experts(side_sums.astype(low), rows).reshape(ep, rows, 2, local, hidden_width)
    side_out = side_out.transpose(2, 0, 3, 1, 4).reshape(2, EXPERTS, rows, hidden_width).astype(jnp.float32)

    outer_grad = cotangent.astype(jnp.float32)
    input_grad_part = returned[:, :D]
    picked = returned[:, D : D + EXPERTS] + returned[:, D + EXPERTS : D + 2 * EXPERTS]
    logit_grad = (gates * (picked - jnp.sum(gates * picked, -1, keepdims=True))).astype(low)
    router_sums = contract_rows(normed2, logit_grad)
    second_grad = input_grad_part + times_transpose(logit_grad, router_full)
    middle_back, gain_two_sums = norm_back(second_grad, middle, second_inverse, gain_two)
    middle_grad = outer_grad + middle_back
    attention_grad = middle_grad.astype(low)
    output_sums = contract_rows(attention_grad, mixed_low)
    mixed_grad = jnp.dot(attention_grad, output_turned, preferred_element_type=jnp.float32).astype(low)
    mixed_heads = mixed_grad.reshape(tokens, key_groups, groups, HD)
    delta = jnp.sum(mixed_heads.astype(jnp.float32) * mixed_low.reshape(mixed_heads.shape), -1)

    def back_two(number, state):
        offset = number * tokens
        key_piece = lax.dynamic_slice_in_dim(key_all, offset, tokens, 0)
        value_piece = lax.dynamic_slice_in_dim(value_all, offset, tokens, 0)

        def back_compute(inner):
            query_sum, pair_sum = inner
            scores, seen, key_heads = block_scores(key_piece, offset)
            probs = jnp.where(seen, jnp.exp(scores - log_total[..., None]), 0.0)
            value_heads = value_piece.reshape(tokens, key_groups, HD)
            prob_grad = jnp.einsum(
                "qkgd,nkd->qkgn", mixed_heads, value_heads, preferred_element_type=jnp.float32
            )
            score_grad = (probs * (prob_grad - delta[..., None])).astype(low)
            query_sum = (
                query_sum
                + jnp.einsum(
                    "qkgn,nkd->qkgd", score_grad, key_heads, preferred_element_type=jnp.float32
                )
                * scale
            )
            key_block = (
                jnp.einsum(
                    "qkgn,qkgd->nkd", score_grad, grouped, preferred_element_type=jnp.float32
                )
                * scale
            )
            value_block = jnp.einsum(
                "qkgn,qkgd->nkd", probs.astype(low), mixed_heads, preferred_element_type=jnp.float32
            )
            pair = jnp.concatenate([key_block.reshape(tokens, -1), value_block.reshape(tokens, -1)], 1)
            return (query_sum, lax.dynamic_update_slice_in_dim(pair_sum, pair, offset, 0))

        return lax.cond(masked_away(offset, tokens), lambda inner: inner, back_compute, state)

    back_state = (
        jnp.zeros((tokens, key_groups, groups, HD), jnp.float32),
        jnp.zeros((seq_len, 2 * kv_width), jnp.float32),
    )
    query_sum, pair_sum = lax.fori_loop(0, seq_len // tokens, back_two, back_state)
    if lax.axis_size("ctx") == 4:
        pair_local, down_out = sum_keys(pair_sum.astype(low), down_mine, 7)
    else:
        pair_local = lax.psum_scatter(
            pair_sum.astype(low), "ctx", scatter_dimension=0, tiled=True
        ).astype(jnp.float32)
        down_out = collect_experts(down_sums.astype(low), rows)
    down_out = down_out.reshape(ep, rows, local, hidden_width)
    down_out = down_out.transpose(0, 2, 3, 1).reshape(EXPERTS, hidden_width, rows).astype(jnp.float32)
    query_back = rotate(query_sum.reshape(tokens, -1), cosine, -sine)
    key_back = rotate(pair_local[:, :kv_width], cosine, -sine)
    qkv_back = jnp.concatenate([query_back, key_back, pair_local[:, kv_width:]], 1).astype(low)
    qkv_sums = contract_rows(normed1, qkv_back)
    first_part = times_transpose(qkv_back, qkv_full)
    first_grad = add_pair(first_part.astype(low), 5)
    input_back, gain_one_sums = norm_back(first_grad, inputs, first_inverse, gain_one)
    input_grad = middle_grad + input_back
    small_sums = jnp.concatenate([router_sums, gain_one_sums[:, None], gain_two_sums[:, None]], 1)
    small_sums = jnp.pad(small_sums, ((0, 0), (0, 128 - small_sums.shape[1])))
    attn_sums = jnp.concatenate([qkv_sums.astype(low), small_sums.astype(low), output_sums.astype(low)], 1)
    mixture_low = mixture_part.astype(low)
    if lax.axis_size("ctx") == 4:
        attn_out, mixture = sum_last(attn_sums, mixture_low, 6)
    else:
        attn_out = lax.psum_scatter(attn_sums, both, scatter_dimension=0, tiled=True).astype(jnp.float32)
        mixture = lax.psum_scatter(
            lax.psum(mixture_low, "tp"), "fsdp", scatter_dimension=0, tiled=True
        ).astype(jnp.float32)
    layer_output = (middle + mixture).astype(low)
    small_out = attn_out[:, qkv_width : qkv_width + 128]
    return (
        layer_output,
        input_grad,
        small_out[:, EXPERTS],
        attn_out[:, :width],
        attn_out[:, width : width + kv_width],
        attn_out[:, width + kv_width : qkv_width],
        attn_out[:, qkv_width + 128 :].T,
        small_out[:, EXPERTS + 1],
        small_out[:, :EXPERTS],
        side_out[0],
        side_out[1],
        down_out,
    )


def solution(mesh):
    in_specs = (
        P(("fsdp", "ctx"), None),
        P("fsdp", None),
        P(("fsdp", "ctx"), None),
        P(("fsdp", "ctx")),
        P(("fsdp", "ctx"), "tp"),
        P(("fsdp", "ctx"), "tp"),
        P(("fsdp", "ctx"), "tp"),
        P("tp", ("fsdp", "ctx")),
        P(("fsdp", "ctx")),
        P(("fsdp", "ctx"), None),
        P(None, ("fsdp", "ctx"), "tp"),
        P(None, ("fsdp", "ctx"), "tp"),
        P(None, "tp", ("fsdp", "ctx")),
        P(("fsdp", "ctx"), None),
    )
    out_specs = (
        P(("fsdp", "ctx"), None),
        P(("fsdp", "ctx"), None),
        P(("fsdp", "ctx")),
        P(("fsdp", "ctx"), "tp"),
        P(("fsdp", "ctx"), "tp"),
        P(("fsdp", "ctx"), "tp"),
        P("tp", ("fsdp", "ctx")),
        P(("fsdp", "ctx")),
        P(("fsdp", "ctx"), None),
        P(None, ("fsdp", "ctx"), "tp"),
        P(None, ("fsdp", "ctx"), "tp"),
        P(None, "tp", ("fsdp", "ctx")),
    )
    return jax.shard_map(shards, mesh=mesh, in_specs=in_specs, out_specs=out_specs, check_vma=False)
```

time: 718 us -> 569 us (0.79)
  waiting for transfers between devices: 150 us -> 0.02 us
  Pallas kernels: 334 us -> 368 us
  other arithmetic: 34.4 us -> 20.7 us
  blocking collectives: 9.83 us -> 0 us
  matrix products: 90.7 us -> 82.2 us
    reduce_scatter x2 -> x1, waiting for transfers between devices: 61.5 us -> 0.01 us  [collect_experts(): mine = lax.psum_scatter(turned, 'ctx', scatter_dimension=0, tiled=True)]
    reduce_scatter x2 -> x0, waiting for transfers between devices: 61.2 us -> none  [the longest x1 59.9 us: shards(): lax.psum_scatter(lax.psum(mixture_part.astype(low), 'tp'), 'fsdp', scatte...]
    pallas_call x4, Pallas kernels: 329 us -> 365 us  [the longest x1 179 us: front(): pl.pallas_call(front_kernel, out_shape=(shape((total, 3 * local * gate.sh...]
    all_gather x1 -> x0, waiting for transfers between devices: 14.7 us -> none  [shards(): lax.all_gather(jnp.concatenate([key, value], 1), 'ctx', axis=0, tiled=True)]
    all_to_all x2 -> x1, waiting for transfers between devices: 12.5 us -> 0.01 us  [collect_experts(): return lax.all_to_all(mine, 'fsdp', 0, 0, tiled=True)]
    all_gather x1 -> x0, blocking collectives: 9.83 us -> none  [shards(): routes_all = lax.all_gather(routes, 'fsdp', axis=0, tiled=True)]
    dot_general x2 -> x0, matrix products: 7.6 us -> none  [the longest x1 4.25 us: shards(): jnp.einsum('qkgn,nkd->qkgd', weights.astype(low), value_all.reshape(seq_l...]
    dot_general x5 -> x4, matrix products: 24.2 us -> 23.7 us  [times_transpose(): lax.dot_general(left, right, (((1,), (1,)), ((), ())), preferred_element_...]
  transfers between devices with their start and end apart: 8 -> 2, of which waited for: 5 -> 0; matrix products, arithmetic and copies ran while one was open for 15% -> 17% of each run, Pallas kernels for 19% -> 34%
where the time goes in v2:
time: 569 us; the launch traced here: 559 us
  Pallas kernels  368 us (65%)
  matrix products  82.2 us (14%)
  local copies, waits for them, and re-layouts  59.6 us (10%)
  other arithmetic  20.7 us (4%)
  between operations  15.1 us (3%)
  loops' own time  8.1 us (1%)
    pallas_call x1, Pallas kernels, front(): pl.pallas_call(front_kernel, out_shape=(shape((total, 3 * local * gate.sh...  179 us
    pallas_call x1, Pallas kernels, sum_last(): pl.pallas_call(last_kernel, out_shape=(jax.ShapeDtypeStruct((rows, width)...  96.5 us
    pallas_call x1, Pallas kernels, sum_back(): pl.pallas_call(back_kernel, out_shape=(jax.ShapeDtypeStruct((tokens, widt...  47.5 us
    pallas_call x1, Pallas kernels, sum_keys(): pl.pallas_call(keys_kernel, out_shape=(jax.ShapeDtypeStruct((tokens, widt...  42.1 us
    dot_general x4, matrix products, times_transpose(): lax.dot_general(left, right, (((1,), (1,)), ((), ())), preferred_element_...  23.7 us
    dot_general x5, matrix products, contract_rows(): lax.dot_general(left, right, (((0,), (0,)), ((), ())), preferred_element_...  19.7 us
    dot_general x1, matrix products, shards(): jnp.dot(outer_all, down_turned, preferred_element_type=jnp.float32)  14.2 us
    unnamed x88, local copies, waits for them, and re-layouts  12.2 us
  transfers between devices with their start and end apart: 2, of which 0 were waited for; matrix products, arithmetic and copies ran while one was open for 17% of the time, Pallas kernels for 34%

profile of v2, /device:TPU:9, one launch (start us, length us, event | category | flops | bytes accessed | tf_op | source)
XLA Modules:
  0.0 558.5 jit_solution(2149456820404024672)
XLA Ops:
  7.2 0.9 constant_dynamic-update-slice_fusion.2
  9.0 1.5 copy.189.routes_ref
  11.1 0.8 constant_dynamic-update-slice_fusion.1
  11.9 0.8 constant_dynamic-update-slice_fusion
  12.7 0.9 bitcast_dynamic-update-slice_fusion.attn_ref
  13.7 0.7 copy-done.28
  14.4 179.4 %front.1 = (bf16[1536,3072]{1,0:T(8,128)(2,1)}, bf16[1024,1536]{1,0:T(8,128)(2,1)}, s32[1024,8]{1,0:T(8,128)}, bf16[1024,1536]{1,0:T(8,128)(2,1)}, bf16[1536,217...) custom-call(bf16[96,2176]{1,0:T(8,128)(2,1)} %copy-done.28, ...), custom_call_target="tpu_custom_call" | custom-call | bytes 664200000 | tf_op jit(solution)/shard_map/front/pallas_call | solution.py:382
  193.8 1.2 copy.191
  195.3 3.0 fusion.74
  199.1 11.8 %fusion.19 = f32[1024,2048]{0,1:T(8,128)} fusion(bf16[1024,1536]{1,0:T(8,128)(2,1)} %get-tuple-element.573, bf16[1536,3072]{1,0:T(8,128)(2,1)} %get-tuple-element.571), kind=kOutput, calls=%fused_computation.31 | convolution fusion | flops 6442450944 | bytes 17825792 | tf_op jit(solution)/shard_map/dot_general | solution.py:941
  210.8 1.2 dynamic-slice_reduce_fusion.3
  212.5 14.2 %multiply_convert_fusion.2 = (bf16[1024,1024]{0,1:T(8,128)(2,1)S(1)}, bf16[1024,1024]{0,1:T(8,128)(2,1)}, f32[1024,1024]{0,1:T(8,128)}, f32[1024,1024]{0,1:T(8,128)}) fusion(f32[1024,2048]{0,1:T(8,128)} %fusion.19, f32[1024,256]{0,1:T(8,128)S(1)} %broadcast_in_dim.113, f32[1024,256]{0,1:T(8,128)S(1)} %broadcast_in_dim.111, ...), kind=kOutput, calls=%fused_computation.40 | convolution fusion | flops 3242196992 | bytes 31457280 | tf_op jit(solution)/shard_map/dot_general | solution.py:944
  226.8 10.2 %convolution_convert_fusion = bf16[1536,2048]{1,0:T(8,128)(2,1)S(1)} fusion(bf16[1024,1536]{1,0:T(8,128)(2,1)} %get-tuple-element.573, bf16[1024,1024]{0,1:T(8,128)(2,1)} %get-tuple-element.775, bf16[1024,1024]{0,1:T(8,128)(2,1)S(1)} %get-tuple-element.774), kind=kOutput, calls=%fused_computation.25 | convolution fusion | flops 6453985280 | bytes 13631488 | tf_op jit(solution)/shard_map/dot_general | solution.py:51
  236.9 3.3 copy.213
  240.3 4.1 fusion.52
  244.7 1.3 fusion.72
  245.9 1.0 copy.201
  247.1 1.0 copy.202
  248.4 3.1 dynamic_update_slice.9
  251.7 10.4 %fusion.27 = bf16[1024,1536]{1,0:T(8,128)(2,1)S(1)} fusion(bf16[1536,3072]{1,0:T(8,128)(2,1)} %get-tuple-element.571, bf16[1024,1024]{0,1:T(8,128)(2,1)} %get-tuple-element.775, bf16[1024,1024]{0,1:T(8,128)(2,1)} %copy-done.42), kind=kOutput, calls=%fused_computation.45 | convolution fusion | flops 6452412416 | bytes 13631488 | tf_op jit(solution)/shard_map/dot_general | solution.py:57
  262.1 2.1 pad_maximum_fusion.2.part_ref
  264.2 1.4 copy-done.11
  266.3 5.0 convolution_convert_fusion.3.down_ref
  271.3 47.5 %sum_back.1 = (f32[256,1664]{1,0:T(8,128)S(1)}, bf16[4,96,1024]{2,1,0:T(8,128)(2,1)S(1)}) custom-call(bf16[1024,1664]{1,0:T(8,128)(2,1)} %pad_maximum_fusion.2.part_ref, bf16[1536,1024]{1,0:T(8,128)(2,1)S(1)} %convolution_convert_fusion.3.down_ref), custom_call_target="tpu_custom_call" | custom-call | bytes 166050000 | tf_op jit(solution)/shard_map/sum_back/pallas_call | solution.py:628
  318.9 2.4 convert_reduce_fusion
  321.7 2.3 multiply_reduce_fusion.1
  324.5 1.1 copy-done.6
  325.6 2.6 fusion.46
  328.3 0.9 copy.199
  329.2 1.2 copy.200
  331.6 1.1 multiply_reduce_fusion.3
  332.9 26.7 %while.19 = (s32[]{:T(128)}, f32[256,4,3,64]{0,3,2,1:T(8,128)S(1)}, bf16[1024,512]{0,1:T(8,128)(2,1)S(1)}, s32[256]{0:T(256)S(1)}, s32[1024]{0:T(1024)}, /*index...) while((s32[]{:T(128)}, f32[256,4,3,64]{0,3,2,1:T(8,128)S(1)}, ...), condition=%wide.region_14.15_spmd, body=%wide.region_11.14_spmd.sunk | while | flops 512426240 | bytes 33426952 | solution.py:1033
  334.1 1.3 dynamic_slice.80
  337.2 9.2 %conditional.2 = ((f32[256,4,3,64]{0,3,2,1:T(8,128)S(1)}, bf16[1024,512]{0,1:T(8,128)(2,1)S(1)})) conditional(s32[]{:T(128)} %convert_element_type.246, (s32[]{:T(128)}, s32[1024]{0:T(1024)}, s32[256]{0:T(256)S(1)}, s32[256]{0:T(256)S(1)}, bf16[1024,256]{0,1:T(8,128)(2,1)}, /*index=5*/bf16[256,4,3,64]{0,3,2,1:T(8,128)(2,1)S(1)}, ...), branch_computations={%region_12.12_spmd, %region_13.13_spmd} | conditional | flops 512426240 | bytes 33426562 | solution.py:1027
  337.2 1.0 constant_dynamic-slice_fusion
  338.2 2.3 fusion.75
  340.6 0.8 dynamic_slice.55
  341.5 3.1 fusion.1
  347.7 1.3 dynamic_slice.80
  352.1 1.3 dynamic_slice.80
  356.4 1.3 dynamic_slice.80
  359.6 1.0 copy-done.12
  360.6 1.7 copy.205.part_ref
  362.3 42.1 %sum_keys.1 = (f32[256,512]{1,0:T(8,128)S(1)}, bf16[4,96,1024]{2,1,0:T(8,128)(2,1)S(1)}) custom-call(bf16[1024,512]{1,0:T(8,128)(2,1)S(1)} %copy.205.part_ref, bf16[4,96,1024]{2,1,0:T(8,128)(2,1)S(1)} %get-tuple-element.581.down_ref), custom_call_target="tpu_custom_call" | custom-call | bytes 73800000 | tf_op jit(solution)/shard_map/sum_keys/pallas_call | solution.py:686
  404.4 0.9 copy-done.2
  406.8 3.4 fusion.33.part_ref
  410.3 2.9 add_pair.1
  413.5 1.0 fusion.45
  414.5 1.4 convolution_convert_fusion.5
  416.5 1.1 copy.211
  417.7 1.9 convolution_convert_fusion.4
  419.7 1.2 convolution_convert_fusion.1
  420.9 3.1 fusion.16.part_ref
  424.0 4.5 all-to-all-start
  428.5 7.6 %convolution_convert_fusion.2.mixture_ref = bf16[1024,1536]{1,0:T(8,128)(2,1)S(1)} fusion(bf16[1536,3072]{1,0:T(8,128)(2,1)} %get-tuple-element.571, f32[1024,1024]{0,1:T(8,128)} %get-tuple-element.776, f32[1024,256]{0,1:T(8,128)S(1)} %copy-done.21, f32[1024,256]{0,1:T(8,128)} %copy-done.22, f32[1024,256]{0,1:T(8,128)} %copy-done.24, f32[1024,256]{0,1:T(8,128)} %copy-done.26), kind=kOutput, calls=%fused_computation.46 | convolution fusion | flops 3228041216 | bytes 14680064 | tf_op jit(solution)/shard_map/dot_general | solution.py:57
  436.1 96.5 %sum_last.1 = (f32[96,2176]{1,0:T(8,128)S(1)}, f32[256,1536]{1,0:T(8,128)S(1)}) custom-call(bf16[1536,2176]{1,0:T(8,128)(2,1)} %fusion.16.part_ref, bf16[1024,1536]{1,0:T(8,128)(2,1)S(1)} %convolution_convert_fusion.2.mixture_ref), custom_call_target="tpu_custom_call" | custom-call | bytes 276750016 | tf_op jit(solution)/shard_map/sum_last/pallas_call | solution.py:773
  532.6 0.9 copy-done
  534.2 2.8 reshape.221
  536.9 3.0 copy.216
  541.3 0.8 slice_bitcast_fusion
  542.2 2.1 fusion.44
  544.3 3.8 reshape.220
  548.7 1.4 copy.214
  550.1 1.4 copy.215
  (156 shorter events, 18.3 us)
Async XLA Ops:
  7.2 416.8 %reduce-scatter.2.cloned.1.call-start = ((), (), s32[]{:S(2)}) async-start(), calls=%async_computation.2 | async-start | bytes 7864320 | tf_op jit(solution)/shard_map/reduce_scatter | solution.py:76
  13.7 0.8 copy-start.28
  212.1 14.6 %copy-start.19 = (f32[1024,256]{0,1:T(8,128)}, f32[1024,256]{0,1:T(8,128)S(1)}, u32[]{:S(2)}) copy-start(f32[1024,256]{0,1:T(8,128)S(1)} %broadcast_in_dim.113) | copy-start | bytes 3145732
  212.2 14.5 %copy-start.22 = (f32[1024,256]{0,1:T(8,128)}, f32[1024,256]{0,1:T(8,128)S(1)}, u32[]{:S(2)}) copy-start(f32[1024,256]{0,1:T(8,128)S(1)} %broadcast_in_dim.111) | copy-start | bytes 3145732
  212.4 14.4 %copy-start.24 = (f32[1024,256]{0,1:T(8,128)}, f32[1024,256]{0,1:T(8,128)S(1)}, u32[]{:S(2)}) copy-start(f32[1024,256]{0,1:T(8,128)S(1)} %broadcast_in_dim.109) | copy-start | bytes 3145732
  212.5 14.3 %copy-start.26 = (f32[1024,256]{0,1:T(8,128)}, f32[1024,256]{0,1:T(8,128)S(1)}, u32[]{:S(2)}) copy-start(f32[1024,256]{0,1:T(8,128)S(1)} %broadcast_in_dim.107) | copy-start | bytes 3145732
  226.8 10.2 %copy-start.42 = (bf16[1024,1024]{0,1:T(8,128)(2,1)}, bf16[1024,1024]{0,1:T(8,128)(2,1)S(1)}, u32[]{:S(2)}) copy-start(bf16[1024,1024]{0,1:T(8,128)(2,1)S(1)} %get-tuple-element.774) | copy-start | bytes 6291460
  244.4 2.5 copy-start.35
  251.7 12.5 %copy-start.25 = (f32[1024,256]{0,1:T(8,128)S(1)}, f32[1024,256]{0,1:T(8,128)}, u32[]{:S(2)}) copy-start(f32[1024,256]{0,1:T(8,128)} %copy-done.24) | copy-start | bytes 3145732
  251.7 12.5 %copy-start.27 = (f32[1024,256]{0,1:T(8,128)S(1)}, f32[1024,256]{0,1:T(8,128)}, u32[]{:S(2)}) copy-start(f32[1024,256]{0,1:T(8,128)} %copy-done.26) | copy-start | bytes 3145732
  251.7 12.5 %copy-start.41 = (bf16[1024,1536]{1,0:T(8,128)(2,1)S(1)}, bf16[1024,1536]{1,0:T(8,128)(2,1)}, u32[]{:S(2)}) copy-start(bf16[1024,1536]{1,0:T(8,128)(2,1)} %get-tuple-element.570) | copy-start | bytes 9437188
  262.1 3.5 copy-start.11
  262.1 3.8 copy-start.20
  262.1 4.1 copy-start.23
  271.2 50.1 %copy-start.4 = (f32[256,1536]{1,0:T(8,128)S(1)}, f32[256,1536]{1,0:T(8,128)}, u32[]{:S(2)}) copy-start(f32[256,1536]{1,0:T(8,128)} %get-tuple-element.565) | copy-start | bytes 4718596
  321.5 2.5 copy-start.13
  321.7 2.8 copy-start.29
  324.5 1.1 copy-start.6
  325.6 4.7 copy-start.15
  341.5 3.6 copy-start.3
  341.5 3.6 copy-start.16
  359.6 1.0 copy-start.12
  360.6 45.0 %copy-start.37 = (f32[256,128]{1,0:T(8,128)S(1)}, f32[256,128]{1,0:T(8,128)}, u32[]{:S(2)}) copy-start(f32[256,128]{1,0:T(8,128)} %get-tuple-element.579) | copy-start | bytes 393220
  360.6 45.2 %copy-start.36 = (f32[256,128]{1,0:T(8,128)S(1)}, f32[256,128]{1,0:T(8,128)}, u32[]{:S(2)}) copy-start(f32[256,128]{1,0:T(8,128)} %get-tuple-element.578) | copy-start | bytes 393220
  404.4 0.9 copy-start.2
  405.4 0.7 copy-start.31
  405.9 0.7 copy-start.33
  406.1 0.8 copy-start.17
  406.8 6.4 %copy-start.39 = (bf16[1536]{0:T(1024)(128)(2,1)S(1)}, bf16[1536]{0:T(1024)(128)(2,1)}, u32[]{:S(2)}) copy-start(bf16[1536]{0:T(1024)(128)(2,1)} %get-tuple-element.737) | copy-start | bytes 9220
  406.8 6.4 %copy-start.9 = (bf16[256,1536]{1,0:T(8,128)(2,1)S(1)}, bf16[256,1536]{1,0:T(8,128)(2,1)}, u32[]{:S(2)}) copy-start(bf16[256,1536]{1,0:T(8,128)(2,1)} %input_ref.1) | copy-start | bytes 2359300
  410.2 3.2 copy-start.38
  410.3 4.2 copy-start.30
  410.3 7.4 %copy-start.7 = (f32[256,1536]{1,0:T(8,128)S(1)}, f32[256,1536]{1,0:T(8,128)}, u32[]{:S(2)}) copy-start(f32[256,1536]{1,0:T(8,128)} %copy-done.6) | copy-start | bytes 4718596
  417.7 2.0 copy-start.14
  417.7 2.0 copy-start.18
  417.7 2.0 copy-start.32
  417.7 2.0 copy-start.34
  424.0 4.5 copy-start.21
  424.0 120.3 %all-to-all-start = ((bf16[4,96,2048]{2,1,0:T(8,128)(2,1)}), bf16[4,96,2048]{2,1,0:T(8,128)(2,1)}, u32[]{:S(2)}, u32[]{:S(2)}) async-start(bf16[4,96,2048]{2,1,0:T(8,128)(2,1)} %bitcast.115), calls=%async_computation.1 | async-start | bytes 3145728 | tf_op jit(solution)/shard_map/all_to_all | solution.py:77
  532.6 0.9 copy-start
  532.6 8.0 %copy-start.40 = (f32[256]{0:T(256)S(1)}, f32[256]{0:T(256)}, u32[]{:S(2)}) copy-start(f32[256]{0:T(256)} %get-tuple-element.738) | copy-start | bytes 3076
  536.9 3.0 copy-start.1
  536.9 5.2 copy-start.5
  536.9 5.2 copy-start.8
  536.9 5.2 copy-start.10
Sparse Core Ops, SparseCore 0:
  240.4 86.6 reduce-scatter.1

commit v3 on v2

--- a/solution.py
+++ b/solution.py
@@ -101,7 +101,7 @@
 def front_kernel(
     attn_ref, gate_ref, up_ref, down_ref, outer_ref, routes_ref, input_ref, segment_ref, freq_ref,
     expert_out, outer_out, routes_out, normed2_out,
-    attn_out, normed1_out, query_out, pair_out, mixed_out, log_out, middle_out, cos_out, sin_out,
+    attn_out, normed1_out, query_out, pair_out, mixed_out, log_out, middle_out, cos_out, sin_out, extra_out,
     query_s, key_s, value_s, mixed_s, bias_s, part_s, other_s, normed2_s,
     local_sem, z_send, z_recv, plane_send, plane_recv, relay_send, relay_recv, core_send, core_recv,
     key_send, key_recv, pair_send, pair_recv,
@@ -313,7 +313,7 @@
         total = jnp.sum(weights, -1, keepdims=True)
         summed = jnp.dot(weights.astype(low), value_s[g], preferred_element_type=jnp.float32)
         mixed_s[h] = (summed / total).astype(low)
-        log_out[h] = top + jnp.log(total)
+        log_out[h] = jnp.broadcast_to(top + jnp.log(total), (tokens, 128)).T[:1, :]
         return carry
 
     lax.fori_loop(0, heads, attend, 0)
@@ -360,6 +360,7 @@
         remote(
             expert_out.at[mine], expert_out.at[mine], z_send.at[1, d - 1], z_recv.at[1, d - 1], core
         ).wait_send()
+    extra_out[...] = attn_out[:, qkv_width : qkv_width + 128]
     own_outer.wait()
     own_routes.wait()
     own_normed2.wait()
@@ -391,13 +392,14 @@
             shape((tokens, heads * HD), low),
             shape((length, 2 * key_heads * HD), low),
             shape((tokens, heads * HD), low),
-            shape((heads, tokens, 1), jnp.float32),
+            shape((heads, 1, tokens), jnp.float32),
             shape((tokens, model), jnp.float32),
             shape((tokens, 128), jnp.float32),
             shape((tokens, 128), jnp.float32),
+            shape((total, 128), low),
         ),
         in_specs=[anywhere] * 6 + [vmem] * 3,
-        out_specs=(anywhere,) * 4 + (vmem,) * 9,
+        out_specs=(anywhere,) * 4 + (vmem,) * 10,
         scratch_shapes=[
             pltpu.VMEM((heads, tokens, HD), low),
             pltpu.VMEM((key_heads, length, HD), low),
@@ -447,15 +449,14 @@
 class ZSum:
     size = 9
 
-    def __init__(self, part, out, scratch, sent):
-        self.part, self.out, self.sent = part, out, sent
+    def __init__(self, part, scratch, sent, own=None):
+        self.part, self.own, self.sent = part, own, sent
         (
             self.core_in, self.z_out, self.z_in, self.core_send, self.core_recv,
             self.z_send, self.z_recv, self.back_send, self.back_recv,
         ) = scratch
-        self.ep = self.core_in.shape[0]
+        self.ep, self.half = self.core_in.shape[0], self.core_in.shape[1]
         self.f, self.c, self.t = lax.axis_index("fsdp"), lax.axis_index("ctx"), lax.axis_index("tp")
-        self.half = out.shape[0] // 2
         self.core = at_device(self.f, self.c, 1 - self.t)
 
     def peer(self, distance):
@@ -463,94 +464,117 @@
 
     def place(self, fsdp, part):
         return pl.ds(pl.multiple_of(fsdp * 2 * self.half + part * self.half, 16), self.half)
+
+    def rows(self, part):
+        return pl.ds(pl.multiple_of(part * self.half, 16), self.half)
 
     def send(self, copy):
         copy.start()
         self.sent.append(copy)
 
-    def to_core(self):
-        for d in list(range(1, self.ep)) + [0]:
-            self.send(
-                remote(
-                    self.part.at[self.place(self.peer(d), 1 - self.t)], self.core_in.at[d],
-                    self.core_send.at[d], self.core_recv.at[d], self.core,
-                )
+    def to_core(self, d):
+        self.send(
+            remote(
+                self.part.at[self.place(self.peer(d), 1 - self.t)], self.core_in.at[d],
+                self.core_send.at[d], self.core_recv.at[d], self.core,
             )
+        )
 
     def added(self, d):
         landing = self.core_in.at[d]
         remote(landing, landing, self.core_send.at[d], self.core_recv.at[d], self.core).wait_recv()
-        mine = self.part[self.place(self.peer(d), self.t), :]
+        mine = self.part[self.place(self.peer(d), self.t), :] if self.own is None else self.own[d]
         return mine.astype(jnp.float32) + self.core_in[d].astype(jnp.float32)
 
-    def to_z(self):
-        for d in range(1, self.ep):
-            self.z_out[d - 1] = self.added(d).astype(self.z_out.dtype)
-            self.send(
-                remote(
-                    self.z_out.at[d - 1], self.z_in.at[d - 1], self.z_send.at[d - 1], self.z_recv.at[d - 1],
-                    at_device(self.peer(d), self.c, self.t),
-                )
+    def to_z(self, d):
+        self.z_out[d - 1] = self.added(d).astype(self.z_out.dtype)
+        self.send(
+            remote(
+                self.z_out.at[d - 1], self.z_in.at[d - 1], self.z_send.at[d - 1], self.z_recv.at[d - 1],
+                at_device(self.peer(d), self.c, self.t),
             )
-
-    def from_z(self):
-        rows = pl.ds(pl.multiple_of(self.t * self.half, 16), self.half)
-        self.out[rows, :] = self.added(0)
+        )
+
+    def collect(self):
+        total = self.added(0)
         for d in range(1, self.ep):
             landing = self.z_in.at[d - 1]
             remote(landing, landing, self.z_send.at[d - 1], self.z_recv.at[d - 1], self.core).wait_recv()
-            self.out[rows, :] += self.z_in[d - 1].astype(jnp.float32)
-        mine = self.out.at[rows]
+            total = total + self.z_in[d - 1].astype(jnp.float32)
+        return total
+
+    def share(self, out):
+        mine = out.at[self.rows(self.t)]
         self.send(remote(mine, mine, self.back_send, self.back_recv, self.core))
 
-    def finish(self):
-        other = self.out.at[pl.ds(pl.multiple_of((1 - self.t) * self.half, 16), self.half)]
+    def finish(self, out):
+        other = out.at[self.rows(1 - self.t)]
         remote(other, other, self.back_send, self.back_recv, self.core).wait_recv()
 
 
-def plane_sum_scratch(ep, rows, width, low):
-    cut = -(-width // 256) * 128
+def shard_sum_scratch(ep, rows, width, low, along_z=True):
+    cut = first_columns(width)
+    widths = [cut] if cut == width else [cut, width - cut]
     dma = pltpu.SemaphoreType.DMA
-    return [
-        pltpu.VMEM((ep, 2, rows, cut), low),
-        pltpu.VMEM((ep, 2, rows, width - cut), low),
-        pltpu.VMEM((ep, rows, cut), low),
-        pltpu.VMEM((ep, rows, width - cut), low),
-        pltpu.VMEM((ep, rows, cut), low),
-        pltpu.VMEM((ep, rows, width - cut), low),
-        dma((2, ep, 2)),
-        dma((2, ep, 2)),
-        dma((2, ep)),
-        dma((2, ep)),
+    scratch = []
+    for part in widths:
+        scratch += [pltpu.VMEM((ep, 2, rows, part), low), pltpu.VMEM((ep, rows, part), low)]
+        if along_z:
+            scratch.append(pltpu.VMEM((ep - 1, rows, part), low))
+    return scratch + [
+        dma((2, ep, 2)), dma((2, ep, 2)), dma((2, ep)), dma((2, ep)), dma((2, ep)), dma((2, ep))
     ]
 
 
-class PlaneSum:
-    size = 10
-
-    def __init__(self, part, rows, scratch, sent):
-        self.part, self.rows, self.sent = part, rows, sent
-        self.first_in, self.second_out, self.second_in = scratch[0:2], scratch[2:4], scratch[4:6]
-        self.first_send, self.first_recv, self.second_send, self.second_recv = scratch[6:10]
+def first_columns(width):
+    return width if width == 128 else -(-width // 256) * 128
+
+
+class ShardSum:
+    def __init__(self, part, rows, width, scratch, sent, own=None, relay=None):
+        self.part, self.rows, self.sent, self.own, self.relay = part, rows, sent, own, relay
+        cut = first_columns(width)
+        self.columns = [pl.ds(0, cut)] + ([] if cut == width else [pl.ds(cut, width - cut)])
+        self.ways = range(len(self.columns))
+        (
+            self.first_send, self.first_recv, self.second_send, self.second_recv, self.z_send, self.z_recv
+        ) = scratch[-6:]
+        each = (len(scratch) - 6) // len(self.columns)
+        self.first_in = [scratch[each * way] for way in self.ways]
+        self.second_in = [scratch[each * way + 1] for way in self.ways]
+        self.z_in = [scratch[each * way + 2] for way in self.ways] if each == 3 else None
         self.ep = self.first_in[0].shape[0]
         self.f, self.c, self.t = lax.axis_index("fsdp"), lax.axis_index("ctx"), lax.axis_index("tp")
-        cut = self.first_in[0].shape[-1]
-        self.columns = (pl.ds(0, cut), pl.ds(cut, part.shape[1] - cut))
         self.neighbours = (at_device(self.f, self.c ^ 1, self.t), at_device(self.f, self.c ^ 2, self.t))
         self.order = list(range(1, self.ep)) + [0]
 
+    def peer(self, distance):
+        return lax.rem(self.f + distance, self.ep)
+
     def block(self, distance, ctx, way):
-        start = (lax.rem(self.f + distance, self.ep) * 4 + ctx) * self.rows
+        start = (self.peer(distance) * 4 + ctx) * self.rows
         return pl.ds(pl.multiple_of(start, 16), self.rows), self.columns[way]
 
     def send(self, copy):
         copy.start()
         self.sent.append(copy)
 
+    def load(self, sem):
+        for d in range(self.ep):
+            for way in self.ways:
+                for target, ctx in ((self.own, self.c), (self.relay, self.c ^ (2 >> way))):
+                    pltpu.make_async_copy(
+                        self.part.at[self.block(d, ctx, way)], target.at[d, :, self.columns[way]], sem
+                    ).start()
+
+    def loaded(self, sem):
+        for target in (self.own, self.relay):
+            pltpu.make_async_copy(target, target, sem).wait()
+
     def first(self):
         for d in self.order:
             for number in range(2):
-                for way in range(2):
+                for way in self.ways:
                     target = self.c ^ 3 if number == 0 else self.c ^ (1 << way)
                     self.send(
                         remote(
@@ -560,35 +584,85 @@
                         )
                     )
 
-    def second(self):
-        for d in self.order:
-            for way in range(2):
-                for number in range(2):
-                    landing = self.first_in[way].at[d, number]
-                    remote(
-                        landing, landing, self.first_send.at[way, d, number],
-                        self.first_recv.at[way, d, number], self.neighbours[way],
-                    ).wait_recv()
-                own = self.part[self.block(d, self.c ^ (2 >> way), way)]
-                added = own.astype(jnp.float32) + self.first_in[way][d, 0].astype(jnp.float32)
-                self.second_out[way][d] = added.astype(self.part.dtype)
-                self.send(
-                    remote(
-                        self.second_out[way].at[d], self.second_in[way].at[d],
-                        self.second_send.at[way, d], self.second_recv.at[way, d], self.neighbours[1 - way],
-                    )
+    def second(self, d):
+        for way in self.ways:
+            for number in range(2):
+                landing = self.first_in[way].at[d, number]
+                remote(
+                    landing, landing, self.first_send.at[way, d, number],
+                    self.first_recv.at[way, d, number], self.neighbours[way],
+                ).wait_recv()
+            if self.relay is None:
+                term = self.part[self.block(d, self.c ^ (2 >> way), way)]
+            else:
+                term = self.relay[d, :, self.columns[way]]
+            added = term.astype(jnp.float32) + self.first_in[way][d, 0].astype(jnp.float32)
+            self.first_in[way][d, 0] = added.astype(self.part.dtype)
+            self.send(
+                remote(
+                    self.first_in[way].at[d, 0], self.second_in[way].at[d],
+                    self.second_send.at[way, d], self.second_recv.at[way, d], self.neighbours[1 - way],
                 )
+            )
 
     def total(self, d, way):
         landing = self.second_in[way].at[d]
         remote(
             landing, landing, self.second_send.at[way, d], self.second_recv.at[way, d], self.neighbours[1 - way]
         ).wait_recv()
+        term = self.part[self.block(d, self.c, way)] if self.own is None else self.own[d, :, self.columns[way]]
         return (
-            self.part[self.block(d, self.c, way)].astype(jnp.float32)
+            term.astype(jnp.float32)
             + self.first_in[way][d, 1].astype(jnp.float32)
             + self.second_in[way][d].astype(jnp.float32)
         )
+
+    def to_z(self, d, out):
+        for way in self.ways:
+            total = self.total(d, way)
+            if d == 0:
+                out[:, self.columns[way]] = total
+                continue
+            self.first_in[way][d, 1] = total.astype(self.part.dtype)
+            self.send(
+                remote(
+                    self.first_in[way].at[d, 1], self.z_in[way].at[d - 1],
+                    self.z_send.at[way, d], self.z_recv.at[way, d], at_device(self.peer(d), self.c, self.t),
+                )
+            )
+
+    def from_z(self, out):
+        for way in self.ways:
+            for d in range(1, self.ep):
+                landing = self.z_in[way].at[d - 1]
+                remote(
+                    landing, landing, self.z_send.at[way, d], self.z_recv.at[way, d], self.neighbours[0]
+                ).wait_recv()
+                out[:, self.columns[way]] += self.z_in[way][d - 1].astype(jnp.float32)
+
+    def swap_z(self, d, out):
+        for way in self.ways:
+            self.first_in[way][d, 1] = self.total(d, way).astype(self.part.dtype)
+            source, target = self.first_in[way].at[d, 1], out.at[self.f, :, self.columns[way]]
+            if d == 0:
+                pltpu.make_async_copy(source, target, self.z_send.at[way, 0]).start()
+            else:
+                self.send(
+                    remote(
+                        source, target, self.z_send.at[way, d], self.z_recv.at[way, d],
+                        at_device(self.peer(d), self.c, self.t),
+                    )
+                )
+
+    def swapped_z(self, out):
+        for way in self.ways:
+            target = out.at[self.f, :, self.columns[way]]
+            pltpu.make_async_copy(self.first_in[way].at[0, 1], target, self.z_send.at[way, 0]).wait()
+            for d in range(1, self.ep):
+                landing = out.at[self.peer(self.ep - d), :, self.columns[way]]
+                remote(
+                    landing, landing, self.z_send.at[way, d], self.z_recv.at[way, d], self.neighbours[0]
+                ).wait_recv()
 
 
 def all_partners(ep):
@@ -597,204 +671,430 @@
     return line + [at_device(f, c ^ 1, t), at_device(f, c ^ 2, t), at_device(f, c, 1 - t)]
 
 
-def back_kernel(part_ref, down_ref, sum_ref, down_out, *scratch):
-    ep, rows = down_out.shape[0], down_out.shape[1]
+def experts_kernel(
+    tokens_ref, outer_ref, routes_ref, extra_ref, weight_ref,
+    returned_ref, mixture_out, sums_out, gates_out,
+    gates_s, gated_s, side_s, part_s, *scratch,
+):
+    ep = lax.axis_size("fsdp")
+    f = lax.axis_index("fsdp")
+    low = jnp.bfloat16
+    reach, model = tokens_ref.shape
+    span = weight_ref.shape[1] // 3
+    tokens = reach // ep
+    local = EXPERTS // ep
+    hidden = span // local
     sent = []
-    tokens = ZSum(part_ref, sum_ref, scratch[: ZSum.size], sent)
-    plane = PlaneSum(down_ref, rows, scratch[ZSum.size :], sent)
-    greet(all_partners(ep))
-    tokens.to_core()
-    plane.first()
-    tokens.to_z()
-    plane.second()
-    tokens.from_z()
-    for d in plane.order:
-        for way in range(2):
-            down_out[plane_row(d, ep), :, plane.columns[way]] = plane.total(d, way).astype(down_out.dtype)
-    tokens.finish()
+    back = ZSum(part_s, scratch, sent)
+    partners = all_partners(ep)
+    greet(partners[: ep - 1] + partners[-1:])
+
+    lane = lax.broadcasted_iota(jnp.int32, (reach, 128), 1)
+    chosen = routes_ref[:, 0:1] == lane
+    for k in range(1, routes_ref.shape[1]):
+        chosen = chosen | (routes_ref[:, k : k + 1] == lane)
+    logits = jnp.dot(tokens_ref[...], extra_ref[...], preferred_element_type=jnp.float32)
+    logits = jnp.where(chosen, logits, MASKED_SCORE)
+    lifted = jnp.where(chosen, jnp.exp(logits - jnp.max(logits, -1, keepdims=True)), 0.0)
+    gates_s[...] = lifted / jnp.sum(lifted, -1, keepdims=True)
+    own = pl.ds(pl.multiple_of(f * tokens, 16), tokens)
+    gates_out[...] = gates_s[own, :]
+    small_lane = lax.broadcasted_iota(jnp.int32, (tokens, 128), 1)
+
+    def block(d):
+        here = pl.ds(pl.multiple_of(back.peer(d) * tokens, 16), tokens)
+        gates = gates_s[here, :]
+        dgates = jnp.zeros((tokens, 128), jnp.float32)
+        for e in range(local):
+            at = slice(e * hidden, (e + 1) * hidden)
+            mine = small_lane == f * local + e
+            gate = jnp.sum(jnp.where(mine, gates, 0.0), -1, keepdims=True)
+            former = jnp.dot(tokens_ref[here, :], weight_ref[:, at], preferred_element_type=jnp.float32)
+            at_up = slice(span + e * hidden, span + (e + 1) * hidden)
+            latter = jnp.dot(tokens_ref[here, :], weight_ref[:, at_up], preferred_element_type=jnp.float32)
+            at_down = slice(2 * span + e * hidden, 2 * span + (e + 1) * hidden)
+            grad = jnp.dot(outer_ref[here, :], weight_ref[:, at_down], preferred_element_type=jnp.float32)
+            logistic = 1.0 / (1.0 + jnp.exp(-former))
+            active = former * logistic
+            value = (active * latter).astype(low).astype(jnp.float32)
+            gated_s[here, at] = (value * gate).astype(low)
+            picked = jnp.sum(value * grad, -1, keepdims=True)
+            dgates = jnp.where(mine & (gate > 0.0), picked, dgates)
+            grad = grad * gate
+            side_s[here, at] = (grad * latter * logistic * (1.0 + former * (1.0 - logistic))).astype(low)
+            side_s[here, at_up] = (grad * active).astype(low)
+        high = dgates.astype(low).astype(jnp.float32)
+        part_s[here, model:] = (high + pltpu.roll(dgates - high, EXPERTS, 1)).astype(low)
+
+        def tile(n, carry):
+            at = pl.ds(pl.multiple_of(n * 256, 256), 256)
+            part_s[here, at] = lax.dot_general(
+                side_s[here, :], weight_ref[at, : 2 * span], (((1,), (1,)), ((), ())),
+                preferred_element_type=jnp.float32,
+            ).astype(low)
+            mixture_out[here, at] = lax.dot_general(
+                gated_s[here, :], weight_ref[at, 2 * span :], (((1,), (1,)), ((), ())),
+                preferred_element_type=jnp.float32,
+            ).astype(low)
+            return carry
+
+        lax.fori_loop(0, model // 256, tile, 0)
+
+    order = list(range(1, ep)) + [0]
+    for step, d in enumerate(order):
+        block(d)
+        back.to_core(d)
+        if step > 0:
+            back.to_z(order[step - 1])
+
+    def sums(n, carry):
+        at = pl.ds(pl.multiple_of(n * 256, 256), 256)
+        over = (((0,), (0,)), ((), ()))
+        sums_out[at, : 2 * span] = lax.dot_general(
+            tokens_ref[:, at], side_s[...], over, preferred_element_type=jnp.float32
+        ).astype(low)
+        sums_out[at, 2 * span :] = lax.dot_general(
+            outer_ref[:, at], gated_s[...], over, preferred_element_type=jnp.float32
+        ).astype(low)
+        return carry
+
+    lax.fori_loop(0, model // 256, sums, 0)
+    returned_ref[back.rows(back.t), :] = back.collect()
+    back.share(returned_ref)
+    back.finish(returned_ref)
     for copy in sent:
         copy.wait_send()
 
 
-def plane_row(distance, ep):
-    return lax.rem(lax.axis_index("fsdp") + distance, ep)
-
-
-def sum_back(part, down, collective_id):
+def run_experts(tokens_all, outer_all, routes_all, extra, weights, collective_id):
     ep = lax.axis_size("fsdp")
-    rows = down.shape[0] // (4 * ep)
-    tokens, width = part.shape[0] // ep, part.shape[1]
+    reach, model = tokens_all.shape
+    tokens, low = reach // ep, tokens_all.dtype
+    span = weights.shape[1] // 3
     vmem = pl.BlockSpec(memory_space=pltpu.VMEM)
+    shape = jax.ShapeDtypeStruct
     return pl.pallas_call(
-        back_kernel,
+        experts_kernel,
         out_shape=(
-            jax.ShapeDtypeStruct((tokens, width), jnp.float32),
-            jax.ShapeDtypeStruct((ep, rows, down.shape[1]), down.dtype),
+            shape((tokens, model + 128), jnp.float32),
+            shape((reach, model), low),
+            shape(weights.shape, low),
+            shape((tokens, 128), jnp.float32),
         ),
-        in_specs=[vmem] * 2,
-        out_specs=(vmem,) * 2,
-        scratch_shapes=z_sum_scratch(ep, tokens, width, part.dtype)
-        + plane_sum_scratch(ep, rows, down.shape[1], down.dtype),
+        in_specs=[vmem] * 5,
+        out_specs=(vmem,) * 4,
+        scratch_shapes=[
+            pltpu.VMEM((reach, 128), jnp.float32),
+            pltpu.VMEM((reach, span), low),
+            pltpu.VMEM((reach, 2 * span), low),
+            pltpu.VMEM((reach, model + 128), low),
+        ]
+        + z_sum_scratch(ep, tokens, model + 128, low),
         compiler_params=pltpu.CompilerParams(
-            collective_id=collective_id, has_side_effects=True, vmem_limit_bytes=48 * 1024 * 1024
+            collective_id=collective_id, has_side_effects=True, vmem_limit_bytes=60 * 1024 * 1024
         ),
-        cost_estimate=lasting(45),
-        name="sum_back",
-    )(part, down)
-
-
-def keys_kernel(part_ref, down_ref, sum_ref, down_out, landing, send, recv, z_send, z_recv):
-    ep = down_ref.shape[0]
+        cost_estimate=lasting(70),
+        name="experts",
+    )(tokens_all, outer_all, routes_all, extra, weights)
+
+
+def rear_kernel(
+    returned_ref, gates_ref, middle_ref, input_ref, outer_ref, normed1_ref, query_ref, pair_ref, mixed_ref,
+    log_ref, cos_ref, sin_ref, segment_ref, extra_ref, mixture_ref, sums_ref, attn_ref,
+    input_grad, layer_out, qkv_out, wo_out, small_out, expert_out,
+    wo_s, qkv_s, small_s, query_s, grad_s, mixed_s, key_s, value_s, bias_s, query_grad_s, key_grad_s, value_grad_s,
+    pair_s, landing_s, back_s, attn_grad_s, part_s, other_s, logit_s, gains_s, mixture_s, own_s, relay_s,
+    local_sem, key_send, key_recv, pair_send, pair_recv, *scratch,
+):
+    ep, rows = expert_out.shape[0], expert_out.shape[1]
     f, c, t = lax.axis_index("fsdp"), lax.axis_index("ctx"), lax.axis_index("tp")
-    tokens = sum_ref.shape[0]
-
-    def peer(distance):
-        return lax.rem(f + distance, ep)
-
+    low = jnp.bfloat16
+    tokens, model = input_ref.shape
+    heads, key_heads = query_s.shape[0], key_s.shape[0]
+    groups = heads // key_heads
+    width, kv_width = heads * HD, key_heads * HD
+    qkv_width = width + 2 * kv_width
+    sent = []
+    mixture = ZSum(mixture_ref, scratch[: ZSum.size], sent, mixture_s)
+    scratch = scratch[ZSum.size :]
+    size = len(shard_sum_scratch(ep, rows, 256, low, False))
+    experts = ShardSum(sums_ref, rows, sums_ref.shape[1], scratch[:size], sent, own_s, relay_s)
+    scratch = scratch[size:]
+    size = len(shard_sum_scratch(ep, rows, 256, low))
+    wo = ShardSum(wo_s, rows, width, scratch[:size], sent)
+    qkv = ShardSum(qkv_s, rows, qkv_width, scratch[size : 2 * size], sent)
+    small = ShardSum(small_s, rows, 128, scratch[2 * size :], sent)
+    partners = all_partners(ep)
     plane = [at_device(f, c ^ k, t) for k in range(1, 4)]
-    greet([at_device(peer(d), c, t) for d in range(1, ep)] + plane)
-    sent = []
+    core = partners[-1]
+
+    copies = [
+        pltpu.make_async_copy(attn_ref.at[:, pl.ds(qkv_width + 128, width)], wo_s, local_sem.at[0]),
+        pltpu.make_async_copy(attn_ref.at[:, pl.ds(0, qkv_width)], qkv_s, local_sem.at[1]),
+    ]
+    for copy in copies:
+        copy.start()
+    for d in range(ep):
+        pltpu.make_async_copy(
+            mixture_ref.at[mixture.place(mixture.peer(d), t)], mixture_s.at[d], local_sem.at[2]
+        ).start()
+    experts.load(local_sem.at[3])
+    greet(partners + plane[2:])
+    for d in experts.order:
+        mixture.to_core(d)
+    experts.first()
+
+    small_lane = lax.broadcasted_iota(jnp.int32, (tokens, 128), 1)
+    gains = extra_ref[...].astype(jnp.float32).T
+    gain_one, gain_two = gains[EXPERTS : EXPERTS + 1, :], gains[EXPERTS + 1 : EXPERTS + 2, :]
+    tail = returned_ref[:, model:]
+    picked = jnp.where(small_lane < EXPERTS, tail + pltpu.roll(tail, 128 - EXPERTS, 1), 0.0)
+    gates = gates_ref[...]
+    logit_grad = (gates * (picked - jnp.sum(gates * picked, -1, keepdims=True))).astype(low)
+    logit_s[...] = logit_grad
+    second_grad = returned_ref[:, :model] + lax.dot_general(
+        logit_grad, extra_ref[...], (((1,), (1,)), ((), ())), preferred_element_type=jnp.float32
+    )
+    middle = middle_ref[...]
+    inverse = lax.rsqrt(jnp.mean(middle * middle, -1, keepdims=True) + EPSILON)
+    scaled = second_grad * gain_two
+    mean_term = jnp.mean(scaled * middle, -1, keepdims=True)
+    gains_s[1:2, :] = jnp.sum(second_grad * middle * inverse, 0, keepdims=True)
+    middle_grad = outer_ref[...].astype(jnp.float32) + (
+        inverse * scaled - middle * (inverse * inverse * inverse) * mean_term
+    )
+    input_grad[...] = middle_grad
+    attn_grad_s[...] = middle_grad.astype(low)
+
+    copies[0].wait()
+    for start in range(0, width, 256):
+        tile = jnp.dot(
+            attn_grad_s[...], wo_s[:, start : start + 256], preferred_element_type=jnp.float32
+        ).astype(low)
+        for side in range(0, 256, HD):
+            grad_s[(start + side) // HD] = tile[:, side : side + HD]
+
+    def wo_sums(n, carry):
+        at = pl.ds(pl.multiple_of(n * 256, 256), 256)
+        wo_s[at, :] = lax.dot_general(
+            attn_grad_s[:, at], mixed_ref[...], (((0,), (0,)), ((), ())), preferred_element_type=jnp.float32
+        ).astype(low)
+        return carry
+
+    lax.fori_loop(0, model // 256, wo_sums, 0)
+    pltpu.make_async_copy(mixture_s, mixture_s, local_sem.at[2]).wait()
+    for d in range(1, ep):
+        mixture.to_z(d)
+    wo.first()
+
+    length = segment_ref.shape[1]
+    seg_keys = jnp.broadcast_to(segment_ref[...].astype(jnp.float32), (128, length)).T[:, :1]
+    seg_queries = segment_ref[:, pl.ds(pl.multiple_of(c * tokens, 128), tokens)].astype(jnp.float32)
+    key_order = lax.broadcasted_iota(jnp.int32, (length, tokens), 0)
+    query_order = lax.broadcasted_iota(jnp.int32, (length, tokens), 1) + c * tokens
+    bias_s[...] = jnp.where((seg_keys == seg_queries) & (key_order <= query_order), 0.0, MASKED_SCORE)
+    for h in range(heads):
+        query_s[h] = query_ref[:, h * HD : (h + 1) * HD]
+        mixed_s[h] = mixed_ref[:, h * HD : (h + 1) * HD]
+    for g in range(key_heads):
+        key_s[g] = pair_ref[:, g * HD : (g + 1) * HD]
+        value_s[g] = pair_ref[:, kv_width + g * HD : kv_width + (g + 1) * HD]
+    across = (((1,), (1,)), ((), ()))
+
+    def attend_back(g, carry):
+        key_grad = jnp.zeros((length, HD), jnp.float32)
+        value_grad = jnp.zeros((length, HD), jnp.float32)
+        for number in range(groups):
+            h = g * groups + number
+            query = query_s[h] * jnp.asarray(HD**-0.5, low)
+            grad = grad_s[h]
+            scores = lax.dot_general(key_s[g], query, across, preferred_element_type=jnp.float32) + bias_s[...]
+            probs = jnp.exp(scores - log_ref[h])
+            value_grad += jnp.dot(probs.astype(low), grad, preferred_element_type=jnp.float32)
+            prob_grad = lax.dot_general(value_s[g], grad, across, preferred_element_type=jnp.float32)
+            delta = jnp.sum((grad.astype(jnp.float32) * mixed_s[h].astype(jnp.float32)).T, 0, keepdims=True)
+            score_grad = (probs * (prob_grad - delta)).astype(low)
+            key_grad += jnp.dot(score_grad, query, preferred_element_type=jnp.float32)
+            query_grad = lax.dot_general(
+                key_s[g], score_grad, (((0,), (0,)), ((), ())), preferred_element_type=jnp.float32
+            )
+            query_grad_s[h] = query_grad.T * (HD**-0.5)
+        key_grad_s[g] = key_grad.astype(low)
+        value_grad_s[g] = value_grad.astype(low)
+        return carry
+
+    lax.fori_loop(0, key_heads, attend_back, 0)
+    for g in range(key_heads):
+        pair_s[:, g * HD : (g + 1) * HD] = key_grad_s[g]
+        pair_s[:, kv_width + g * HD : kv_width + (g + 1) * HD] = value_grad_s[g]
     for k in (3, 1, 2):
         place = pl.ds(pl.multiple_of((c ^ k) * tokens, 16), tokens)
-        copy = remote(part_ref.at[place], landing.at[k - 1], send.at[k - 1], recv.at[k - 1], plane[k - 1])
+        copy = remote(pair_s.at[place], landing_s.at[k - 1], key_send.at[k - 1], key_recv.at[k - 1], plane[k - 1])
         copy.start()
         sent.append(copy)
-    for d in range(1, ep):
-        copy = remote(
-            down_ref.at[peer(d)], down_out.at[f], z_send.at[d - 1], z_recv.at[d - 1], at_device(peer(d), c, t)
-        )
-        copy.start()
-        sent.append(copy)
-    down_out[f] = down_ref[f]
-    sum_ref[...] = part_ref[pl.ds(pl.multiple_of(c * tokens, 16), tokens), :].astype(jnp.float32)
+    first_half = lax.rem(small_lane, HD) < HD // 2
+
+    def turned_back(tile):
+        swapped = jnp.where(first_half, pltpu.roll(tile, 128 - HD // 2, 1), pltpu.roll(tile, HD // 2, 1))
+        return tile * cos_ref[...] - swapped * sin_ref[...]
+
+    for start in range(0, width, 128):
+        tile = jnp.concatenate([query_grad_s[start // HD], query_grad_s[start // HD + 1]], 1)
+        back_s[:, start : start + 128] = turned_back(tile).astype(low)
+
+    experts.loaded(local_sem.at[3])
+    for d in experts.order:
+        experts.second(d)
+    total = mixture.collect()
+    half = mixture.rows(t)
+    layer_out[half, :] = (middle_ref[half, :] + total).astype(low)
+    mixture.share(layer_out)
+
+    pair = pair_s[pl.ds(pl.multiple_of(c * tokens, 16), tokens), :].astype(jnp.float32)
     for k in (1, 2, 3):
-        block = landing.at[k - 1]
-        remote(block, block, send.at[k - 1], recv.at[k - 1], plane[k - 1]).wait_recv()
-        sum_ref[...] += landing[k - 1].astype(jnp.float32)
-    for d in range(1, ep):
-        block = down_out.at[peer(ep - d)]
-        remote(block, block, z_send.at[d - 1], z_recv.at[d - 1], plane[0]).wait_recv()
+        block = landing_s.at[k - 1]
+        remote(block, block, key_send.at[k - 1], key_recv.at[k - 1], plane[k - 1]).wait_recv()
+        pair = pair + landing_s[k - 1].astype(jnp.float32)
+    for start in range(0, kv_width, 128):
+        back_s[:, width + start : width + start + 128] = turned_back(pair[:, start : start + 128]).astype(low)
+    back_s[:, width + kv_width :] = pair[:, kv_width:].astype(low)
+    copies[1].wait()
+    for start in range(0, model, 256):
+        part_s[:, start : start + 256] = lax.dot_general(
+            back_s[...], qkv_s[start : start + 256, :], across, preferred_element_type=jnp.float32
+        ).astype(low)
+    exchange = remote(part_s, other_s, pair_send, pair_recv, core)
+    exchange.start()
+    sent.append(exchange)
+
+    def qkv_sums(n, carry):
+        at = pl.ds(pl.multiple_of(n * 256, 256), 256)
+        qkv_s[at, :] = lax.dot_general(
+            normed1_ref[:, at], back_s[...], (((0,), (0,)), ((), ())), preferred_element_type=jnp.float32
+        ).astype(low)
+        return carry
+
+    lax.fori_loop(0, model // 256, qkv_sums, 0)
+    qkv.first()
+    for d in wo.order:
+        wo.second(d)
+    for d in experts.order:
+        experts.swap_z(d, expert_out)
+
+    exchange.wait_recv()
+    first_grad = part_s[...].astype(jnp.float32) + other_s[...].astype(jnp.float32)
+    inputs = input_ref[...].astype(jnp.float32)
+    inverse = lax.rsqrt(jnp.mean(inputs * inputs, -1, keepdims=True) + EPSILON)
+    gains_s[0:1, :] = jnp.sum(first_grad * inputs * inverse, 0, keepdims=True)
+    scaled = first_grad * gain_one
+    mean_term = jnp.mean(scaled * inputs, -1, keepdims=True)
+    input_grad[...] += inverse * scaled - inputs * (inverse * inverse * inverse) * mean_term
+    middle = middle_ref[...]
+    inverse = lax.rsqrt(jnp.mean(middle * middle, -1, keepdims=True) + EPSILON)
+    normed2 = (middle * inverse * gain_two).astype(low)
+    router_sums = lax.dot_general(
+        normed2, logit_s[...], (((0,), (0,)), ((), ())), preferred_element_type=jnp.float32
+    )
+    line = lax.broadcasted_iota(jnp.int32, (128, model), 0)
+    turned = jnp.where(line == EXPERTS, gains_s[0:1, :], jnp.where(line == EXPERTS + 1, gains_s[1:2, :], 0.0)).T
+    small_s[...] = (router_sums + turned).astype(low)
+    small.first()
+
+    for d in wo.order:
+        wo.to_z(d, wo_out)
+    for d in qkv.order:
+        qkv.second(d)
+    for d in small.order:
+        small.second(d)
+    for d in qkv.order:
+        qkv.to_z(d, qkv_out)
+    for d in small.order:
+        small.to_z(d, small_out)
+    mixture.finish(layer_out)
+    experts.swapped_z(expert_out)
+    wo.from_z(wo_out)
+    small.from_z(small_out)
+    qkv.from_z(qkv_out)
     for copy in sent:
         copy.wait_send()
 
 
-def sum_keys(part, down, collective_id):
+def rear(
+    returned, gates, middle, inputs, outer, normed1, query, pair, mixed, log_total, cosine, sine, segments, extra,
+    mixture, sums, attn, collective_id,
+):
     ep = lax.axis_size("fsdp")
-    tokens, width = part.shape[0] // 4, part.shape[1]
+    tokens, model = inputs.shape
+    rows = sums.shape[0] // (4 * ep)
+    heads, key_heads = query.shape[1] // HD, pair.shape[1] // (2 * HD)
+    width, kv_width = heads * HD, key_heads * HD
+    qkv_width = width + 2 * kv_width
+    length = pair.shape[0]
+    low = jnp.bfloat16
     dma = pltpu.SemaphoreType.DMA
+    anywhere = pl.BlockSpec(memory_space=pl.ANY)
     vmem = pl.BlockSpec(memory_space=pltpu.VMEM)
+    shape = jax.ShapeDtypeStruct
+    room = pltpu.VMEM
     return pl.pallas_call(
-        keys_kernel,
+        rear_kernel,
         out_shape=(
-            jax.ShapeDtypeStruct((tokens, width), jnp.float32),
-            jax.ShapeDtypeStruct(down.shape, down.dtype),
+            shape((tokens, model), jnp.float32),
+            shape((tokens, model), low),
+            shape((rows, qkv_width), jnp.float32),
+            shape((rows, width), jnp.float32),
+            shape((rows, 128), jnp.float32),
+            shape((ep, rows, sums.shape[1]), low),
         ),
-        in_specs=[vmem] * 2,
-        out_specs=(vmem,) * 2,
+        in_specs=[vmem] * 14 + [anywhere] * 3,
+        out_specs=(vmem,) * 5 + (anywhere,),
         scratch_shapes=[
-            pltpu.VMEM((3, tokens, width), part.dtype), dma((3,)), dma((3,)), dma((ep - 1,)), dma((ep - 1,))
-        ],
+            room((model, width), low),
+            room((model, qkv_width), low),
+            room((model, 128), low),
+            room((heads, tokens, HD), low),
+            room((heads, tokens, HD), low),
+            room((heads, tokens, HD), low),
+            room((key_heads, length, HD), low),
+            room((key_heads, length, HD), low),
+            room((length, tokens), jnp.float32),
+            room((heads, tokens, HD), jnp.float32),
+            room((key_heads, length, HD), low),
+            room((key_heads, length, HD), low),
+            room((length, 2 * kv_width), low),
+            room((3, tokens, 2 * kv_width), low),
+            room((tokens, qkv_width), low),
+            room((tokens, model), low),
+            room((tokens, model), low),
+            room((tokens, model), low),
+            room((tokens, 128), low),
+            room((8, model), jnp.float32),
+            room((ep, tokens // 2, model), low),
+            room((ep, rows, sums.shape[1]), low),
+            room((ep, rows, sums.shape[1]), low),
+            dma((4,)),
+            dma((3,)),
+            dma((3,)),
+            dma,
+            dma,
+        ]
+        + z_sum_scratch(ep, tokens, model, low)
+        + shard_sum_scratch(ep, rows, sums.shape[1], low, False)
+        + shard_sum_scratch(ep, rows, width, low)
+        + shard_sum_scratch(ep, rows, qkv_width, low)
+        + shard_sum_scratch(ep, rows, 128, low),
         compiler_params=pltpu.CompilerParams(
-            collective_id=collective_id, has_side_effects=True, vmem_limit_bytes=32 * 1024 * 1024
+            collective_id=collective_id, has_side_effects=True, vmem_limit_bytes=63 * 1024 * 1024
         ),
-        cost_estimate=lasting(20),
-        name="sum_keys",
-    )(part, down)
-
-
-def pair_kernel(part_ref, sum_ref, other, send, recv):
-    f, c, t = lax.axis_index("fsdp"), lax.axis_index("ctx"), lax.axis_index("tp")
-    core = at_device(f, c, 1 - t)
-    greet([core])
-    copy = remote(part_ref, other, send, recv, core)
-    copy.start()
-    copy.wait()
-    sum_ref[...] = part_ref[...].astype(jnp.float32) + other[...].astype(jnp.float32)
-
-
-def add_pair(part, collective_id):
-    dma = pltpu.SemaphoreType.DMA
-    vmem = pl.BlockSpec(memory_space=pltpu.VMEM)
-    return pl.pallas_call(
-        pair_kernel,
-        out_shape=jax.ShapeDtypeStruct(part.shape, jnp.float32),
-        in_specs=[vmem],
-        out_specs=vmem,
-        scratch_shapes=[pltpu.VMEM(part.shape, part.dtype), dma, dma],
-        compiler_params=pltpu.CompilerParams(
-            collective_id=collective_id, has_side_effects=True, vmem_limit_bytes=32 * 1024 * 1024
-        ),
-        cost_estimate=lasting(5),
-        name="add_pair",
-    )(part)
-
-
-def last_kernel(part_ref, mixture_ref, sum_ref, mixed_ref, *scratch):
-    ep = lax.axis_size("fsdp")
-    rows = sum_ref.shape[0]
-    sent = []
-    tokens = ZSum(mixture_ref, mixed_ref, scratch[: ZSum.size], sent)
-    plane = PlaneSum(part_ref, rows, scratch[ZSum.size : ZSum.size + PlaneSum.size], sent)
-    z_out, z_in, z_send, z_recv = scratch[ZSum.size + PlaneSum.size :]
-    partners = all_partners(ep)
-    greet(partners)
-    plane.first()
-    tokens.to_core()
-    tokens.to_z()
-    plane.second()
-    for d in plane.order:
-        for way in range(2):
-            total = plane.total(d, way)
-            if d == 0:
-                sum_ref[:, plane.columns[way]] = total
-            else:
-                z_out[d - 1, :, plane.columns[way]] = total.astype(z_out.dtype)
-        if d > 0:
-            copy = remote(z_out.at[d - 1], z_in.at[d - 1], z_send.at[d - 1], z_recv.at[d - 1], partners[d - 1])
-            copy.start()
-            sent.append(copy)
-    tokens.from_z()
-    for d in range(1, ep):
-        landing = z_in.at[d - 1]
-        remote(landing, landing, z_send.at[d - 1], z_recv.at[d - 1], partners[d - 1]).wait_recv()
-        sum_ref[...] += z_in[d - 1].astype(jnp.float32)
-    tokens.finish()
-    for copy in sent:
-        copy.wait_send()
-
-
-def sum_last(part, mixture, collective_id):
-    ep = lax.axis_size("fsdp")
-    rows = part.shape[0] // (4 * ep)
-    width, low = part.shape[1], part.dtype
-    tokens = mixture.shape[0] // ep
-    dma = pltpu.SemaphoreType.DMA
-    vmem = pl.BlockSpec(memory_space=pltpu.VMEM)
-    return pl.pallas_call(
-        last_kernel,
-        out_shape=(
-            jax.ShapeDtypeStruct((rows, width), jnp.float32),
-            jax.ShapeDtypeStruct((tokens, mixture.shape[1]), jnp.float32),
-        ),
-        in_specs=[vmem] * 2,
-        out_specs=(vmem,) * 2,
-        scratch_shapes=z_sum_scratch(ep, tokens, mixture.shape[1], low)
-        + plane_sum_scratch(ep, rows, width, low)
-        + [
-            pltpu.VMEM((ep - 1, rows, width), low),
-            pltpu.VMEM((ep - 1, rows, width), low),
-            dma((ep - 1,)),
-            dma((ep - 1,)),
-        ],
-        compiler_params=pltpu.CompilerParams(
-            collective_id=collective_id, has_side_effects=True, vmem_limit_bytes=48 * 1024 * 1024
-        ),
-        cost_estimate=lasting(75),
-        name="sum_last",
-    )(part, mixture)
-
-
-def shards(
+        cost_estimate=lasting(170),
+        name="rear",
+    )(
+        returned, gates, middle, inputs, outer, normed1, query, pair, mixed, log_total, cosine, sine, segments,
+        extra, mixture, sums, attn,
+    )
+
+
+def plain_shards(
     layer_input,
     segments,
     routes,
@@ -846,60 +1146,47 @@
             attn_full[:, qkv_width + 128 :],
         )
 
-    if lax.axis_size("ctx") == 4:
-        (
-            expert_full, outer_all, routes_all, normed2_all,
-            attn_full, normed1, query, pair_all, mixed_low, log_total, middle, cosine, sine,
-        ) = front(
-            attn_shard, gate_weight, up_weight, down_shard, cotangent, routes, layer_input, segments,
-            jnp.tile(freq, 4)[None, :], width // HD, key_groups,
-        )
-        qkv_full, router_full, gain_one, gain_two, output_turned = unpack(attn_full)
-        log_total = log_total[:, :, 0].T.reshape(tokens, key_groups, groups)
-        cosine, sine = cosine[:, : HD // 2], sine[:, HD // 2 : HD]
-        first_inverse = lax.rsqrt(jnp.mean(inputs * inputs, -1, keepdims=True) + EPSILON)
-        second_inverse = lax.rsqrt(jnp.mean(middle * middle, -1, keepdims=True) + EPSILON)
-        normed2 = lax.dynamic_slice_in_dim(normed2_all, lax.axis_index("fsdp") * tokens, tokens)
-    else:
-        attn_full = lax.all_gather(attn_shard, both, axis=0, tiled=True)
-        qkv_full, router_full, gain_one, gain_two, output_turned = unpack(attn_full)
-        packed = jnp.concatenate([gate_weight, up_weight, down_shard], -1)
-        expert_full = spread_experts(packed)
-        expert_full = expert_full.reshape(D, local, 3, hidden_width).transpose(0, 2, 1, 3)
-        expert_full = expert_full.reshape(D, 3 * span)
-        outer_all = lax.all_gather(cotangent, "fsdp", axis=0, tiled=True)
-        routes_all = lax.all_gather(routes, "fsdp", axis=0, tiled=True)
-        place = lax.dynamic_slice_in_dim(document_place(segment_row), begin, tokens)
-        angle = place.astype(jnp.float32)[:, None] * freq[None, :]
-        cosine, sine = jnp.cos(angle), jnp.sin(angle)
-        first_norm, first_inverse = normalize(inputs, gain_one)
-        normed1 = first_norm.astype(low)
-        projected = jnp.dot(normed1, qkv_full, preferred_element_type=jnp.float32)
-        query = rotate(projected[:, :width], cosine, sine).astype(low)
-        key = rotate(projected[:, width : width + kv_width], cosine, sine).astype(low)
-        value = projected[:, width + kv_width :].astype(low)
-        pair_all = lax.all_gather(jnp.concatenate([key, value], 1), "ctx", axis=0, tiled=True)
-        heads = query.reshape(tokens, key_groups, groups, HD)
-        key_heads = pair_all[:, :kv_width].reshape(seq_len, key_groups, HD)
-        value_heads = pair_all[:, kv_width:].reshape(seq_len, key_groups, HD)
-        scores = jnp.einsum("qkgd,nkd->qkgn", heads, key_heads, preferred_element_type=jnp.float32) * scale
-        seen = (segment_row[None, :] == query_doc[:, None]) & (
-            jnp.arange(seq_len, dtype=jnp.int32)[None, :] <= query_order[:, None]
-        )
-        scores = jnp.where(seen[:, None, None, :], scores, MASKED_SCORE)
-        running = jnp.max(scores, -1)
-        weights = jnp.exp(scores - running[..., None])
-        summed = jnp.einsum(
-            "qkgn,nkd->qkgd", weights.astype(low), value_heads, preferred_element_type=jnp.float32
-        )
-        totals = jnp.sum(weights, -1)
-        log_total = running + jnp.log(totals)
-        mixed_low = (summed / totals[..., None]).reshape(tokens, -1).astype(low)
-        attention = add_pair(times_transpose(mixed_low, output_turned).astype(low), 3)
-        middle = inputs + attention
-        second_norm, second_inverse = normalize(middle, gain_two)
-        normed2 = second_norm.astype(low)
-        normed2_all = lax.all_gather(normed2, "fsdp", axis=0, tiled=True)
+    attn_full = lax.all_gather(attn_shard, both, axis=0, tiled=True)
+    qkv_full, router_full, gain_one, gain_two, output_turned = unpack(attn_full)
+    packed = jnp.concatenate([gate_weight, up_weight, down_shard], -1)
+    expert_full = spread_experts(packed)
+    expert_full = expert_full.reshape(D, local, 3, hidden_width).transpose(0, 2, 1, 3)
+    expert_full = expert_full.reshape(D, 3 * span)
+    outer_all = lax.all_gather(cotangent, "fsdp", axis=0, tiled=True)
+    routes_all = lax.all_gather(routes, "fsdp", axis=0, tiled=True)
+    place = lax.dynamic_slice_in_dim(document_place(segment_row), begin, tokens)
+    angle = place.astype(jnp.float32)[:, None] * freq[None, :]
+    cosine, sine = jnp.cos(angle), jnp.sin(angle)
+    first_norm, first_inverse = normalize(inputs, gain_one)
+    normed1 = first_norm.astype(low)
+    projected = jnp.dot(normed1, qkv_full, preferred_element_type=jnp.float32)
+    query = rotate(projected[:, :width], cosine, sine).astype(low)
+    key = rotate(projected[:, width : width + kv_width], cosine, sine).astype(low)
+    value = projected[:, width + kv_width :].astype(low)
+    pair_all = lax.all_gather(jnp.concatenate([key, value], 1), "ctx", axis=0, tiled=True)
+    heads = query.reshape(tokens, key_groups, groups, HD)
+    key_heads = pair_all[:, :kv_width].reshape(seq_len, key_groups, HD)
+    value_heads = pair_all[:, kv_width:].reshape(seq_len, key_groups, HD)
+    scores = jnp.einsum("qkgd,nkd->qkgn", heads, key_heads, preferred_element_type=jnp.float32) * scale
+    seen = (segment_row[None, :] == query_doc[:, None]) & (
+        jnp.arange(seq_len, dtype=jnp.int32)[None, :] <= query_order[:, None]
+    )
+    scores = jnp.where(seen[:, None, None, :], scores, MASKED_SCORE)
+    running = jnp.max(scores, -1)
+    weights = jnp.exp(scores - running[..., None])
+    summed = jnp.einsum(
+        "qkgn,nkd->qkgd", weights.astype(low), value_heads, preferred_element_type=jnp.float32
+    )
+    totals = jnp.sum(weights, -1)
+    log_total = running + jnp.log(totals)
+    mixed_low = (summed / totals[..., None]).reshape(tokens, -1).astype(low)
+    attention = lax.psum(
+        times_transpose(mixed_low, output_turned).astype(low), "tp"
+    ).astype(jnp.float32)
+    middle = inputs + attention
+    second_norm, second_inverse = normalize(middle, gain_two)
+    normed2 = second_norm.astype(low)
+    normed2_all = lax.all_gather(normed2, "fsdp", axis=0, tiled=True)
     gate_up = expert_full[:, : 2 * span]
     down_turned = expert_full[:, 2 * span :]
     key_all = pair_all[:, :kv_width]
@@ -924,6 +1211,7 @@
         last_doc = lax.dynamic_index_in_dim(segment_row, offset + count - 1, keepdims=False)
         return (offset > query_order[tokens - 1]) | (last_doc < query_doc[0])
 
+    place_z = lax.axis_index("fsdp")
     logits_all = jnp.dot(normed2_all, router_full, preferred_element_type=jnp.float32)
     expert_ids = jnp.arange(EXPERTS, dtype=jnp.int32)
     chosen_all = jnp.any(routes_all[:, :, None] == expert_ids[None, None, :], 1)
@@ -931,7 +1219,6 @@
     top = jnp.max(masked_logits, -1, keepdims=True)
     lifted = jnp.where(chosen_all, jnp.exp(masked_logits - top), 0.0)
     gates_all = lifted / jnp.sum(lifted, -1, keepdims=True)
-    place_z = lax.axis_index("fsdp")
     gates_here = lax.dynamic_slice_in_dim(gates_all, place_z * local, local, 1)
     chosen_here = lax.dynamic_slice_in_dim(chosen_all, place_z * local, local, 1)
     chosen = lax.dynamic_slice_in_dim(chosen_all, place_z * tokens, tokens, 0)
@@ -955,7 +1242,7 @@
     former_grad = (scaled_grad * latter * logistic * (1.0 + former * (1.0 - logistic))).astype(low)
     latter_grad = (scaled_grad * active).astype(low)
     side_grads = jnp.concatenate([former_grad, latter_grad], 1)
-    mixture_part = times_transpose(gated, down_turned)
+    mixture_low = times_transpose(gated, down_turned).astype(low)
     input_part = times_transpose(side_grads, gate_up)
     side_sums = contract_rows(normed2_all, side_grads)
     down_sums = contract_rows(outer_all, gated)
@@ -968,14 +1255,14 @@
     dgates_sent = jnp.concatenate([dgates_high, dgates_rest], 1)
     dgates_sent = jnp.pad(dgates_sent, ((0, 0), (0, 128 - 2 * EXPERTS)))
     back_part = jnp.concatenate([input_part.astype(low), dgates_sent], 1)
-    if lax.axis_size("ctx") == 4:
-        returned, down_mine = sum_back(back_part, down_sums.astype(low), 4)
-    else:
-        returned = lax.psum_scatter(
-            lax.psum(back_part, "tp"), "fsdp", scatter_dimension=0, tiled=True
-        ).astype(jnp.float32)
-    side_out = collect_experts(side_sums.astype(low), rows).reshape(ep, rows, 2, local, hidden_width)
-    side_out = side_out.transpose(2, 0, 3, 1, 4).reshape(2, EXPERTS, rows, hidden_width).astype(jnp.float32)
+    returned = lax.psum_scatter(
+        lax.psum(back_part, "tp"), "fsdp", scatter_dimension=0, tiled=True
+    ).astype(jnp.float32)
+    expert_sums = jnp.concatenate([side_sums, down_sums], 1).astype(low)
+    expert_out = collect_experts(expert_sums, rows).reshape(ep, rows, 3, local, hidden_width)
+    side_out = expert_out[:, :, :2].transpose(2, 0, 3, 1, 4).reshape(2, EXPERTS, rows, hidden_width)
+    side_out = side_out.astype(jnp.float32)
+    down_out = expert_out[:, :, 2].transpose(0, 2, 3, 1).reshape(EXPERTS, hidden_width, rows).astype(jnp.float32)
 
     outer_grad = cotangent.astype(jnp.float32)
     input_grad_part = returned[:, :D]
@@ -1031,34 +1318,24 @@
         jnp.zeros((seq_len, 2 * kv_width), jnp.float32),
     )
     query_sum, pair_sum = lax.fori_loop(0, seq_len // tokens, back_two, back_state)
-    if lax.axis_size("ctx") == 4:
-        pair_local, down_out = sum_keys(pair_sum.astype(low), down_mine, 7)
-    else:
-        pair_local = lax.psum_scatter(
-            pair_sum.astype(low), "ctx", scatter_dimension=0, tiled=True
-        ).astype(jnp.float32)
-        down_out = collect_experts(down_sums.astype(low), rows)
-    down_out = down_out.reshape(ep, rows, local, hidden_width)
-    down_out = down_out.transpose(0, 2, 3, 1).reshape(EXPERTS, hidden_width, rows).astype(jnp.float32)
+    pair_local = lax.psum_scatter(
+        pair_sum.astype(low), "ctx", scatter_dimension=0, tiled=True
+    ).astype(jnp.float32)
     query_back = rotate(query_sum.reshape(tokens, -1), cosine, -sine)
     key_back = rotate(pair_local[:, :kv_width], cosine, -sine)
     qkv_back = jnp.concatenate([query_back, key_back, pair_local[:, kv_width:]], 1).astype(low)
     qkv_sums = contract_rows(normed1, qkv_back)
     first_part = times_transpose(qkv_back, qkv_full)
-    first_grad = add_pair(first_part.astype(low), 5)
+    first_grad = lax.psum(first_part.astype(low), "tp").astype(jnp.float32)
     input_back, gain_one_sums = norm_back(first_grad, inputs, first_inverse, gain_one)
     input_grad = middle_grad + input_back
     small_sums = jnp.concatenate([router_sums, gain_one_sums[:, None], gain_two_sums[:, None]], 1)
     small_sums = jnp.pad(small_sums, ((0, 0), (0, 128 - small_sums.shape[1])))
     attn_sums = jnp.concatenate([qkv_sums.astype(low), small_sums.astype(low), output_sums.astype(low)], 1)
-    mixture_low = mixture_part.astype(low)
-    if lax.axis_size("ctx") == 4:
-        attn_out, mixture = sum_last(attn_sums, mixture_low, 6)
-    else:
-        attn_out = lax.psum_scatter(attn_sums, both, scatter_dimension=0, tiled=True).astype(jnp.float32)
-        mixture = lax.psum_scatter(
-            lax.psum(mixture_low, "tp"), "fsdp", scatter_dimension=0, tiled=True
-        ).astype(jnp.float32)
+    attn_out = lax.psum_scatter(attn_sums, both, scatter_dimension=0, tiled=True).astype(jnp.float32)
+    mixture = lax.psum_scatter(
+        lax.psum(mixture_low, "tp"), "fsdp", scatter_dimension=0, tiled=True
+    ).astype(jnp.float32)
     layer_output = (middle + mixture).astype(low)
     small_out = attn_out[:, qkv_width : qkv_width + 128]
     return (
@@ -1069,6 +1346,66 @@
         attn_out[:, width : width + kv_width],
         attn_out[:, width + kv_width : qkv_width],
         attn_out[:, qkv_width + 128 :].T,
+        small_out[:, EXPERTS + 1],
+        small_out[:, :EXPERTS],
+        side_out[0],
+        side_out[1],
+        down_out,
+    )
+
+
+def shards(
+    layer_input,
+    segments,
+    routes,
+    norm_gain,
+    query_weight,
+    key_weight,
+    value_weight,
+    output_weight,
+    ffn_gain,
+    router_weight,
+    gate_weight,
+    up_weight,
+    down_weight,
+    cotangent,
+):
+    low = jnp.bfloat16
+    ep = lax.axis_size("fsdp")
+    rows, width = query_weight.shape
+    kv_width = key_weight.shape[1]
+    hidden_width = gate_weight.shape[2]
+    local = EXPERTS // ep
+    extra = jnp.concatenate([router_weight, norm_gain[:, None], ffn_gain[:, None]], 1)
+    extra = jnp.pad(extra, ((0, 0), (0, 128 - extra.shape[1])))
+    attn_shard = jnp.concatenate([query_weight, key_weight, value_weight, extra, output_weight.T], 1)
+    freq = 10000.0 ** (-2.0 * jnp.arange(HD // 2, dtype=jnp.float32) / HD)
+    (
+        expert_full, outer_all, routes_all, normed2_all,
+        attn_full, normed1, query, pair_all, mixed, log_total, middle, cosine, sine, extra_all,
+    ) = front(
+        attn_shard, gate_weight, up_weight, down_weight.transpose(0, 2, 1), cotangent, routes, layer_input,
+        segments, jnp.tile(freq, 4)[None, :], width // HD, kv_width // HD,
+    )
+    returned, mixture, expert_sums, gates = run_experts(
+        normed2_all, outer_all, routes_all, extra_all, expert_full, 2
+    )
+    input_grad, layer_output, qkv_out, wo_out, small_out, expert_out = rear(
+        returned, gates, middle, layer_input, cotangent, normed1, query, pair_all, mixed, log_total, cosine, sine,
+        segments, extra_all, mixture, expert_sums, attn_full, 3,
+    )
+    expert_out = expert_out.reshape(ep, rows, 3, local, hidden_width)
+    side_out = expert_out[:, :, :2].transpose(2, 0, 3, 1, 4).reshape(2, EXPERTS, rows, hidden_width)
+    side_out = side_out.astype(jnp.float32)
+    down_out = expert_out[:, :, 2].transpose(0, 2, 3, 1).reshape(EXPERTS, hidden_width, rows).astype(jnp.float32)
+    return (
+        layer_output,
+        input_grad,
+        small_out[:, EXPERTS],
+        qkv_out[:, :width],
+        qkv_out[:, width : width + kv_width],
+        qkv_out[:, width + kv_width :],
+        wo_out.T,
         small_out[:, EXPERTS + 1],
         small_out[:, :EXPERTS],
         side_out[0],
@@ -1108,4 +1445,5 @@
         P(None, ("fsdp", "ctx"), "tp"),
         P(None, "tp", ("fsdp", "ctx")),
     )
-    return jax.shard_map(shards, mesh=mesh, in_specs=in_specs, out_specs=out_specs, check_vma=False)
+    body = shards if mesh.shape["ctx"] == 4 else plain_shards
+    return jax.shard_map(body, mesh=mesh, in_specs=in_specs, out_specs=out_specs, check_vma=False)

time: 569 us -> 463 us (0.81)
  matrix products: 82.2 us -> 0 us
  Pallas kernels: 368 us -> 429 us
  local copies, waits for them, and re-layouts: 59.6 us -> 24.9 us
  other arithmetic: 20.7 us -> 1.39 us
  between operations: 15.1 us -> 1 us
  loops' own time: 8.1 us -> 0 us
    dot_general x18 -> x0, matrix products: 82.2 us -> none  [the longest x4 23.7 us: times_transpose(): lax.dot_general(left, right, (((1,), (1,)), ((), ())), preferred_element_...]
    pallas_call x4 -> x2, Pallas kernels: 189 us -> 250 us  [the longest x1 182 us: rear(): pl.pallas_call(rear_kernel, out_shape=(shape((tokens, model), jnp.float32...]
    convert_element_type x5 -> x1, local copies, waits for them, and re-layouts: 11.6 us -> 1.42 us  [shards(): expert_out[:, :, 2].transpose(0, 2, 3, 1)]
    another operation x5 -> x0, loops' own time: 8.1 us -> none  [the longest x1 7.96 us: shards(): lax.fori_loop(0, seq_len // tokens, back_two, back_state)]
    dynamic_slice x7 -> x0, local copies, waits for them, and re-layouts: 7.54 us -> none  [the longest x4 5.09 us: masked_away(): lax.dynamic_index_in_dim(segment_row, offset + count - 1, keepdims=False)]
    reduce_sum x7 -> x0, other arithmetic: 7.16 us -> none  [the longest x1 4.09 us: shards(): jnp.sum(hidden[:, part] * hidden_grad[:, part], -1)]
    concatenate x6 -> x0, other arithmetic: 6.03 us -> none  [the longest x1 3.06 us: shards(): jnp.concatenate([qkv_sums.astype(low), small_sums.astype(low), output_sum...]
    unnamed x88 -> x17, local copies, waits for them, and re-layouts: 12.2 us -> 8.99 us
  transfers between devices with their start and end apart: 2 -> 0, of which waited for: 0 -> 0; matrix products, arithmetic and copies ran while one was open for 17% -> 0% of each run, Pallas kernels for 34% -> 0%
where the time goes in v3:
time: 463 us; the launch traced here: 457 us
  Pallas kernels  429 us (93%)
  local copies, waits for them, and re-layouts  24.9 us (5%)
    pallas_call x1, Pallas kernels, rear(): pl.pallas_call(rear_kernel, out_shape=(shape((tokens, model), jnp.float32...  182 us
    pallas_call x1, Pallas kernels, front(): pl.pallas_call(front_kernel, out_shape=(shape((total, 3 * local * gate.sh...  179 us
    pallas_call x1, Pallas kernels, run_experts(): pl.pallas_call(experts_kernel, out_shape=(shape((tokens, model + 128), jn...  68.3 us

profile of v3, /device:TPU:9, one launch (start us, length us, event | category | flops | bytes accessed | tf_op | source)
XLA Modules:
  0.0 456.5 jit_solution(1691493208793278213)
XLA Ops:
  0.7 0.6 broadcast_in_dim_tile.3.freq_ref
  1.3 0.7 pad_maximum_fusion
  2.0 0.1 copy.42
  2.1 1.5 copy.43.routes_ref
  3.6 0.9 constant_dynamic-update-slice_fusion.2
  4.5 0.8 constant_dynamic-update-slice_fusion.1
  5.3 0.8 constant_dynamic-update-slice_fusion
  6.1 0.9 bitcast_dynamic-update-slice_fusion.attn_ref
  7.1 0.0 copy-start.2
  7.1 0.7 copy-done.2
  7.8 179.1 %front.1 = (bf16[1536,3072]{1,0:T(8,128)(2,1)}, bf16[1024,1536]{1,0:T(8,128)(2,1)}, s32[1024,8]{1,0:T(8,128)}, bf16[1024,1536]{1,0:T(8,128)(2,1)}, bf16[1536,217...) custom-call(bf16[96,2176]{1,0:T(8,128)(2,1)} %copy-done.2, ...), custom_call_target="tpu_custom_call" | custom-call | bytes 664200000 | tf_op jit(solution)/shard_map/front/pallas_call | solution.py:383
  186.9 68.3 %experts.1 = (f32[256,1664]{1,0:T(8,128)}, bf16[1024,1536]{1,0:T(8,128)(2,1)}, bf16[1536,3072]{1,0:T(8,128)(2,1)}, f32[256,128]{1,0:T(8,128)}) custom-call(bf16[1024,1536]{1,0:T(8,128)(2,1)} %get-tuple-element.36.tokens_ref, bf16[1024,1536]{1,0:T(8,128)(2,1)} %get-tuple-element.37.outer_ref, s32[1024,8]{1,0:T(8,128)} %get-tuple-element.38.routes_ref, ...), custom_call_target="tpu_custom_call" | custom-call | bytes 258300000 | tf_op jit(solution)/shard_map/experts/pallas_call | solution.py:776
  255.2 181.9 %rear.1 = (f32[256,1536]{1,0:T(8,128)}, bf16[256,1536]{1,0:T(8,128)(2,1)}, f32[96,1280]{1,0:T(8,128)}, f32[96,768]{1,0:T(8,128)}, f32[96,128]{1,0:T(8,128)}, /*index=5*/bf16[4,96,3072]{2,1,0:T(8,128)(2,1)}) custom-call(f32[256,1664]{1,0:T(8,128)} %get-tuple-element.41.returned_ref, f32[256,128]{1,0:T(8,128)} %get-tuple-element.42.gates_ref, ...), custom_call_target="tpu_custom_call" | custom-call | bytes 627299968 | tf_op jit(solution)/shard_map/rear/pallas_call | solution.py:1039
  437.1 1.6 slice_reduce_fusion
  438.7 1.5 copy.47
  440.2 1.6 fusion.1
  441.8 1.7 slice.33
  443.5 4.5 reshape.43
  448.0 0.2 convert_bitcast_fusion.1
  448.2 1.4 copy.46
  449.6 0.4 convert_bitcast_fusion
  450.1 0.6 fusion
  450.7 1.4 copy.45
  452.1 0.0 copy-start.1
  452.1 0.0 copy-start
  452.1 1.4 copy.44
  453.5 0.0 copy-done.1
  453.5 0.9 copy.55
  454.4 0.0 copy-done
  454.4 0.0 copy-start.3
  454.4 1.1 copy.56
  455.5 0.0 copy-done.3
  455.5 0.7 copy.57
  (3 shorter events, 0.0 us)
Async XLA Ops:
  7.1 0.8 copy-start.2
  452.1 1.4 copy-start.1
  452.1 2.3 copy-start
  454.4 1.1 copy-start.3

commit v4 on v3

--- a/solution.py
+++ b/solution.py
@@ -10,6 +10,7 @@
 D = 1536
 HD = 64
 EXPERTS = 16
+EARLY = 768
 
 
 EPSILON = 1e-05
@@ -104,7 +105,7 @@
     attn_out, normed1_out, query_out, pair_out, mixed_out, log_out, middle_out, cos_out, sin_out, extra_out,
     query_s, key_s, value_s, mixed_s, bias_s, part_s, other_s, normed2_s,
     local_sem, z_send, z_recv, plane_send, plane_recv, relay_send, relay_recv, core_send, core_recv,
-    key_send, key_recv, pair_send, pair_recv,
+    key_send, key_recv, pair_send, pair_recv, chain_send, chain_recv,
 ):
     ep = z_send.shape[1] + 1
     f, c, t = lax.axis_index("fsdp"), lax.axis_index("ctx"), lax.axis_index("tp")
@@ -140,9 +141,18 @@
     mine = shard_rows(f, c)
     sent = []
 
-    def send(copy):
-        copy.start()
-        sent.append(copy)
+    def send(copy, when=None):
+        if when is None:
+            copy.start()
+        else:
+            pl.when(when)(copy.start)
+        sent.append((when, copy))
+
+    def await_arrival(copy, when=None):
+        if when is None:
+            copy.wait_recv()
+        else:
+            pl.when(when)(copy.wait_recv)
 
     def z_arrival(kind, d):
         place = shard_rows(peer(ep - d), c)
@@ -150,40 +160,72 @@
             outs[kind].at[place], outs[kind].at[place], z_send.at[kind, d - 1], z_recv.at[kind, d - 1], x_device
         ).wait_recv()
 
-    def spread(kind, d):
-        place = shard_rows(peer(ep - d), c)
+    def spread(kind, g, when=None):
+        place = shard_rows(g, c)
         for step in range(2):
             for way, device in enumerate((x_device, y_device)):
                 side = step ^ way
                 block = outs[kind].at[place, columns(kind, side)]
                 send(
                     remote(
-                        block, block, plane_send.at[kind, d, way, side], plane_recv.at[kind, d, way, side], device
-                    )
+                        block, block, plane_send.at[kind, g, way, side], plane_recv.at[kind, g, way, side], device
+                    ),
+                    when,
                 )
 
-    def pass_on(kind, d):
+    def pass_on(kind, g, when=None):
         for way, device in enumerate((y_device, x_device)):
-            place = shard_rows(peer(ep - d), c ^ (1 << way))
+            place = shard_rows(g, c ^ (1 << way))
             block = outs[kind].at[place, columns(kind, way)]
-            remote(
-                block, block, plane_send.at[kind, d, way, way], plane_recv.at[kind, d, way, way], device
-            ).wait_recv()
-            send(remote(block, block, relay_send.at[kind, d, way], relay_recv.at[kind, d, way], device))
+            await_arrival(
+                remote(
+                    block, block, plane_send.at[kind, g, way, way], plane_recv.at[kind, g, way, way], device
+                ),
+                when,
+            )
+            send(remote(block, block, relay_send.at[kind, g, way], relay_recv.at[kind, g, way], device), when)
 
     def settle(kind):
-        for d in range(ep):
-            back = peer(ep - d)
+        for g in range(ep):
             for way, device in enumerate((x_device, y_device)):
                 side = 1 - way
-                block = outs[kind].at[shard_rows(back, c ^ (1 << way)), columns(kind, side)]
+                block = outs[kind].at[shard_rows(g, c ^ (1 << way)), columns(kind, side)]
                 remote(
-                    block, block, plane_send.at[kind, d, way, side], plane_recv.at[kind, d, way, side], device
+                    block, block, plane_send.at[kind, g, way, side], plane_recv.at[kind, g, way, side], device
                 ).wait_recv()
-                block = outs[kind].at[shard_rows(back, c ^ 3), columns(kind, way)]
+                block = outs[kind].at[shard_rows(g, c ^ 3), columns(kind, way)]
                 remote(
-                    block, block, relay_send.at[kind, d, way], relay_recv.at[kind, d, way], device
+                    block, block, relay_send.at[kind, g, way], relay_recv.at[kind, g, way], device
                 ).wait_recv()
+
+    nexts = (at_device(jnp.minimum(f + 1, ep - 1), c, t), at_device(jnp.maximum(f - 1, 0), c, t))
+    more = (f < ep - 1, f > 0)
+
+    def chain_origin(way, hop):
+        if way == 0:
+            return jnp.maximum(f - hop, 0), f >= hop
+        return jnp.minimum(f + hop, ep - 1), f + hop < ep
+
+    def chain_begin(kind, source, target):
+        for way in range(2):
+            send(
+                remote(source, target, chain_send.at[kind, way, 0], chain_recv.at[kind, way, 0], nexts[way]),
+                more[way],
+            )
+
+    def chain_hop(kind, way, hop, block):
+        there = chain_origin(way, hop)[1]
+        await_arrival(
+            remote(
+                block, block, chain_send.at[kind, way, hop - 1], chain_recv.at[kind, way, hop - 1], nexts[way]
+            ),
+            there,
+        )
+        if hop < ep - 1:
+            send(
+                remote(block, block, chain_send.at[kind, way, hop], chain_recv.at[kind, way, hop], nexts[way]),
+                there & more[way],
+            )
 
     def line_place(fsdp, part):
         return pl.ds(pl.multiple_of(fsdp * tokens + part * half, 16), half)
@@ -203,15 +245,14 @@
         for d in range(1, ep):
             block = target.at[line_place(peer(ep - d), t)]
             remote(block, block, z_send.at[kind, d - 1], z_recv.at[kind, d - 1], core).wait_recv()
-            send(remote(block, block, core_send.at[kind - 2, d - 1], core_recv.at[kind - 2, d - 1], core))
+            send(remote(block, block, core_send.at[kind - 2, d], core_recv.at[kind - 2, d], core))
 
     def line_settle(kind, target):
         for d in range(1, ep):
             block = target.at[line_place(peer(ep - d), 1 - t)]
-            remote(block, block, core_send.at[kind - 2, d - 1], core_recv.at[kind - 2, d - 1], core).wait_recv()
-
-    for d in range(1, ep):
-        send(remote(attn_ref, attn_out.at[mine], z_send.at[0, d - 1], z_recv.at[0, d - 1], line[d - 1]))
+            remote(block, block, core_send.at[kind - 2, d], core_recv.at[kind - 2, d], core).wait_recv()
+
+    chain_begin(0, attn_ref, attn_out.at[mine])
     own_attn = pltpu.make_async_copy(attn_ref, attn_out.at[mine], local_sem.at[0])
     own_attn.start()
     own_outer = pltpu.make_async_copy(outer_ref, outer_out.at[own_tokens], local_sem.at[2])
@@ -229,7 +270,7 @@
             target = expert_out.at[mine, pl.ds((kind * local + e) * hidden, hidden)]
             pltpu.make_async_copy(ref.at[f * local + e], target, local_sem.at[1]).start()
     own_attn.wait()
-    spread(0, 0)
+    spread(0, f)
 
     length = segment_ref.shape[1]
     seg_keys = segment_ref[...].astype(jnp.float32)
@@ -251,18 +292,27 @@
     inputs = input_ref[...].astype(jnp.float32)
     inverse = lax.rsqrt(jnp.mean(inputs * inputs, -1, keepdims=True) + EPSILON)
 
-    for d in range(1, ep):
-        z_arrival(0, d)
-        spread(0, d)
-        pass_on(0, d - 1)
+    pass_on(0, f)
+    for hop in range(1, ep):
+        for way in range(2):
+            g, there = chain_origin(way, hop)
+            chain_hop(0, way, hop, attn_out.at[shard_rows(g, c)])
+            spread(0, g, there)
+        if hop > 1:
+            for way in range(2):
+                pass_on(0, *chain_origin(way, hop - 1))
+    for way in range(2):
+        pass_on(0, *chain_origin(way, ep - 1))
     for d in range(1, ep):
         for kind, ref in enumerate((gate_ref, up_ref, down_ref)):
             for e in range(local):
                 target = expert_out.at[mine, pl.ds((kind * local + e) * hidden, hidden)]
                 remote(
-                    ref.at[peer(d) * local + e], target, z_send.at[1, d - 1], z_recv.at[1, d - 1], line[d - 1]
+                    ref.at[peer(d) * local + e], target, z_send.at[1, d - 1], z_recv.at[1, d - 1],
+                    line[d - 1],
                 ).start()
-    pass_on(0, ep - 1)
+    pltpu.make_async_copy(expert_out.at[mine], expert_out.at[mine], local_sem.at[1]).wait()
+    spread(1, f)
     settle(0)
 
     gains = attn_out[:, qkv_width : qkv_width + 128].astype(jnp.float32).T
@@ -292,15 +342,17 @@
             query_out[:, start + side : start + side + 128] = turned(tile[:, side : side + 128]).astype(low)
     for h in range(heads):
         query_s[h] = query_out[:, h * HD : (h + 1) * HD]
-    pltpu.make_async_copy(expert_out.at[mine], expert_out.at[mine], local_sem.at[1]).wait()
     for k in range(1, 4):
         block = pair_out.at[pl.ds(pl.multiple_of((c ^ k) * tokens, 16), tokens)]
         remote(block, block, key_send.at[k - 1], key_recv.at[k - 1], plane[k - 1]).wait_recv()
-    spread(1, 0)
     for g in range(key_heads):
         key_s[g] = pair_out[:, g * HD : (g + 1) * HD]
         value_s[g] = pair_out[:, kv_width + g * HD : kv_width + (g + 1) * HD]
-    pass_on(1, 0)
+    pass_on(1, f)
+    for d in range(1, ep):
+        z_arrival(1, d)
+        spread(1, peer(ep - d))
+    line_send(2, outer_ref.at[my_half], outer_out)
 
     def attend(h, carry):
         g = lax.div(h, heads // key_heads)
@@ -319,10 +371,6 @@
     lax.fori_loop(0, heads, attend, 0)
     for h in range(heads):
         mixed_out[:, h * HD : (h + 1) * HD] = mixed_s[h]
-    z_arrival(1, 1)
-    spread(1, 1)
-    line_send(2, outer_ref.at[my_half], outer_out)
-
     model = input_ref.shape[1]
     for start in range(0, model, 256):
         part_s[:, start : start + 256] = lax.dot_general(
@@ -331,10 +379,7 @@
         ).astype(low)
     exchange = remote(part_s, other_s, pair_send, pair_recv, core)
     send(exchange)
-    for d in range(2, ep):
-        z_arrival(1, d)
-        spread(1, d)
-        pass_on(1, d - 1)
+    pass_on(1, peer(ep - 1))
     exchange.wait_recv()
     middle = input_ref[...].astype(jnp.float32) + (
         part_s[...].astype(jnp.float32) + other_s[...].astype(jnp.float32)
@@ -343,15 +388,23 @@
     inverse = lax.rsqrt(jnp.mean(middle * middle, -1, keepdims=True) + EPSILON)
     gains = attn_out[:, qkv_width : qkv_width + 128].astype(jnp.float32).T
     normed2_s[...] = (middle * inverse * gains[EXPERTS + 1 : EXPERTS + 2, :]).astype(low)
-    line_send(3, normed2_s.at[my_half], normed2_out)
+    chain_begin(1, normed2_s.at[my_half], normed2_out.at[line_place(f, t)])
     own_normed2 = pltpu.make_async_copy(normed2_s, normed2_out.at[own_tokens], local_sem.at[4])
     own_normed2.start()
-    pass_on(1, ep - 1)
+    for d in range(2, ep):
+        pass_on(1, peer(ep - d))
+    for hop in range(1, ep):
+        for way in range(2):
+            g, there = chain_origin(way, hop)
+            block = normed2_out.at[line_place(g, t)]
+            chain_hop(1, way, hop, block)
+            send(remote(block, block, core_send.at[1, g], core_recv.at[1, g], core), there)
     line_forward(2, outer_out)
-    line_forward(3, normed2_out)
     settle(1)
     line_settle(2, outer_out)
-    line_settle(3, normed2_out)
+    for g in range(ep):
+        block = normed2_out.at[line_place(g, 1 - t)]
+        await_arrival(remote(block, block, core_send.at[1, g], core_recv.at[1, g], core), f != g)
     for d in range(1, ep):
         place = pl.ds(pl.multiple_of(peer(ep - d) * tokens, 16), tokens)
         remote(
@@ -364,8 +417,7 @@
     own_outer.wait()
     own_routes.wait()
     own_normed2.wait()
-    for copy in sent:
-        copy.wait_send()
+    all_sent(sent)
 
 
 def front(attn, gate, up, down, outer, routes, inputs, segments, freq, heads, key_heads):
@@ -416,12 +468,14 @@
             dma((2, ep, 2, 2)),
             dma((2, ep, 2)),
             dma((2, ep, 2)),
-            dma((2, ep - 1)),
-            dma((2, ep - 1)),
+            dma((2, ep)),
+            dma((2, ep)),
             dma((3,)),
             dma((3,)),
             dma,
             dma,
+            dma((2, 2, ep - 1)),
+            dma((2, 2, ep - 1)),
         ],
         compiler_params=pltpu.CompilerParams(
             collective_id=1, has_side_effects=True, vmem_limit_bytes=56 * 1024 * 1024
@@ -470,12 +524,13 @@
 
     def send(self, copy):
         copy.start()
-        self.sent.append(copy)
+        self.sent.append((None, copy))
 
     def to_core(self, d):
         self.send(
             remote(
-                self.part.at[self.place(self.peer(d), 1 - self.t)], self.core_in.at[d],
+                self.part.at[self.place(self.peer(d), 1 - self.t), pl.ds(0, self.core_in.shape[2])],
+                self.core_in.at[d],
                 self.core_send.at[d], self.core_recv.at[d], self.core,
             )
         )
@@ -483,7 +538,10 @@
     def added(self, d):
         landing = self.core_in.at[d]
         remote(landing, landing, self.core_send.at[d], self.core_recv.at[d], self.core).wait_recv()
-        mine = self.part[self.place(self.peer(d), self.t), :] if self.own is None else self.own[d]
+        if self.own is None:
+            mine = self.part[self.place(self.peer(d), self.t), : self.core_in.shape[2]]
+        else:
+            mine = self.own[d]
         return mine.astype(jnp.float32) + self.core_in[d].astype(jnp.float32)
 
     def to_z(self, d):
@@ -512,15 +570,25 @@
         remote(other, other, self.back_send, self.back_recv, self.core).wait_recv()
 
 
-def shard_sum_scratch(ep, rows, width, low, along_z=True):
+def all_sent(sent):
+    for when, copy in sent:
+        if when is None:
+            copy.wait_send()
+        else:
+            pl.when(when)(copy.wait_send)
+
+
+def shard_sum_scratch(ep, rows, width, low):
     cut = first_columns(width)
     widths = [cut] if cut == width else [cut, width - cut]
     dma = pltpu.SemaphoreType.DMA
     scratch = []
     for part in widths:
-        scratch += [pltpu.VMEM((ep, 2, rows, part), low), pltpu.VMEM((ep, rows, part), low)]
-        if along_z:
-            scratch.append(pltpu.VMEM((ep - 1, rows, part), low))
+        scratch += [
+            pltpu.VMEM((ep, 2, rows, part), low),
+            pltpu.VMEM((ep, rows, part), low),
+            pltpu.VMEM((ep - 1, rows, part), low),
+        ]
     return scratch + [
         dma((2, ep, 2)), dma((2, ep, 2)), dma((2, ep)), dma((2, ep)), dma((2, ep)), dma((2, ep))
     ]
@@ -531,18 +599,17 @@
 
 
 class ShardSum:
-    def __init__(self, part, rows, width, scratch, sent, own=None, relay=None):
-        self.part, self.rows, self.sent, self.own, self.relay = part, rows, sent, own, relay
+    def __init__(self, part, rows, width, scratch, sent):
+        self.part, self.rows, self.sent = part, rows, sent
         cut = first_columns(width)
         self.columns = [pl.ds(0, cut)] + ([] if cut == width else [pl.ds(cut, width - cut)])
         self.ways = range(len(self.columns))
         (
             self.first_send, self.first_recv, self.second_send, self.second_recv, self.z_send, self.z_recv
         ) = scratch[-6:]
-        each = (len(scratch) - 6) // len(self.columns)
-        self.first_in = [scratch[each * way] for way in self.ways]
-        self.second_in = [scratch[each * way + 1] for way in self.ways]
-        self.z_in = [scratch[each * way + 2] for way in self.ways] if each == 3 else None
+        self.first_in = [scratch[3 * way] for way in self.ways]
+        self.second_in = [scratch[3 * way + 1] for way in self.ways]
+        self.z_in = [scratch[3 * way + 2] for way in self.ways]
         self.ep = self.first_in[0].shape[0]
         self.f, self.c, self.t = lax.axis_index("fsdp"), lax.axis_index("ctx"), lax.axis_index("tp")
         self.neighbours = (at_device(self.f, self.c ^ 1, self.t), at_device(self.f, self.c ^ 2, self.t))
@@ -557,32 +624,19 @@
 
     def send(self, copy):
         copy.start()
-        self.sent.append(copy)
-
-    def load(self, sem):
-        for d in range(self.ep):
+        self.sent.append((None, copy))
+
+    def first(self, d):
+        for number in range(2):
             for way in self.ways:
-                for target, ctx in ((self.own, self.c), (self.relay, self.c ^ (2 >> way))):
-                    pltpu.make_async_copy(
-                        self.part.at[self.block(d, ctx, way)], target.at[d, :, self.columns[way]], sem
-                    ).start()
-
-    def loaded(self, sem):
-        for target in (self.own, self.relay):
-            pltpu.make_async_copy(target, target, sem).wait()
-
-    def first(self):
-        for d in self.order:
-            for number in range(2):
-                for way in self.ways:
-                    target = self.c ^ 3 if number == 0 else self.c ^ (1 << way)
-                    self.send(
-                        remote(
-                            self.part.at[self.block(d, target, way)], self.first_in[way].at[d, number],
-                            self.first_send.at[way, d, number], self.first_recv.at[way, d, number],
-                            self.neighbours[way],
-                        )
+                target = self.c ^ 3 if number == 0 else self.c ^ (1 << way)
+                self.send(
+                    remote(
+                        self.part.at[self.block(d, target, way)], self.first_in[way].at[d, number],
+                        self.first_send.at[way, d, number], self.first_recv.at[way, d, number],
+                        self.neighbours[way],
                     )
+                )
 
     def second(self, d):
         for way in self.ways:
@@ -592,10 +646,7 @@
                     landing, landing, self.first_send.at[way, d, number],
                     self.first_recv.at[way, d, number], self.neighbours[way],
                 ).wait_recv()
-            if self.relay is None:
-                term = self.part[self.block(d, self.c ^ (2 >> way), way)]
-            else:
-                term = self.relay[d, :, self.columns[way]]
+            term = self.part[self.block(d, self.c ^ (2 >> way), way)]
             added = term.astype(jnp.float32) + self.first_in[way][d, 0].astype(jnp.float32)
             self.first_in[way][d, 0] = added.astype(self.part.dtype)
             self.send(
@@ -610,7 +661,7 @@
         remote(
             landing, landing, self.second_send.at[way, d], self.second_recv.at[way, d], self.neighbours[1 - way]
         ).wait_recv()
-        term = self.part[self.block(d, self.c, way)] if self.own is None else self.own[d, :, self.columns[way]]
+        term = self.part[self.block(d, self.c, way)]
         return (
             term.astype(jnp.float32)
             + self.first_in[way][d, 1].astype(jnp.float32)
@@ -640,30 +691,6 @@
                 ).wait_recv()
                 out[:, self.columns[way]] += self.z_in[way][d - 1].astype(jnp.float32)
 
-    def swap_z(self, d, out):
-        for way in self.ways:
-            self.first_in[way][d, 1] = self.total(d, way).astype(self.part.dtype)
-            source, target = self.first_in[way].at[d, 1], out.at[self.f, :, self.columns[way]]
-            if d == 0:
-                pltpu.make_async_copy(source, target, self.z_send.at[way, 0]).start()
-            else:
-                self.send(
-                    remote(
-                        source, target, self.z_send.at[way, d], self.z_recv.at[way, d],
-                        at_device(self.peer(d), self.c, self.t),
-                    )
-                )
-
-    def swapped_z(self, out):
-        for way in self.ways:
-            target = out.at[self.f, :, self.columns[way]]
-            pltpu.make_async_copy(self.first_in[way].at[0, 1], target, self.z_send.at[way, 0]).wait()
-            for d in range(1, self.ep):
-                landing = out.at[self.peer(self.ep - d), :, self.columns[way]]
-                remote(
-                    landing, landing, self.z_send.at[way, d], self.z_recv.at[way, d], self.neighbours[0]
-                ).wait_recv()
-
 
 def all_partners(ep):
     f, c, t = lax.axis_index("fsdp"), lax.axis_index("ctx"), lax.axis_index("tp")
@@ -671,10 +698,49 @@
     return line + [at_device(f, c ^ 1, t), at_device(f, c ^ 2, t), at_device(f, c, 1 - t)]
 
 
+class PlaneHalf:
+    def __init__(self, part, rows, landings, send_sem, recv_sem, sent):
+        self.part, self.rows, self.landings, self.sent = part, rows, landings, sent
+        self.send_sem, self.recv_sem = send_sem, recv_sem
+        cut = landings[0].shape[-1]
+        self.columns = (pl.ds(0, cut), pl.ds(cut, part.shape[1] - cut))
+        self.ep = landings[0].shape[0]
+        self.f, self.c, t = lax.axis_index("fsdp"), lax.axis_index("ctx"), lax.axis_index("tp")
+        self.neighbours = (at_device(self.f, self.c ^ 1, t), at_device(self.f, self.c ^ 2, t))
+
+    def block(self, distance, ctx, way):
+        start = (lax.rem(self.f + distance, self.ep) * 4 + ctx) * self.rows
+        return pl.ds(pl.multiple_of(start, 16), self.rows), self.columns[way]
+
+    def start(self, d):
+        for number in range(2):
+            for way in range(2):
+                target = self.c ^ 3 if number == 0 else self.c ^ (1 << way)
+                copy = remote(
+                    self.part.at[self.block(d, target, way)], self.landings[way].at[d, number],
+                    self.send_sem.at[way, d, number], self.recv_sem.at[way, d, number], self.neighbours[way],
+                )
+                copy.start()
+                self.sent.append((None, copy))
+
+    def finish(self, d):
+        for way in range(2):
+            for number in range(2):
+                landing = self.landings[way].at[d, number]
+                remote(
+                    landing, landing, self.send_sem.at[way, d, number], self.recv_sem.at[way, d, number],
+                    self.neighbours[way],
+                ).wait_recv()
+                ctx = self.c ^ (2 >> way) if number == 0 else self.c
+                term = self.part[self.block(d, ctx, way)].astype(jnp.float32)
+                added = term + self.landings[way][d, number].astype(jnp.float32)
+                self.landings[way][d, number] = added.astype(self.part.dtype)
+
+
 def experts_kernel(
     tokens_ref, outer_ref, routes_ref, extra_ref, weight_ref,
-    returned_ref, mixture_out, sums_out, gates_out,
-    gates_s, gated_s, side_s, part_s, *scratch,
+    returned_ref, mixed_ref, mixture_out, relay_out, own_out, gates_out,
+    gates_s, gated_s, side_s, part_s, mixture_s, sums_s, first_x, first_y, plane_send, plane_recv, local_sem, *scratch,
 ):
     ep = lax.axis_size("fsdp")
     f = lax.axis_index("fsdp")
@@ -682,12 +748,14 @@
     reach, model = tokens_ref.shape
     span = weight_ref.shape[1] // 3
     tokens = reach // ep
+    rows = model // (4 * ep)
     local = EXPERTS // ep
     hidden = span // local
     sent = []
-    back = ZSum(part_s, scratch, sent)
-    partners = all_partners(ep)
-    greet(partners[: ep - 1] + partners[-1:])
+    back = ZSum(part_s, scratch[: ZSum.size], sent)
+    mixture = ZSum(mixture_s, scratch[ZSum.size :], sent)
+    plane = PlaneHalf(sums_s, rows, (first_x, first_y), plane_send, plane_recv, sent)
+    greet(all_partners(ep))
 
     lane = lax.broadcasted_iota(jnp.int32, (reach, 128), 1)
     chosen = routes_ref[:, 0:1] == lane
@@ -699,112 +767,144 @@
     gates_s[...] = lifted / jnp.sum(lifted, -1, keepdims=True)
     own = pl.ds(pl.multiple_of(f * tokens, 16), tokens)
     gates_out[...] = gates_s[own, :]
-    small_lane = lax.broadcasted_iota(jnp.int32, (tokens, 128), 1)
-
-    def block(d):
+
+    part_s[:, model:] = jnp.zeros((reach, 128), low)
+    for e in range(local):
+        at = slice(e * hidden, (e + 1) * hidden)
+        at_up = slice(span + e * hidden, span + (e + 1) * hidden)
+        at_down = slice(2 * span + e * hidden, 2 * span + (e + 1) * hidden)
+        mine = lane == f * local + e
+        gate = jnp.sum(jnp.where(mine, gates_s[...], 0.0), -1, keepdims=True)
+        former = jnp.dot(tokens_ref[...], weight_ref[:, at], preferred_element_type=jnp.float32)
+        latter = jnp.dot(tokens_ref[...], weight_ref[:, at_up], preferred_element_type=jnp.float32)
+        grad = jnp.dot(outer_ref[...], weight_ref[:, at_down], preferred_element_type=jnp.float32)
+        logistic = 1.0 / (1.0 + jnp.exp(-former))
+        active = former * logistic
+        value = (active * latter).astype(low).astype(jnp.float32)
+        gated_s[:, at] = (value * gate).astype(low)
+        picked = jnp.sum(value * grad, -1, keepdims=True)
+        dgate = jnp.where(mine & (gate > 0.0), picked, 0.0)
+        high = dgate.astype(low).astype(jnp.float32)
+        part_s[:, model:] += (high + pltpu.roll(dgate - high, EXPERTS, 1)).astype(low)
+        grad = grad * gate
+        side_s[:, at] = (grad * latter * logistic * (1.0 + former * (1.0 - logistic))).astype(low)
+        side_s[:, at_up] = (grad * active).astype(low)
+
+    order = list(range(1, ep)) + [0]
+    over = (((0,), (0,)), ((), ()))
+    across = (((1,), (1,)), ((), ()))
+
+    def mixtures(n, carry):
+        at = pl.ds(pl.multiple_of(n * 256, 256), 256)
+        mixture_s[:, at] = lax.dot_general(
+            gated_s[...], weight_ref[at, 2 * span :], across, preferred_element_type=jnp.float32
+        ).astype(low)
+        return carry
+
+    for step, d in enumerate(order):
+        if step == 1:
+            lax.fori_loop(0, model // 256, mixtures, 0)
+            for g in order:
+                mixture.to_core(g)
+            later = pltpu.make_async_copy(mixture_s.at[:, pl.ds(EARLY, model - EARLY)], mixture_out, local_sem.at[2])
+            later.start()
+        if step > 1:
+            mixture.to_z(order[step - 2])
+        at = pl.ds(pl.multiple_of(back.peer(d) * 4 * rows, 128), 4 * rows)
+        sums_s[at, : 2 * span] = lax.dot_general(
+            tokens_ref[:, at], side_s[...], over, preferred_element_type=jnp.float32
+        ).astype(low)
+        sums_s[at, 2 * span :] = lax.dot_general(
+            outer_ref[:, at], gated_s[...], over, preferred_element_type=jnp.float32
+        ).astype(low)
+        plane.start(d)
+
+    mixture.to_z(order[2])
+    for step, d in enumerate(order):
         here = pl.ds(pl.multiple_of(back.peer(d) * tokens, 16), tokens)
-        gates = gates_s[here, :]
-        dgates = jnp.zeros((tokens, 128), jnp.float32)
-        for e in range(local):
-            at = slice(e * hidden, (e + 1) * hidden)
-            mine = small_lane == f * local + e
-            gate = jnp.sum(jnp.where(mine, gates, 0.0), -1, keepdims=True)
-            former = jnp.dot(tokens_ref[here, :], weight_ref[:, at], preferred_element_type=jnp.float32)
-            at_up = slice(span + e * hidden, span + (e + 1) * hidden)
-            latter = jnp.dot(tokens_ref[here, :], weight_ref[:, at_up], preferred_element_type=jnp.float32)
-            at_down = slice(2 * span + e * hidden, 2 * span + (e + 1) * hidden)
-            grad = jnp.dot(outer_ref[here, :], weight_ref[:, at_down], preferred_element_type=jnp.float32)
-            logistic = 1.0 / (1.0 + jnp.exp(-former))
-            active = former * logistic
-            value = (active * latter).astype(low).astype(jnp.float32)
-            gated_s[here, at] = (value * gate).astype(low)
-            picked = jnp.sum(value * grad, -1, keepdims=True)
-            dgates = jnp.where(mine & (gate > 0.0), picked, dgates)
-            grad = grad * gate
-            side_s[here, at] = (grad * latter * logistic * (1.0 + former * (1.0 - logistic))).astype(low)
-            side_s[here, at_up] = (grad * active).astype(low)
-        high = dgates.astype(low).astype(jnp.float32)
-        part_s[here, model:] = (high + pltpu.roll(dgates - high, EXPERTS, 1)).astype(low)
 
         def tile(n, carry):
             at = pl.ds(pl.multiple_of(n * 256, 256), 256)
             part_s[here, at] = lax.dot_general(
-                side_s[here, :], weight_ref[at, : 2 * span], (((1,), (1,)), ((), ())),
-                preferred_element_type=jnp.float32,
-            ).astype(low)
-            mixture_out[here, at] = lax.dot_general(
-                gated_s[here, :], weight_ref[at, 2 * span :], (((1,), (1,)), ((), ())),
-                preferred_element_type=jnp.float32,
+                side_s[here, :], weight_ref[at, : 2 * span], across, preferred_element_type=jnp.float32
             ).astype(low)
             return carry
 
         lax.fori_loop(0, model // 256, tile, 0)
-
-    order = list(range(1, ep)) + [0]
-    for step, d in enumerate(order):
-        block(d)
         back.to_core(d)
         if step > 0:
             back.to_z(order[step - 1])
 
-    def sums(n, carry):
-        at = pl.ds(pl.multiple_of(n * 256, 256), 256)
-        over = (((0,), (0,)), ((), ()))
-        sums_out[at, : 2 * span] = lax.dot_general(
-            tokens_ref[:, at], side_s[...], over, preferred_element_type=jnp.float32
-        ).astype(low)
-        sums_out[at, 2 * span :] = lax.dot_general(
-            outer_ref[:, at], gated_s[...], over, preferred_element_type=jnp.float32
-        ).astype(low)
-        return carry
-
-    lax.fori_loop(0, model // 256, sums, 0)
+    for d in order:
+        plane.finish(d)
+        for way in range(2):
+            for number, out in enumerate((relay_out, own_out)):
+                pltpu.make_async_copy(
+                    plane.landings[way].at[d, number], out.at[d, :, plane.columns[way]], local_sem.at[number]
+                ).start()
     returned_ref[back.rows(back.t), :] = back.collect()
     back.share(returned_ref)
+    mixed_ref[...] = mixture.collect()
+    later.wait()
     back.finish(returned_ref)
-    for copy in sent:
-        copy.wait_send()
+    for number, out in enumerate((relay_out, own_out)):
+        pltpu.make_async_copy(out, out, local_sem.at[number]).wait()
+    all_sent(sent)
 
 
 def run_experts(tokens_all, outer_all, routes_all, extra, weights, collective_id):
     ep = lax.axis_size("fsdp")
     reach, model = tokens_all.shape
     tokens, low = reach // ep, tokens_all.dtype
-    span = weights.shape[1] // 3
+    rows = model // (4 * ep)
+    full = weights.shape[1]
+    span = full // 3
+    dma = pltpu.SemaphoreType.DMA
+    anywhere = pl.BlockSpec(memory_space=pl.ANY)
     vmem = pl.BlockSpec(memory_space=pltpu.VMEM)
     shape = jax.ShapeDtypeStruct
     return pl.pallas_call(
         experts_kernel,
         out_shape=(
             shape((tokens, model + 128), jnp.float32),
-            shape((reach, model), low),
-            shape(weights.shape, low),
+            shape((tokens // 2, EARLY), jnp.float32),
+            shape((reach, model - EARLY), low),
+            shape((ep, rows, full), low),
+            shape((ep, rows, full), low),
             shape((tokens, 128), jnp.float32),
         ),
         in_specs=[vmem] * 5,
-        out_specs=(vmem,) * 4,
+        out_specs=(vmem, vmem, anywhere, anywhere, anywhere, vmem),
         scratch_shapes=[
             pltpu.VMEM((reach, 128), jnp.float32),
             pltpu.VMEM((reach, span), low),
             pltpu.VMEM((reach, 2 * span), low),
             pltpu.VMEM((reach, model + 128), low),
+            pltpu.VMEM((reach, model), low),
+            pltpu.VMEM(weights.shape, low),
+            pltpu.VMEM((ep, 2, rows, full // 2), low),
+            pltpu.VMEM((ep, 2, rows, full // 2), low),
+            dma((2, ep, 2)),
+            dma((2, ep, 2)),
+            dma((3,)),
         ]
-        + z_sum_scratch(ep, tokens, model + 128, low),
+        + z_sum_scratch(ep, tokens, model + 128, low)
+        + z_sum_scratch(ep, tokens, EARLY, low),
         compiler_params=pltpu.CompilerParams(
-            collective_id=collective_id, has_side_effects=True, vmem_limit_bytes=60 * 1024 * 1024
+            collective_id=collective_id, has_side_effects=True, vmem_limit_bytes=63 * 1024 * 1024
         ),
-        cost_estimate=lasting(70),
+        cost_estimate=lasting(90),
         name="experts",
     )(tokens_all, outer_all, routes_all, extra, weights)
 
 
 def rear_kernel(
     returned_ref, gates_ref, middle_ref, input_ref, outer_ref, normed1_ref, query_ref, pair_ref, mixed_ref,
-    log_ref, cos_ref, sin_ref, segment_ref, extra_ref, mixture_ref, sums_ref, attn_ref,
-    input_grad, layer_out, qkv_out, wo_out, small_out, expert_out,
-    wo_s, qkv_s, small_s, query_s, grad_s, mixed_s, key_s, value_s, bias_s, query_grad_s, key_grad_s, value_grad_s,
-    pair_s, landing_s, back_s, attn_grad_s, part_s, other_s, logit_s, gains_s, mixture_s, own_s, relay_s,
-    local_sem, key_send, key_recv, pair_send, pair_recv, *scratch,
+    log_ref, cos_ref, sin_ref, segment_ref, extra_ref, mixed_sum_ref, mixture_ref, relay_ref, own_ref, attn_ref,
+    input_grad, layer_out, qkv_out, wo_out, expert_out,
+    wo_s, qkv_s, query_s, grad_s, mixed_s, key_s, value_s, bias_s, query_grad_s, key_grad_s, value_grad_s,
+    pair_s, landing_s, back_s, attn_grad_s, part_s, other_s, router_s, gains_s, mixture_s, own_s, second_s,
+    local_sem, key_send, key_recv, pair_send, pair_recv, second_send, second_recv, swap_send, swap_recv, *scratch,
 ):
     ep, rows = expert_out.shape[0], expert_out.shape[1]
     f, c, t = lax.axis_index("fsdp"), lax.axis_index("ctx"), lax.axis_index("tp")
@@ -817,20 +917,16 @@
     sent = []
     mixture = ZSum(mixture_ref, scratch[: ZSum.size], sent, mixture_s)
     scratch = scratch[ZSum.size :]
-    size = len(shard_sum_scratch(ep, rows, 256, low, False))
-    experts = ShardSum(sums_ref, rows, sums_ref.shape[1], scratch[:size], sent, own_s, relay_s)
-    scratch = scratch[size:]
     size = len(shard_sum_scratch(ep, rows, 256, low))
     wo = ShardSum(wo_s, rows, width, scratch[:size], sent)
-    qkv = ShardSum(qkv_s, rows, qkv_width, scratch[size : 2 * size], sent)
-    small = ShardSum(small_s, rows, 128, scratch[2 * size :], sent)
+    qkv = ShardSum(qkv_s, rows, qkv_width + 128, scratch[size:], sent)
     partners = all_partners(ep)
     plane = [at_device(f, c ^ k, t) for k in range(1, 4)]
     core = partners[-1]
 
     copies = [
         pltpu.make_async_copy(attn_ref.at[:, pl.ds(qkv_width + 128, width)], wo_s, local_sem.at[0]),
-        pltpu.make_async_copy(attn_ref.at[:, pl.ds(0, qkv_width)], qkv_s, local_sem.at[1]),
+        pltpu.make_async_copy(attn_ref.at[:, pl.ds(0, qkv_width + 128)], qkv_s, local_sem.at[1]),
     ]
     for copy in copies:
         copy.start()
@@ -838,11 +934,41 @@
         pltpu.make_async_copy(
             mixture_ref.at[mixture.place(mixture.peer(d), t)], mixture_s.at[d], local_sem.at[2]
         ).start()
-    experts.load(local_sem.at[3])
+    copies.append(pltpu.make_async_copy(own_ref, own_s, local_sem.at[3]))
+    copies[2].start()
     greet(partners + plane[2:])
-    for d in experts.order:
+    order = wo.order
+    for d in order:
         mixture.to_core(d)
-    experts.first()
+    full = relay_ref.shape[2]
+    seconds = {}
+
+    def second(d):
+        for way in range(2):
+            block = (d, slice(None), pl.ds(way * (full // 2), full // 2))
+            copy = remote(
+                relay_ref.at[block], second_s.at[block], second_send.at[way, d], second_recv.at[way, d],
+                plane[1 - way],
+            )
+            copy.start()
+            sent.append((None, copy))
+            seconds[way, d] = copy
+
+    def swap(d):
+        for way in range(2):
+            seconds[way, d].wait_recv()
+        own_s[d] = (own_s[d].astype(jnp.float32) + second_s[d].astype(jnp.float32)).astype(low)
+        if d == 0:
+            copy = pltpu.make_async_copy(own_s.at[0], expert_out.at[f], swap_send.at[0])
+            copy.start()
+            copies.append(copy)
+        else:
+            copy = remote(own_s.at[d], expert_out.at[f], swap_send.at[d], swap_recv.at[d], partners[d - 1])
+            copy.start()
+            sent.append((None, copy))
+
+    for d in order:
+        second(d)
 
     small_lane = lax.broadcasted_iota(jnp.int32, (tokens, 128), 1)
     gains = extra_ref[...].astype(jnp.float32).T
@@ -851,7 +977,6 @@
     picked = jnp.where(small_lane < EXPERTS, tail + pltpu.roll(tail, 128 - EXPERTS, 1), 0.0)
     gates = gates_ref[...]
     logit_grad = (gates * (picked - jnp.sum(gates * picked, -1, keepdims=True))).astype(low)
-    logit_s[...] = logit_grad
     second_grad = returned_ref[:, :model] + lax.dot_general(
         logit_grad, extra_ref[...], (((1,), (1,)), ((), ())), preferred_element_type=jnp.float32
     )
@@ -866,6 +991,9 @@
     input_grad[...] = middle_grad
     attn_grad_s[...] = middle_grad.astype(low)
 
+    pltpu.make_async_copy(mixture_s, mixture_s, local_sem.at[2]).wait()
+    for d in range(1, ep):
+        mixture.to_z(d)
     copies[0].wait()
     for start in range(0, width, 256):
         tile = jnp.dot(
@@ -873,19 +1001,6 @@
         ).astype(low)
         for side in range(0, 256, HD):
             grad_s[(start + side) // HD] = tile[:, side : side + HD]
-
-    def wo_sums(n, carry):
-        at = pl.ds(pl.multiple_of(n * 256, 256), 256)
-        wo_s[at, :] = lax.dot_general(
-            attn_grad_s[:, at], mixed_ref[...], (((0,), (0,)), ((), ())), preferred_element_type=jnp.float32
-        ).astype(low)
-        return carry
-
-    lax.fori_loop(0, model // 256, wo_sums, 0)
-    pltpu.make_async_copy(mixture_s, mixture_s, local_sem.at[2]).wait()
-    for d in range(1, ep):
-        mixture.to_z(d)
-    wo.first()
 
     length = segment_ref.shape[1]
     seg_keys = jnp.broadcast_to(segment_ref[...].astype(jnp.float32), (128, length)).T[:, :1]
@@ -931,7 +1046,25 @@
         place = pl.ds(pl.multiple_of((c ^ k) * tokens, 16), tokens)
         copy = remote(pair_s.at[place], landing_s.at[k - 1], key_send.at[k - 1], key_recv.at[k - 1], plane[k - 1])
         copy.start()
-        sent.append(copy)
+        sent.append((None, copy))
+    def wo_sums(n, carry):
+        at = pl.ds(pl.multiple_of(n * 256, 256), 256)
+        wo_s[at, :] = lax.dot_general(
+            attn_grad_s[:, at], mixed_ref[...], (((0,), (0,)), ((), ())), preferred_element_type=jnp.float32
+        ).astype(low)
+        return carry
+
+    lax.fori_loop(0, model // 256, wo_sums, 0)
+    router_s[...] = lax.dot_general(
+        (middle * inverse * gain_two).astype(low), logit_grad, (((0,), (0,)), ((), ())),
+        preferred_element_type=jnp.float32,
+    )
+
+    copies[2].wait()
+    for d in order:
+        wo.first(d)
+    for d in order:
+        swap(d)
     first_half = lax.rem(small_lane, HD) < HD // 2
 
     def turned_back(tile):
@@ -941,14 +1074,6 @@
     for start in range(0, width, 128):
         tile = jnp.concatenate([query_grad_s[start // HD], query_grad_s[start // HD + 1]], 1)
         back_s[:, start : start + 128] = turned_back(tile).astype(low)
-
-    experts.loaded(local_sem.at[3])
-    for d in experts.order:
-        experts.second(d)
-    total = mixture.collect()
-    half = mixture.rows(t)
-    layer_out[half, :] = (middle_ref[half, :] + total).astype(low)
-    mixture.share(layer_out)
 
     pair = pair_s[pl.ds(pl.multiple_of(c * tokens, 16), tokens), :].astype(jnp.float32)
     for k in (1, 2, 3):
@@ -961,71 +1086,70 @@
     copies[1].wait()
     for start in range(0, model, 256):
         part_s[:, start : start + 256] = lax.dot_general(
-            back_s[...], qkv_s[start : start + 256, :], across, preferred_element_type=jnp.float32
+            back_s[...], qkv_s[start : start + 256, :qkv_width], across, preferred_element_type=jnp.float32
         ).astype(low)
     exchange = remote(part_s, other_s, pair_send, pair_recv, core)
     exchange.start()
-    sent.append(exchange)
+    sent.append((None, exchange))
 
     def qkv_sums(n, carry):
         at = pl.ds(pl.multiple_of(n * 256, 256), 256)
-        qkv_s[at, :] = lax.dot_general(
+        qkv_s[at, :qkv_width] = lax.dot_general(
             normed1_ref[:, at], back_s[...], (((0,), (0,)), ((), ())), preferred_element_type=jnp.float32
         ).astype(low)
         return carry
 
     lax.fori_loop(0, model // 256, qkv_sums, 0)
-    qkv.first()
-    for d in wo.order:
-        wo.second(d)
-    for d in experts.order:
-        experts.swap_z(d, expert_out)
-
     exchange.wait_recv()
     first_grad = part_s[...].astype(jnp.float32) + other_s[...].astype(jnp.float32)
     inputs = input_ref[...].astype(jnp.float32)
     inverse = lax.rsqrt(jnp.mean(inputs * inputs, -1, keepdims=True) + EPSILON)
     gains_s[0:1, :] = jnp.sum(first_grad * inputs * inverse, 0, keepdims=True)
+    line = lax.broadcasted_iota(jnp.int32, (128, model), 0)
+    turned = jnp.where(line == EXPERTS, gains_s[0:1, :], jnp.where(line == EXPERTS + 1, gains_s[1:2, :], 0.0)).T
+    qkv_s[:, qkv_width:] = (router_s[...] + turned).astype(low)
+    qkv.first(1)
+    qkv.first(2)
+    for d in wo.order:
+        wo.second(d)
     scaled = first_grad * gain_one
     mean_term = jnp.mean(scaled * inputs, -1, keepdims=True)
     input_grad[...] += inverse * scaled - inputs * (inverse * inverse * inverse) * mean_term
-    middle = middle_ref[...]
-    inverse = lax.rsqrt(jnp.mean(middle * middle, -1, keepdims=True) + EPSILON)
-    normed2 = (middle * inverse * gain_two).astype(low)
-    router_sums = lax.dot_general(
-        normed2, logit_s[...], (((0,), (0,)), ((), ())), preferred_element_type=jnp.float32
-    )
-    line = lax.broadcasted_iota(jnp.int32, (128, model), 0)
-    turned = jnp.where(line == EXPERTS, gains_s[0:1, :], jnp.where(line == EXPERTS + 1, gains_s[1:2, :], 0.0)).T
-    small_s[...] = (router_sums + turned).astype(low)
-    small.first()
-
-    for d in wo.order:
-        wo.to_z(d, wo_out)
-    for d in qkv.order:
-        qkv.second(d)
-    for d in small.order:
-        small.second(d)
-    for d in qkv.order:
-        qkv.to_z(d, qkv_out)
-    for d in small.order:
-        small.to_z(d, small_out)
+    qkv.second(1)
+    qkv.first(3)
+    wo.to_z(1, wo_out)
+    qkv.second(2)
+    qkv.first(0)
+    qkv.to_z(1, qkv_out)
+    wo.to_z(2, wo_out)
+    qkv.second(3)
+    qkv.to_z(2, qkv_out)
+    wo.to_z(3, wo_out)
+    qkv.second(0)
+    qkv.to_z(3, qkv_out)
+    wo.to_z(0, wo_out)
+    qkv.to_z(0, qkv_out)
+    half = mixture.rows(t)
+    layer_out[half, :EARLY] = (middle_ref[half, :EARLY] + mixed_sum_ref[...]).astype(low)
+    layer_out[half, EARLY:] = (middle_ref[half, EARLY:] + mixture.collect()).astype(low)
+    mixture.share(layer_out)
+    copies[3].wait()
+    for d in range(1, ep):
+        landing = expert_out.at[lax.rem(f + ep - d, ep)]
+        remote(landing, landing, swap_send.at[d], swap_recv.at[d], core).wait_recv()
+    wo.from_z(wo_out)
     mixture.finish(layer_out)
-    experts.swapped_z(expert_out)
-    wo.from_z(wo_out)
-    small.from_z(small_out)
     qkv.from_z(qkv_out)
-    for copy in sent:
-        copy.wait_send()
+    all_sent(sent)
 
 
 def rear(
     returned, gates, middle, inputs, outer, normed1, query, pair, mixed, log_total, cosine, sine, segments, extra,
-    mixture, sums, attn, collective_id,
+    mixed_sum, mixture, relay, own, attn, collective_id,
 ):
     ep = lax.axis_size("fsdp")
     tokens, model = inputs.shape
-    rows = sums.shape[0] // (4 * ep)
+    rows = own.shape[1]
     heads, key_heads = query.shape[1] // HD, pair.shape[1] // (2 * HD)
     width, kv_width = heads * HD, key_heads * HD
     qkv_width = width + 2 * kv_width
@@ -1041,17 +1165,15 @@
         out_shape=(
             shape((tokens, model), jnp.float32),
             shape((tokens, model), low),
-            shape((rows, qkv_width), jnp.float32),
+            shape((rows, qkv_width + 128), jnp.float32),
             shape((rows, width), jnp.float32),
-            shape((rows, 128), jnp.float32),
-            shape((ep, rows, sums.shape[1]), low),
+            shape(own.shape, low),
         ),
-        in_specs=[vmem] * 14 + [anywhere] * 3,
-        out_specs=(vmem,) * 5 + (anywhere,),
+        in_specs=[vmem] * 15 + [anywhere] * 4,
+        out_specs=(vmem,) * 4 + (anywhere,),
         scratch_shapes=[
             room((model, width), low),
-            room((model, qkv_width), low),
-            room((model, 128), low),
+            room((model, qkv_width + 128), low),
             room((heads, tokens, HD), low),
             room((heads, tokens, HD), low),
             room((heads, tokens, HD), low),
@@ -1067,22 +1189,24 @@
             room((tokens, model), low),
             room((tokens, model), low),
             room((tokens, model), low),
-            room((tokens, 128), low),
+            room((model, 128), jnp.float32),
             room((8, model), jnp.float32),
-            room((ep, tokens // 2, model), low),
-            room((ep, rows, sums.shape[1]), low),
-            room((ep, rows, sums.shape[1]), low),
+            room((ep, tokens // 2, model - EARLY), low),
+            room(own.shape, low),
+            room(own.shape, low),
             dma((4,)),
             dma((3,)),
             dma((3,)),
             dma,
             dma,
+            dma((2, ep)),
+            dma((2, ep)),
+            dma((ep,)),
+            dma((ep,)),
         ]
-        + z_sum_scratch(ep, tokens, model, low)
-        + shard_sum_scratch(ep, rows, sums.shape[1], low, False)
+        + z_sum_scratch(ep, tokens, model - EARLY, low)
         + shard_sum_scratch(ep, rows, width, low)
-        + shard_sum_scratch(ep, rows, qkv_width, low)
-        + shard_sum_scratch(ep, rows, 128, low),
+        + shard_sum_scratch(ep, rows, qkv_width + 128, low),
         compiler_params=pltpu.CompilerParams(
             collective_id=collective_id, has_side_effects=True, vmem_limit_bytes=63 * 1024 * 1024
         ),
@@ -1090,8 +1214,68 @@
         name="rear",
     )(
         returned, gates, middle, inputs, outer, normed1, query, pair, mixed, log_total, cosine, sine, segments,
-        extra, mixture, sums, attn,
-    )
+        extra, mixed_sum, mixture, relay, own, attn,
+    )
+
+
+def finish_kernel(
+    expert_ref, qkv_ref, wo_ref, query_out, key_out, value_out, output_out, gate_out, up_out, down_out
+):
+    local, _, hidden = gate_out.shape
+    for e in range(local):
+        for kind, out in enumerate((gate_out, up_out, down_out)):
+            start = (kind * local + e) * hidden
+            block = expert_ref[0, :, start : start + hidden].astype(jnp.float32)
+            out[e] = block.T if kind == 2 else block
+
+    @pl.when(pl.program_id(0) == 0)
+    def _():
+        width, kv_width = query_out.shape[1], key_out.shape[1]
+        query_out[...] = qkv_ref[:, :width]
+        key_out[...] = qkv_ref[:, width : width + kv_width]
+        value_out[...] = qkv_ref[:, width + kv_width : width + 2 * kv_width]
+        output_out[...] = wo_ref[...].T
+
+
+def finish(experts, qkv, wo, kv_width, hidden):
+    ep, rows, full = experts.shape
+    width = wo.shape[1]
+    local = full // (3 * hidden)
+    shape = jax.ShapeDtypeStruct
+
+    def whole(*dims):
+        return pl.BlockSpec(dims, lambda i: (0, 0))
+
+    return pl.pallas_call(
+        finish_kernel,
+        grid=(ep,),
+        out_shape=(
+            shape((rows, width), jnp.float32),
+            shape((rows, kv_width), jnp.float32),
+            shape((rows, kv_width), jnp.float32),
+            shape((width, rows), jnp.float32),
+            shape((ep * local, rows, hidden), jnp.float32),
+            shape((ep * local, rows, hidden), jnp.float32),
+            shape((ep * local, hidden, rows), jnp.float32),
+        ),
+        in_specs=[
+            pl.BlockSpec((1, rows, full), lambda i: (i, 0, 0)),
+            whole(*qkv.shape),
+            whole(*wo.shape),
+        ],
+        out_specs=(
+            whole(rows, width),
+            whole(rows, kv_width),
+            whole(rows, kv_width),
+            whole(width, rows),
+            pl.BlockSpec((local, rows, hidden), lambda i: (i, 0, 0)),
+            pl.BlockSpec((local, rows, hidden), lambda i: (i, 0, 0)),
+            pl.BlockSpec((local, hidden, rows), lambda i: (i, 0, 0)),
+        ),
+        compiler_params=pltpu.CompilerParams(vmem_limit_bytes=32 * 1024 * 1024),
+        cost_estimate=lasting(6),
+        name="finish",
+    )(experts, qkv, wo)
 
 
 def plain_shards(
@@ -1371,11 +1555,9 @@
     cotangent,
 ):
     low = jnp.bfloat16
-    ep = lax.axis_size("fsdp")
-    rows, width = query_weight.shape
+    width = query_weight.shape[1]
     kv_width = key_weight.shape[1]
     hidden_width = gate_weight.shape[2]
-    local = EXPERTS // ep
     extra = jnp.concatenate([router_weight, norm_gain[:, None], ffn_gain[:, None]], 1)
     extra = jnp.pad(extra, ((0, 0), (0, 128 - extra.shape[1])))
     attn_shard = jnp.concatenate([query_weight, key_weight, value_weight, extra, output_weight.T], 1)
@@ -1387,29 +1569,29 @@
         attn_shard, gate_weight, up_weight, down_weight.transpose(0, 2, 1), cotangent, routes, layer_input,
         segments, jnp.tile(freq, 4)[None, :], width // HD, kv_width // HD,
     )
-    returned, mixture, expert_sums, gates = run_experts(
+    returned, mixed_sum, mixture, relay, own, gates = run_experts(
         normed2_all, outer_all, routes_all, extra_all, expert_full, 2
     )
-    input_grad, layer_output, qkv_out, wo_out, small_out, expert_out = rear(
+    input_grad, layer_output, qkv_out, wo_out, expert_out = rear(
         returned, gates, middle, layer_input, cotangent, normed1, query, pair_all, mixed, log_total, cosine, sine,
-        segments, extra_all, mixture, expert_sums, attn_full, 3,
-    )
-    expert_out = expert_out.reshape(ep, rows, 3, local, hidden_width)
-    side_out = expert_out[:, :, :2].transpose(2, 0, 3, 1, 4).reshape(2, EXPERTS, rows, hidden_width)
-    side_out = side_out.astype(jnp.float32)
-    down_out = expert_out[:, :, 2].transpose(0, 2, 3, 1).reshape(EXPERTS, hidden_width, rows).astype(jnp.float32)
+        segments, extra_all, mixed_sum, mixture, relay, own, attn_full, 3,
+    )
+    small_out = qkv_out[:, width + 2 * kv_width :]
+    query_out, key_out, value_out, output_out, gate_out, up_out, down_out = finish(
+        expert_out, qkv_out, wo_out, kv_width, hidden_width
+    )
     return (
         layer_output,
         input_grad,
         small_out[:, EXPERTS],
-        qkv_out[:, :width],
-        qkv_out[:, width : width + kv_width],
-        qkv_out[:, width + kv_width :],
-        wo_out.T,
+        query_out,
+        key_out,
+        value_out,
+        output_out,
         small_out[:, EXPERTS + 1],
         small_out[:, :EXPERTS],
-        side_out[0],
-        side_out[1],
+        gate_out,
+        up_out,
         down_out,
     )
 

time: 463 us -> 398 us (0.86)
  Pallas kernels: 429 us -> 373 us
  local copies, waits for them, and re-layouts: 24.9 us -> 18.6 us
    pallas_call x1, Pallas kernels: 182 us -> 114 us  [rear(): pl.pallas_call(rear_kernel, out_shape=(shape((tokens, model), jnp.float32...]
    pallas_call x1, Pallas kernels: 68.3 us -> 98 us  [run_experts(): pl.pallas_call(experts_kernel, out_shape=(shape((tokens, model + 128), jn...]
    pallas_call x1, Pallas kernels: 179 us -> 158 us  [front(): pl.pallas_call(front_kernel, out_shape=(shape((total, 3 * local * gate.sh...]
    slice x5 -> x1, local copies, waits for them, and re-layouts: 6.73 us -> 0.8 us  [shards(): small_out[:, :EXPERTS]]
    unnamed x17 -> x22, local copies, waits for them, and re-layouts: 8.99 us -> 14.5 us
where the time goes in v4:
time: 398 us; the launch traced here: 394 us
  Pallas kernels  373 us (94%)
  local copies, waits for them, and re-layouts  18.6 us (5%)
    pallas_call x1, Pallas kernels, front(): pl.pallas_call(front_kernel, out_shape=(shape((total, 3 * local * gate.sh...  158 us
    pallas_call x1, Pallas kernels, rear(): pl.pallas_call(rear_kernel, out_shape=(shape((tokens, model), jnp.float32...  114 us
    pallas_call x1, Pallas kernels, run_experts(): pl.pallas_call(experts_kernel, out_shape=(shape((tokens, model + 128), jn...  98 us
    unnamed x22, local copies, waits for them, and re-layouts  14.5 us

profile of v4, /device:TPU:9, one launch (start us, length us, event | category | flops | bytes accessed | tf_op | source)
XLA Modules:
  0.0 393.5 jit_solution(5436564746828211001)
XLA Ops:
  0.7 0.6 broadcast_in_dim_tile.3.freq_ref
  1.3 0.7 pad_maximum_fusion
  2.0 0.1 copy.40
  2.1 1.5 copy.41.routes_ref
  3.6 0.9 constant_dynamic-update-slice_fusion.2
  4.5 0.8 constant_dynamic-update-slice_fusion.1
  5.3 0.8 constant_dynamic-update-slice_fusion
  6.1 0.9 bitcast_dynamic-update-slice_fusion.attn_ref
  7.1 0.0 copy-start.5
  7.1 0.7 copy-done.5
  7.8 158.3 %front.1 = (bf16[1536,3072]{1,0:T(8,128)(2,1)}, bf16[1024,1536]{1,0:T(8,128)(2,1)}, s32[1024,8]{1,0:T(8,128)}, bf16[1024,1536]{1,0:T(8,128)(2,1)}, bf16[1536,217...) custom-call(bf16[96,2176]{1,0:T(8,128)(2,1)} %copy-done.5, ...), custom_call_target="tpu_custom_call" | custom-call | bytes 664200000 | tf_op jit(solution)/shard_map/front/pallas_call | solution.py:435
  166.1 98.0 %experts.1 = (f32[256,1664]{1,0:T(8,128)}, f32[128,768]{1,0:T(8,128)}, bf16[1024,768]{1,0:T(8,128)(2,1)}, bf16[4,96,3072]{2,1,0:T(8,128)(2,1)}, bf16[4,96,3072]{2,1,0:T(8,128)(2,1)}, /*index=5*/f32[256,128]{1,0:T(8,128)}) custom-call(bf16[1024,1536]{1,0:T(8,128)(2,1)} %get-tuple-element.44.tokens_ref, bf16[1024,1536]{1,0:T(8,128)(2,1)} %get-tuple-element.45.outer_ref, ...), custom_call_target="tpu_custom_call" | custom-call | bytes 332100000 | tf_op jit(solution)/shard_map/experts/pallas_call | solution.py:866
  264.1 114.4 %rear.1 = (f32[256,1536]{1,0:T(8,128)}, bf16[256,1536]{1,0:T(8,128)(2,1)}, f32[96,1408]{1,0:T(8,128)}, f32[96,768]{1,0:T(8,128)}, bf16[4,96,3072]{2,1,0:T(8,128)(2,1)}) custom-call(f32[256,1664]{1,0:T(8,128)} %get-tuple-element.49.returned_ref, f32[256,128]{1,0:T(8,128)} %get-tuple-element.50.gates_ref, f32[256,1536]{1,0:T(8,128)} %get-tuple-element.51.middle_ref, ...), custom_call_target="tpu_custom_call" | custom-call | bytes 627299968 | tf_op jit(solution)/shard_map/rear/pallas_call | solution.py:1163
  378.6 1.6 slice_reduce_fusion
  380.2 0.8 slice.15
  381.0 0.7 copy.43
  381.6 0.0 copy-start
  381.6 1.7 copy-done
  383.3 0.0 copy-start.1
  383.3 1.0 copy-done.1
  384.4 0.0 copy-start.2
  384.4 1.0 copy-done.2
  385.3 2.6 finish.1
  387.9 0.0 copy-start.4
  387.9 0.9 copy.42
  388.8 1.7 copy.44
  390.5 0.0 copy-done.4
  390.5 0.0 copy-start.3
  390.5 0.9 copy.51
  391.4 0.8 copy-done.3
  392.2 1.1 copy.52
  (3 shorter events, 0.0 us)
Async XLA Ops:
  7.1 0.8 copy-start.5
  381.6 1.7 copy-start
  383.3 1.0 copy-start.1
  384.4 1.0 copy-start.2
  387.9 2.6 copy-start.4
  390.5 1.7 copy-start.3

commit v5 on v4

--- a/solution.py
+++ b/solution.py
@@ -1,5 +1,6 @@
 import jax
 import jax.numpy as jnp
+import numpy as np
 from jax import lax
 from jax.experimental import pallas as pl
 from jax.experimental.pallas import tpu as pltpu
@@ -10,7 +11,6 @@
 D = 1536
 HD = 64
 EXPERTS = 16
-EARLY = 768
 
 
 EPSILON = 1e-05
@@ -82,6 +82,13 @@
     return {"fsdp": fsdp, "ctx": ctx, "tp": tp}
 
 
+def fetch(pairs, sems):
+    copies = [pltpu.make_async_copy(source, target, sems.at[i]) for i, (source, target) in enumerate(pairs)]
+    for copy in copies:
+        copy.start()
+    return copies
+
+
 def greet(partners):
     barrier = pltpu.get_barrier_semaphore()
     for device in partners:
@@ -100,9 +107,11 @@
 
 
 def front_kernel(
-    attn_ref, gate_ref, up_ref, down_ref, outer_ref, routes_ref, input_ref, segment_ref, freq_ref,
+    query_ref, key_ref, value_ref, extra_ref, wo_ref, gate_ref, up_ref, down_ref, outer_ref, routes_ref,
+    input_ref, segment_ref, freq_ref,
     expert_out, outer_out, routes_out, normed2_out,
-    attn_out, normed1_out, query_out, pair_out, mixed_out, log_out, middle_out, cos_out, sin_out, extra_out,
+    attn_hbm, normed1_hbm, query_hbm, pair_hbm, mixed_hbm, middle_hbm, log_out, cos_out, sin_out, extra_out,
+    attn_out, normed1_out, query_out, pair_out, mixed_out, middle_out, out_sem,
     query_s, key_s, value_s, mixed_s, bias_s, part_s, other_s, normed2_s,
     local_sem, z_send, z_recv, plane_send, plane_recv, relay_send, relay_recv, core_send, core_recv,
     key_send, key_recv, pair_send, pair_recv, chain_send, chain_recv,
@@ -110,7 +119,7 @@
     ep = z_send.shape[1] + 1
     f, c, t = lax.axis_index("fsdp"), lax.axis_index("ctx"), lax.axis_index("tp")
     low = jnp.bfloat16
-    rows = attn_ref.shape[0]
+    rows = query_ref.shape[0]
     local = gate_ref.shape[0] // ep
     hidden = gate_ref.shape[2]
     tokens = outer_ref.shape[0]
@@ -233,43 +242,43 @@
     own_tokens = pl.ds(pl.multiple_of(f * tokens, 16), tokens)
     my_half = pl.ds(pl.multiple_of(t * half, 16), half)
 
-    def line_send(kind, source, target):
-        for d in range(1, ep):
-            send(
-                remote(
-                    source, target.at[line_place(f, t)], z_send.at[kind, d - 1], z_recv.at[kind, d - 1], line[d - 1]
-                )
+    def line_hop(kind, hop, target):
+        for way in range(2):
+            g, there = chain_origin(way, hop)
+            block = target.at[line_place(g, t)]
+            chain_hop(kind, way, hop, block)
+            send(remote(block, block, core_send.at[kind - 1, g], core_recv.at[kind - 1, g], core), there)
+
+    def line_settle(kind, target):
+        for g in range(ep):
+            block = target.at[line_place(g, 1 - t)]
+            await_arrival(
+                remote(block, block, core_send.at[kind - 1, g], core_recv.at[kind - 1, g], core), f != g
             )
 
-    def line_forward(kind, target):
-        for d in range(1, ep):
-            block = target.at[line_place(peer(ep - d), t)]
-            remote(block, block, z_send.at[kind, d - 1], z_recv.at[kind, d - 1], core).wait_recv()
-            send(remote(block, block, core_send.at[kind - 2, d], core_recv.at[kind - 2, d], core))
-
-    def line_settle(kind, target):
-        for d in range(1, ep):
-            block = target.at[line_place(peer(ep - d), 1 - t)]
-            remote(block, block, core_send.at[kind - 2, d], core_recv.at[kind - 2, d], core).wait_recv()
-
-    chain_begin(0, attn_ref, attn_out.at[mine])
-    own_attn = pltpu.make_async_copy(attn_ref, attn_out.at[mine], local_sem.at[0])
-    own_attn.start()
+    start = 0
+    for ref in (query_ref, key_ref, value_ref, extra_ref, wo_ref):
+        pltpu.make_async_copy(
+            ref, attn_out.at[mine, pl.ds(start, ref.shape[1])], local_sem.at[0]
+        ).start()
+        start += ref.shape[1]
+    pltpu.make_async_copy(attn_out.at[mine], attn_out.at[mine], local_sem.at[0]).wait()
+    chain_begin(0, attn_out.at[mine], attn_out.at[mine])
     own_outer = pltpu.make_async_copy(outer_ref, outer_out.at[own_tokens], local_sem.at[2])
     own_outer.start()
-    own_routes = pltpu.make_async_copy(routes_ref, routes_out.at[own_tokens], local_sem.at[3])
+    own_columns = (slice(None), pl.ds(pl.multiple_of(f * tokens, 128), tokens))
+    own_routes = pltpu.make_async_copy(routes_ref, routes_out.at[own_columns], local_sem.at[3])
     own_routes.start()
     for d in range(1, ep):
         send(
             remote(
-                routes_ref, routes_out.at[own_tokens], z_send.at[4, d - 1], z_recv.at[4, d - 1], line[d - 1]
+                routes_ref, routes_out.at[own_columns], z_send.at[4, d - 1], z_recv.at[4, d - 1], line[d - 1]
             )
         )
     for kind, ref in enumerate((gate_ref, up_ref, down_ref)):
         for e in range(local):
             target = expert_out.at[mine, pl.ds((kind * local + e) * hidden, hidden)]
             pltpu.make_async_copy(ref.at[f * local + e], target, local_sem.at[1]).start()
-    own_attn.wait()
     spread(0, f)
 
     length = segment_ref.shape[1]
@@ -314,9 +323,16 @@
     pltpu.make_async_copy(expert_out.at[mine], expert_out.at[mine], local_sem.at[1]).wait()
     spread(1, f)
     settle(0)
+    stores = [pltpu.make_async_copy(attn_out, attn_hbm, out_sem.at[0])]
+    stores[0].start()
+
+    def store(number, source, target):
+        stores.append(pltpu.make_async_copy(source, target, out_sem.at[number]))
+        stores[-1].start()
 
     gains = attn_out[:, qkv_width : qkv_width + 128].astype(jnp.float32).T
     normed1_out[...] = (inputs * inverse * gains[EXPERTS : EXPERTS + 1, :]).astype(low)
+    store(1, normed1_out, normed1_hbm)
 
     def project(start):
         return jnp.dot(
@@ -340,11 +356,13 @@
         tile = project(start)
         for side in (0, 128):
             query_out[:, start + side : start + side + 128] = turned(tile[:, side : side + 128]).astype(low)
+    store(2, query_out, query_hbm)
     for h in range(heads):
         query_s[h] = query_out[:, h * HD : (h + 1) * HD]
     for k in range(1, 4):
         block = pair_out.at[pl.ds(pl.multiple_of((c ^ k) * tokens, 16), tokens)]
         remote(block, block, key_send.at[k - 1], key_recv.at[k - 1], plane[k - 1]).wait_recv()
+    store(3, pair_out, pair_hbm)
     for g in range(key_heads):
         key_s[g] = pair_out[:, g * HD : (g + 1) * HD]
         value_s[g] = pair_out[:, kv_width + g * HD : kv_width + (g + 1) * HD]
@@ -352,7 +370,7 @@
     for d in range(1, ep):
         z_arrival(1, d)
         spread(1, peer(ep - d))
-    line_send(2, outer_ref.at[my_half], outer_out)
+    chain_begin(2, outer_ref.at[my_half], outer_out.at[line_place(f, t)])
 
     def attend(h, carry):
         g = lax.div(h, heads // key_heads)
@@ -371,6 +389,7 @@
     lax.fori_loop(0, heads, attend, 0)
     for h in range(heads):
         mixed_out[:, h * HD : (h + 1) * HD] = mixed_s[h]
+    store(4, mixed_out, mixed_hbm)
     model = input_ref.shape[1]
     for start in range(0, model, 256):
         part_s[:, start : start + 256] = lax.dot_general(
@@ -380,11 +399,13 @@
     exchange = remote(part_s, other_s, pair_send, pair_recv, core)
     send(exchange)
     pass_on(1, peer(ep - 1))
+    line_hop(2, 1, outer_out)
     exchange.wait_recv()
     middle = input_ref[...].astype(jnp.float32) + (
         part_s[...].astype(jnp.float32) + other_s[...].astype(jnp.float32)
     )
     middle_out[...] = middle
+    store(5, middle_out, middle_hbm)
     inverse = lax.rsqrt(jnp.mean(middle * middle, -1, keepdims=True) + EPSILON)
     gains = attn_out[:, qkv_width : qkv_width + 128].astype(jnp.float32).T
     normed2_s[...] = (middle * inverse * gains[EXPERTS + 1 : EXPERTS + 2, :]).astype(low)
@@ -393,20 +414,16 @@
     own_normed2.start()
     for d in range(2, ep):
         pass_on(1, peer(ep - d))
-    for hop in range(1, ep):
-        for way in range(2):
-            g, there = chain_origin(way, hop)
-            block = normed2_out.at[line_place(g, t)]
-            chain_hop(1, way, hop, block)
-            send(remote(block, block, core_send.at[1, g], core_recv.at[1, g], core), there)
-    line_forward(2, outer_out)
+    line_hop(1, 1, normed2_out)
+    line_hop(2, 2, outer_out)
+    line_hop(1, 2, normed2_out)
+    line_hop(2, 3, outer_out)
+    line_hop(1, 3, normed2_out)
     settle(1)
     line_settle(2, outer_out)
-    for g in range(ep):
-        block = normed2_out.at[line_place(g, 1 - t)]
-        await_arrival(remote(block, block, core_send.at[1, g], core_recv.at[1, g], core), f != g)
+    line_settle(1, normed2_out)
     for d in range(1, ep):
-        place = pl.ds(pl.multiple_of(peer(ep - d) * tokens, 16), tokens)
+        place = (slice(None), pl.ds(pl.multiple_of(peer(ep - d) * tokens, 128), tokens))
         remote(
             routes_out.at[place], routes_out.at[place], z_send.at[4, d - 1], z_recv.at[4, d - 1], core
         ).wait_recv()
@@ -417,12 +434,18 @@
     own_outer.wait()
     own_routes.wait()
     own_normed2.wait()
+    for copy in stores:
+        copy.wait()
     all_sent(sent)
 
 
-def front(attn, gate, up, down, outer, routes, inputs, segments, freq, heads, key_heads):
+def front(
+    query, key, value, extra, wo, gate, up, down, outer, routes, inputs, segments, freq
+):
     ep = lax.axis_size("fsdp")
-    rows = attn.shape[0]
+    rows = query.shape[0]
+    heads, key_heads = query.shape[1] // HD, key.shape[1] // HD
+    width = sum(part.shape[1] for part in (query, key, value, extra, wo))
     total = rows * ep * lax.axis_size("ctx")
     local = gate.shape[0] // ep
     tokens, model = inputs.shape
@@ -432,27 +455,34 @@
     anywhere = pl.BlockSpec(memory_space=pl.ANY)
     vmem = pl.BlockSpec(memory_space=pltpu.VMEM)
     shape = jax.ShapeDtypeStruct
+    kept = (
+        ((total, width), low),
+        ((tokens, model), low),
+        ((tokens, heads * HD), low),
+        ((length, 2 * key_heads * HD), low),
+        ((tokens, heads * HD), low),
+        ((tokens, model), jnp.float32),
+    )
     return pl.pallas_call(
         front_kernel,
         out_shape=(
             shape((total, 3 * local * gate.shape[2]), low),
             shape((ep * tokens, model), low),
-            shape((ep * tokens, routes.shape[1]), routes.dtype),
+            shape((routes.shape[0], ep * tokens), routes.dtype),
             shape((ep * tokens, model), low),
-            shape((total, attn.shape[1]), low),
-            shape((tokens, model), low),
-            shape((tokens, heads * HD), low),
-            shape((length, 2 * key_heads * HD), low),
-            shape((tokens, heads * HD), low),
+        )
+        + tuple(shape(*each) for each in kept)
+        + (
             shape((heads, 1, tokens), jnp.float32),
-            shape((tokens, model), jnp.float32),
             shape((tokens, 128), jnp.float32),
             shape((tokens, 128), jnp.float32),
             shape((total, 128), low),
         ),
-        in_specs=[anywhere] * 6 + [vmem] * 3,
-        out_specs=(anywhere,) * 4 + (vmem,) * 10,
-        scratch_shapes=[
+        in_specs=[anywhere] * 10 + [vmem] * 3,
+        out_specs=(anywhere,) * 10 + (vmem,) * 4,
+        scratch_shapes=[pltpu.VMEM(*each) for each in kept]
+        + [
+            dma((len(kept),)),
             pltpu.VMEM((heads, tokens, HD), low),
             pltpu.VMEM((key_heads, length, HD), low),
             pltpu.VMEM((key_heads, length, HD), low),
@@ -474,15 +504,15 @@
             dma((3,)),
             dma,
             dma,
-            dma((2, 2, ep - 1)),
-            dma((2, 2, ep - 1)),
+            dma((3, 2, ep - 1)),
+            dma((3, 2, ep - 1)),
         ],
         compiler_params=pltpu.CompilerParams(
-            collective_id=1, has_side_effects=True, vmem_limit_bytes=56 * 1024 * 1024
+            collective_id=1, has_side_effects=True, vmem_limit_bytes=60 * 1024 * 1024
         ),
-        cost_estimate=lasting(180),
+        cost_estimate=lasting(165),
         name="front",
-    )(attn, gate, up, down, outer, routes, inputs, segments, freq)
+    )(query, key, value, extra, wo, gate, up, down, outer, routes, inputs, segments, freq)
 
 
 def z_sum_scratch(ep, tokens, width, low):
@@ -503,8 +533,8 @@
 class ZSum:
     size = 9
 
-    def __init__(self, part, scratch, sent, own=None):
-        self.part, self.own, self.sent = part, own, sent
+    def __init__(self, part, scratch, sent):
+        self.part, self.sent = part, sent
         (
             self.core_in, self.z_out, self.z_in, self.core_send, self.core_recv,
             self.z_send, self.z_recv, self.back_send, self.back_recv,
@@ -529,8 +559,7 @@
     def to_core(self, d):
         self.send(
             remote(
-                self.part.at[self.place(self.peer(d), 1 - self.t), pl.ds(0, self.core_in.shape[2])],
-                self.core_in.at[d],
+                self.part.at[self.place(self.peer(d), 1 - self.t)], self.core_in.at[d],
                 self.core_send.at[d], self.core_recv.at[d], self.core,
             )
         )
@@ -538,10 +567,7 @@
     def added(self, d):
         landing = self.core_in.at[d]
         remote(landing, landing, self.core_send.at[d], self.core_recv.at[d], self.core).wait_recv()
-        if self.own is None:
-            mine = self.part[self.place(self.peer(d), self.t), : self.core_in.shape[2]]
-        else:
-            mine = self.own[d]
+        mine = self.part[self.place(self.peer(d), self.t), :]
         return mine.astype(jnp.float32) + self.core_in[d].astype(jnp.float32)
 
     def to_z(self, d):
@@ -568,6 +594,102 @@
     def finish(self, out):
         other = out.at[self.rows(1 - self.t)]
         remote(other, other, self.back_send, self.back_recv, self.core).wait_recv()
+
+
+def pair_sum_scratch(ep, tokens, width, low):
+    dma = pltpu.SemaphoreType.DMA
+    return [
+        pltpu.VMEM((ep, tokens // 2, width), low),
+        pltpu.VMEM((4, tokens // 2, width), low),
+        dma((ep,)),
+        dma((ep,)),
+        dma((4,)),
+        dma((4,)),
+        dma((2,)),
+    ]
+
+
+class PairSum:
+    def __init__(self, part, mine, scratch, sent):
+        self.part, self.mine, self.sent = part, mine, sent
+        (
+            self.own, self.landing, self.core_send, self.core_recv, self.send_sem, self.recv_sem, self.cross_sem
+        ) = scratch
+        self.ep, self.half = self.own.shape[0], self.own.shape[1]
+        self.f, c, self.t = lax.axis_index("fsdp"), lax.axis_index("ctx"), lax.axis_index("tp")
+        self.core = at_device(self.f, c, 1 - self.t)
+        self.partner = self.f ^ 1
+        self.inner = (self.f == 1) | (self.f == 2)
+        self.others = [2 - (self.f & 2) + j for j in range(2)]
+        self.devices = [at_device(g, c, self.t) for g in self.others]
+        self.beside = at_device(self.partner, c, self.t)
+
+    def place(self, g, part):
+        return pl.ds(pl.multiple_of(g * 2 * self.half + part * self.half, 16), self.half)
+
+    def send(self, copy, when=None):
+        if when is None:
+            copy.start()
+        else:
+            pl.when(when)(copy.start)
+        self.sent.append((when, copy))
+
+    def to_core(self):
+        for g in range(self.ep):
+            self.send(
+                remote(
+                    self.part.at[self.place(g, 1 - self.t)], self.own.at[g],
+                    self.core_send.at[g], self.core_recv.at[g], self.core,
+                )
+            )
+
+    def both_cores(self, g):
+        block = self.own.at[g]
+        remote(block, block, self.core_send.at[g], self.core_recv.at[g], self.core).wait_recv()
+        return self.mine[g].astype(jnp.float32) + self.own[g].astype(jnp.float32)
+
+    def begin(self):
+        outer = jnp.logical_not(self.inner)
+        for j, g in enumerate(self.others):
+            self.own[g] = self.both_cores(g).astype(self.own.dtype)
+            self.send(
+                remote(
+                    self.own.at[g], self.landing.at[1 + j], self.send_sem.at[1 + j], self.recv_sem.at[1 + j],
+                    self.beside,
+                ),
+                outer,
+            )
+        self.own[self.partner] = self.both_cores(self.partner).astype(self.own.dtype)
+        self.send(
+            remote(
+                self.own.at[self.partner], self.landing.at[0], self.send_sem.at[0], self.recv_sem.at[0], self.beside
+            )
+        )
+
+    def cross(self):
+        for j, g in enumerate(self.others):
+
+            @pl.when(self.inner)
+            def _():
+                block = self.landing.at[1 + j]
+                remote(block, block, self.send_sem.at[1 + j], self.recv_sem.at[1 + j], self.beside).wait_recv()
+                added = self.own[g].astype(jnp.float32) + self.landing[1 + j].astype(jnp.float32)
+                self.own[g] = added.astype(self.own.dtype)
+
+            self.send(
+                remote(
+                    self.own.at[g], self.landing.at[3], self.cross_sem.at[j], self.recv_sem.at[3], self.devices[j]
+                ),
+                self.inner,
+            )
+
+    def collect(self):
+        total = self.both_cores(self.f)
+        for slot in (0, 3):
+            block = self.landing.at[slot]
+            remote(block, block, self.send_sem.at[slot], self.recv_sem.at[slot], self.beside).wait_recv()
+            total = total + self.landing[slot].astype(jnp.float32)
+        return total
 
 
 def all_sent(sent):
@@ -699,47 +821,54 @@
 
 
 class PlaneHalf:
-    def __init__(self, part, rows, landings, send_sem, recv_sem, sent):
+    def __init__(self, part, rows, local, landings, send_sem, recv_sem, sent):
         self.part, self.rows, self.landings, self.sent = part, rows, landings, sent
         self.send_sem, self.recv_sem = send_sem, recv_sem
-        cut = landings[0].shape[-1]
-        self.columns = (pl.ds(0, cut), pl.ds(cut, part.shape[1] - cut))
+        self.local, self.cut = local, landings[0].shape[-1] // local
         self.ep = landings[0].shape[0]
         self.f, self.c, t = lax.axis_index("fsdp"), lax.axis_index("ctx"), lax.axis_index("tp")
         self.neighbours = (at_device(self.f, self.c ^ 1, t), at_device(self.f, self.c ^ 2, t))
 
-    def block(self, distance, ctx, way):
+    def block(self, distance, ctx, way, e):
         start = (lax.rem(self.f + distance, self.ep) * 4 + ctx) * self.rows
-        return pl.ds(pl.multiple_of(start, 16), self.rows), self.columns[way]
-
-    def start(self, d):
+        columns = pl.ds((2 * e + way) * self.cut, self.cut)
+        return pl.ds(pl.multiple_of(start, 16), self.rows), columns
+
+    def landed(self, d, number, way):
+        landing = self.landings[way].at[d, number]
+        return remote(
+            landing, landing, self.send_sem.at[way, d, number], self.recv_sem.at[way, d, number],
+            self.neighbours[way],
+        )
+
+    def start(self, d, e):
         for number in range(2):
             for way in range(2):
                 target = self.c ^ 3 if number == 0 else self.c ^ (1 << way)
-                copy = remote(
-                    self.part.at[self.block(d, target, way)], self.landings[way].at[d, number],
+                remote(
+                    self.part.at[self.block(d, target, way, e)],
+                    self.landings[way].at[d, number, :, pl.ds(e * self.cut, self.cut)],
                     self.send_sem.at[way, d, number], self.recv_sem.at[way, d, number], self.neighbours[way],
-                )
-                copy.start()
-                self.sent.append((None, copy))
+                ).start()
 
     def finish(self, d):
         for way in range(2):
             for number in range(2):
-                landing = self.landings[way].at[d, number]
-                remote(
-                    landing, landing, self.send_sem.at[way, d, number], self.recv_sem.at[way, d, number],
-                    self.neighbours[way],
-                ).wait_recv()
+                copy = self.landed(d, number, way)
+                copy.wait_recv()
+                self.sent.append((None, copy))
                 ctx = self.c ^ (2 >> way) if number == 0 else self.c
-                term = self.part[self.block(d, ctx, way)].astype(jnp.float32)
-                added = term + self.landings[way][d, number].astype(jnp.float32)
-                self.landings[way][d, number] = added.astype(self.part.dtype)
+                for e in range(self.local):
+                    at = slice(e * self.cut, (e + 1) * self.cut)
+                    term = self.part[self.block(d, ctx, way, e)].astype(jnp.float32)
+                    added = term + self.landings[way][d, number, :, at].astype(jnp.float32)
+                    self.landings[way][d, number, :, at] = added.astype(self.part.dtype)
 
 
 def experts_kernel(
-    tokens_ref, outer_ref, routes_ref, extra_ref, weight_ref,
-    returned_ref, mixed_ref, mixture_out, relay_out, own_out, gates_out,
+    routes_ref, extra_ref, tokens_hbm, outer_hbm, weight_hbm,
+    returned_ref, mixture_out, relay_out, own_out, gates_out,
+    tokens_ref, outer_ref, weight_ref, in_sem,
     gates_s, gated_s, side_s, part_s, mixture_s, sums_s, first_x, first_y, plane_send, plane_recv, local_sem, *scratch,
 ):
     ep = lax.axis_size("fsdp")
@@ -752,15 +881,25 @@
     local = EXPERTS // ep
     hidden = span // local
     sent = []
-    back = ZSum(part_s, scratch[: ZSum.size], sent)
-    mixture = ZSum(mixture_s, scratch[ZSum.size :], sent)
-    plane = PlaneHalf(sums_s, rows, (first_x, first_y), plane_send, plane_recv, sent)
+    back = ZSum(part_s, scratch, sent)
+    plane = PlaneHalf(sums_s, rows, local, (first_x, first_y), plane_send, plane_recv, sent)
+    pairs = [(tokens_hbm, tokens_ref), (outer_hbm, outer_ref)]
+    for e in range(local):
+        for kind in range(3):
+            at = (slice(None), pl.ds(kind * span + e * hidden, hidden))
+            pairs.insert(1 + 3 * e + kind + (e > 0 or kind > 1), (weight_hbm.at[at], weight_ref.at[at]))
+    coming = fetch(pairs, in_sem)
     greet(all_partners(ep))
 
     lane = lax.broadcasted_iota(jnp.int32, (reach, 128), 1)
-    chosen = routes_ref[:, 0:1] == lane
-    for k in range(1, routes_ref.shape[1]):
-        chosen = chosen | (routes_ref[:, k : k + 1] == lane)
+    uses = routes_ref.shape[0]
+    turned = jnp.concatenate(
+        [routes_ref[...].astype(jnp.float32), jnp.zeros((128 - uses, reach), jnp.float32)], 0
+    ).T.astype(jnp.int32)
+    chosen = turned[:, 0:1] == lane
+    for k in range(1, uses):
+        chosen = chosen | (turned[:, k : k + 1] == lane)
+    coming[0].wait()
     logits = jnp.dot(tokens_ref[...], extra_ref[...], preferred_element_type=jnp.float32)
     logits = jnp.where(chosen, logits, MASKED_SCORE)
     lifted = jnp.where(chosen, jnp.exp(logits - jnp.max(logits, -1, keepdims=True)), 0.0)
@@ -769,12 +908,18 @@
     gates_out[...] = gates_s[own, :]
 
     part_s[:, model:] = jnp.zeros((reach, 128), low)
-    for e in range(local):
+    order = list(range(1, ep)) + [0]
+    over = (((0,), (0,)), ((), ()))
+    across = (((1,), (1,)), ((), ()))
+
+    def act(e):
         at = slice(e * hidden, (e + 1) * hidden)
         at_up = slice(span + e * hidden, span + (e + 1) * hidden)
         at_down = slice(2 * span + e * hidden, 2 * span + (e + 1) * hidden)
         mine = lane == f * local + e
         gate = jnp.sum(jnp.where(mine, gates_s[...], 0.0), -1, keepdims=True)
+        for copy in coming[1:5] if e == 0 else coming[2 + 3 * e : 5 + 3 * e]:
+            copy.wait()
         former = jnp.dot(tokens_ref[...], weight_ref[:, at], preferred_element_type=jnp.float32)
         latter = jnp.dot(tokens_ref[...], weight_ref[:, at_up], preferred_element_type=jnp.float32)
         grad = jnp.dot(outer_ref[...], weight_ref[:, at_down], preferred_element_type=jnp.float32)
@@ -790,9 +935,29 @@
         side_s[:, at] = (grad * latter * logistic * (1.0 + former * (1.0 - logistic))).astype(low)
         side_s[:, at_up] = (grad * active).astype(low)
 
-    order = list(range(1, ep)) + [0]
-    over = (((0,), (0,)), ((), ()))
-    across = (((1,), (1,)), ((), ()))
+    def sums(e):
+        for d in order:
+            at = pl.ds(pl.multiple_of(lax.rem(f + d, ep) * 4 * rows, 128), 4 * rows)
+            start = 3 * e * hidden
+            for kind, (left, right) in enumerate(((tokens_ref, side_s), (tokens_ref, side_s), (outer_ref, gated_s))):
+                column = (kind * span if kind < 2 else 0) + e * hidden
+                sums_s[at, start + kind * hidden : start + (kind + 1) * hidden] = lax.dot_general(
+                    left[:, at], right[:, column : column + hidden], over, preferred_element_type=jnp.float32
+                ).astype(low)
+            plane.start(d, e)
+
+    def dn2(d):
+        here = pl.ds(pl.multiple_of(back.peer(d) * tokens, 16), tokens)
+
+        def tile(n, carry):
+            at = pl.ds(pl.multiple_of(n * 256, 256), 256)
+            part_s[here, at] = lax.dot_general(
+                side_s[here, :], weight_ref[at, : 2 * span], across, preferred_element_type=jnp.float32
+            ).astype(low)
+            return carry
+
+        lax.fori_loop(0, model // 256, tile, 0)
+        back.to_core(d)
 
     def mixtures(n, carry):
         at = pl.ds(pl.multiple_of(n * 256, 256), 256)
@@ -801,51 +966,30 @@
         ).astype(low)
         return carry
 
+    act(0)
+    sums(0)
+    for e in range(1, local):
+        act(e)
+    sums(1)
     for step, d in enumerate(order):
-        if step == 1:
-            lax.fori_loop(0, model // 256, mixtures, 0)
-            for g in order:
-                mixture.to_core(g)
-            later = pltpu.make_async_copy(mixture_s.at[:, pl.ds(EARLY, model - EARLY)], mixture_out, local_sem.at[2])
-            later.start()
-        if step > 1:
-            mixture.to_z(order[step - 2])
-        at = pl.ds(pl.multiple_of(back.peer(d) * 4 * rows, 128), 4 * rows)
-        sums_s[at, : 2 * span] = lax.dot_general(
-            tokens_ref[:, at], side_s[...], over, preferred_element_type=jnp.float32
-        ).astype(low)
-        sums_s[at, 2 * span :] = lax.dot_general(
-            outer_ref[:, at], gated_s[...], over, preferred_element_type=jnp.float32
-        ).astype(low)
-        plane.start(d)
-
-    mixture.to_z(order[2])
-    for step, d in enumerate(order):
-        here = pl.ds(pl.multiple_of(back.peer(d) * tokens, 16), tokens)
-
-        def tile(n, carry):
-            at = pl.ds(pl.multiple_of(n * 256, 256), 256)
-            part_s[here, at] = lax.dot_general(
-                side_s[here, :], weight_ref[at, : 2 * span], across, preferred_element_type=jnp.float32
-            ).astype(low)
-            return carry
-
-        lax.fori_loop(0, model // 256, tile, 0)
-        back.to_core(d)
+        dn2(d)
         if step > 0:
             back.to_z(order[step - 1])
-
+    for e in range(2, local):
+        sums(e)
+    lax.fori_loop(0, model // 256, mixtures, 0)
+    mixture_copy = pltpu.make_async_copy(mixture_s, mixture_out, local_sem.at[2])
+    mixture_copy.start()
     for d in order:
         plane.finish(d)
         for way in range(2):
             for number, out in enumerate((relay_out, own_out)):
                 pltpu.make_async_copy(
-                    plane.landings[way].at[d, number], out.at[d, :, plane.columns[way]], local_sem.at[number]
+                    plane.landings[way].at[d, number], out.at[way, d], local_sem.at[number]
                 ).start()
     returned_ref[back.rows(back.t), :] = back.collect()
     back.share(returned_ref)
-    mixed_ref[...] = mixture.collect()
-    later.wait()
+    mixture_copy.wait()
     back.finish(returned_ref)
     for number, out in enumerate((relay_out, own_out)):
         pltpu.make_async_copy(out, out, local_sem.at[number]).wait()
@@ -867,15 +1011,18 @@
         experts_kernel,
         out_shape=(
             shape((tokens, model + 128), jnp.float32),
-            shape((tokens // 2, EARLY), jnp.float32),
-            shape((reach, model - EARLY), low),
-            shape((ep, rows, full), low),
-            shape((ep, rows, full), low),
+            shape((reach, model), low),
+            shape((2, ep, rows, full // 2), low),
+            shape((2, ep, rows, full // 2), low),
             shape((tokens, 128), jnp.float32),
         ),
-        in_specs=[vmem] * 5,
-        out_specs=(vmem, vmem, anywhere, anywhere, anywhere, vmem),
+        in_specs=[vmem] * 2 + [anywhere] * 3,
+        out_specs=(vmem, anywhere, anywhere, anywhere, vmem),
         scratch_shapes=[
+            pltpu.VMEM(tokens_all.shape, low),
+            pltpu.VMEM(outer_all.shape, low),
+            pltpu.VMEM(weights.shape, low),
+            dma((2 + 3 * EXPERTS // ep,)),
             pltpu.VMEM((reach, 128), jnp.float32),
             pltpu.VMEM((reach, span), low),
             pltpu.VMEM((reach, 2 * span), low),
@@ -888,25 +1035,25 @@
             dma((2, ep, 2)),
             dma((3,)),
         ]
-        + z_sum_scratch(ep, tokens, model + 128, low)
-        + z_sum_scratch(ep, tokens, EARLY, low),
+        + z_sum_scratch(ep, tokens, model + 128, low),
         compiler_params=pltpu.CompilerParams(
             collective_id=collective_id, has_side_effects=True, vmem_limit_bytes=63 * 1024 * 1024
         ),
         cost_estimate=lasting(90),
         name="experts",
-    )(tokens_all, outer_all, routes_all, extra, weights)
+    )(routes_all, extra, tokens_all, outer_all, weights)
 
 
 def rear_kernel(
-    returned_ref, gates_ref, middle_ref, input_ref, outer_ref, normed1_ref, query_ref, pair_ref, mixed_ref,
-    log_ref, cos_ref, sin_ref, segment_ref, extra_ref, mixed_sum_ref, mixture_ref, relay_ref, own_ref, attn_ref,
+    gates_ref, log_ref, cos_ref, sin_ref, segment_ref, returned_hbm, middle_hbm, outer_hbm, extra_hbm,
+    mixed_hbm, query_hbm, pair_hbm, input_hbm, normed1_hbm, mixture_ref, relay_ref, own_ref, attn_ref,
     input_grad, layer_out, qkv_out, wo_out, expert_out,
+    returned_ref, middle_ref, outer_ref, extra_ref, mixed_ref, query_ref, pair_ref, input_ref, normed1_ref, in_sem,
     wo_s, qkv_s, query_s, grad_s, mixed_s, key_s, value_s, bias_s, query_grad_s, key_grad_s, value_grad_s,
     pair_s, landing_s, back_s, attn_grad_s, part_s, other_s, router_s, gains_s, mixture_s, own_s, second_s,
-    local_sem, key_send, key_recv, pair_send, pair_recv, second_send, second_recv, swap_send, swap_recv, *scratch,
+    local_sem, key_send, key_recv, pair_send, pair_recv, second_send, second_recv, swap_send, swap_recv, layer_send, layer_recv, *scratch,
 ):
-    ep, rows = expert_out.shape[0], expert_out.shape[1]
+    ep, rows = expert_out.shape[0], expert_out.shape[2]
     f, c, t = lax.axis_index("fsdp"), lax.axis_index("ctx"), lax.axis_index("tp")
     low = jnp.bfloat16
     tokens, model = input_ref.shape
@@ -915,8 +1062,8 @@
     width, kv_width = heads * HD, key_heads * HD
     qkv_width = width + 2 * kv_width
     sent = []
-    mixture = ZSum(mixture_ref, scratch[: ZSum.size], sent, mixture_s)
-    scratch = scratch[ZSum.size :]
+    mixture = PairSum(mixture_ref, mixture_s, scratch[:7], sent)
+    scratch = scratch[7:]
     size = len(shard_sum_scratch(ep, rows, 256, low))
     wo = ShardSum(wo_s, rows, width, scratch[:size], sent)
     qkv = ShardSum(qkv_s, rows, qkv_width + 128, scratch[size:], sent)
@@ -924,30 +1071,33 @@
     plane = [at_device(f, c ^ k, t) for k in range(1, 4)]
     core = partners[-1]
 
+    coming = fetch(
+        [
+            (returned_hbm, returned_ref), (middle_hbm, middle_ref), (outer_hbm, outer_ref), (extra_hbm, extra_ref),
+            (mixed_hbm, mixed_ref), (query_hbm, query_ref), (pair_hbm, pair_ref), (input_hbm, input_ref),
+            (normed1_hbm, normed1_ref),
+        ],
+        in_sem,
+    )
     copies = [
         pltpu.make_async_copy(attn_ref.at[:, pl.ds(qkv_width + 128, width)], wo_s, local_sem.at[0]),
         pltpu.make_async_copy(attn_ref.at[:, pl.ds(0, qkv_width + 128)], qkv_s, local_sem.at[1]),
     ]
     for copy in copies:
         copy.start()
-    for d in range(ep):
-        pltpu.make_async_copy(
-            mixture_ref.at[mixture.place(mixture.peer(d), t)], mixture_s.at[d], local_sem.at[2]
-        ).start()
+    for g in range(ep):
+        pltpu.make_async_copy(mixture_ref.at[mixture.place(g, t)], mixture_s.at[g], local_sem.at[2]).start()
     copies.append(pltpu.make_async_copy(own_ref, own_s, local_sem.at[3]))
     copies[2].start()
     greet(partners + plane[2:])
     order = wo.order
-    for d in order:
-        mixture.to_core(d)
-    full = relay_ref.shape[2]
+    mixture.to_core()
     seconds = {}
 
     def second(d):
         for way in range(2):
-            block = (d, slice(None), pl.ds(way * (full // 2), full // 2))
             copy = remote(
-                relay_ref.at[block], second_s.at[block], second_send.at[way, d], second_recv.at[way, d],
+                relay_ref.at[way, d], second_s.at[way, d], second_send.at[way, d], second_recv.at[way, d],
                 plane[1 - way],
             )
             copy.start()
@@ -957,20 +1107,21 @@
     def swap(d):
         for way in range(2):
             seconds[way, d].wait_recv()
-        own_s[d] = (own_s[d].astype(jnp.float32) + second_s[d].astype(jnp.float32)).astype(low)
+        own_s[:, d] = (own_s[:, d].astype(jnp.float32) + second_s[:, d].astype(jnp.float32)).astype(low)
         if d == 0:
-            copy = pltpu.make_async_copy(own_s.at[0], expert_out.at[f], swap_send.at[0])
+            copy = pltpu.make_async_copy(own_s.at[:, 0], expert_out.at[f], swap_send.at[0])
             copy.start()
             copies.append(copy)
         else:
-            copy = remote(own_s.at[d], expert_out.at[f], swap_send.at[d], swap_recv.at[d], partners[d - 1])
+            copy = remote(own_s.at[:, d], expert_out.at[f], swap_send.at[d], swap_recv.at[d], partners[d - 1])
             copy.start()
             sent.append((None, copy))
 
-    for d in order:
-        second(d)
+    second(1)
 
     small_lane = lax.broadcasted_iota(jnp.int32, (tokens, 128), 1)
+    for copy in coming[:4]:
+        copy.wait()
     gains = extra_ref[...].astype(jnp.float32).T
     gain_one, gain_two = gains[EXPERTS : EXPERTS + 1, :], gains[EXPERTS + 1 : EXPERTS + 2, :]
     tail = returned_ref[:, model:]
@@ -992,8 +1143,8 @@
     attn_grad_s[...] = middle_grad.astype(low)
 
     pltpu.make_async_copy(mixture_s, mixture_s, local_sem.at[2]).wait()
-    for d in range(1, ep):
-        mixture.to_z(d)
+    mixture.begin()
+    second(2)
     copies[0].wait()
     for start in range(0, width, 256):
         tile = jnp.dot(
@@ -1002,12 +1153,17 @@
         for side in range(0, 256, HD):
             grad_s[(start + side) // HD] = tile[:, side : side + HD]
 
+    copies[2].wait()
+    swap(1)
+    second(3)
     length = segment_ref.shape[1]
     seg_keys = jnp.broadcast_to(segment_ref[...].astype(jnp.float32), (128, length)).T[:, :1]
     seg_queries = segment_ref[:, pl.ds(pl.multiple_of(c * tokens, 128), tokens)].astype(jnp.float32)
     key_order = lax.broadcasted_iota(jnp.int32, (length, tokens), 0)
     query_order = lax.broadcasted_iota(jnp.int32, (length, tokens), 1) + c * tokens
     bias_s[...] = jnp.where((seg_keys == seg_queries) & (key_order <= query_order), 0.0, MASKED_SCORE)
+    for copy in coming[4:]:
+        copy.wait()
     for h in range(heads):
         query_s[h] = query_ref[:, h * HD : (h + 1) * HD]
         mixed_s[h] = mixed_ref[:, h * HD : (h + 1) * HD]
@@ -1038,7 +1194,10 @@
         value_grad_s[g] = value_grad.astype(low)
         return carry
 
-    lax.fori_loop(0, key_heads, attend_back, 0)
+    lax.fori_loop(0, key_heads // 2, attend_back, 0)
+    swap(2)
+    second(0)
+    lax.fori_loop(key_heads // 2, key_heads, attend_back, 0)
     for g in range(key_heads):
         pair_s[:, g * HD : (g + 1) * HD] = key_grad_s[g]
         pair_s[:, kv_width + g * HD : kv_width + (g + 1) * HD] = value_grad_s[g]
@@ -1060,11 +1219,9 @@
         preferred_element_type=jnp.float32,
     )
 
-    copies[2].wait()
-    for d in order:
-        wo.first(d)
-    for d in order:
-        swap(d)
+    swap(3)
+    swap(0)
+    mixture.cross()
     first_half = lax.rem(small_lane, HD) < HD // 2
 
     def turned_back(tile):
@@ -1080,6 +1237,8 @@
         block = landing_s.at[k - 1]
         remote(block, block, key_send.at[k - 1], key_recv.at[k - 1], plane[k - 1]).wait_recv()
         pair = pair + landing_s[k - 1].astype(jnp.float32)
+    for d in order:
+        wo.first(d)
     for start in range(0, kv_width, 128):
         back_s[:, width + start : width + start + 128] = turned_back(pair[:, start : start + 128]).astype(low)
     back_s[:, width + kv_width :] = pair[:, kv_width:].astype(low)
@@ -1129,27 +1288,28 @@
     qkv.to_z(3, qkv_out)
     wo.to_z(0, wo_out)
     qkv.to_z(0, qkv_out)
-    half = mixture.rows(t)
-    layer_out[half, :EARLY] = (middle_ref[half, :EARLY] + mixed_sum_ref[...]).astype(low)
-    layer_out[half, EARLY:] = (middle_ref[half, EARLY:] + mixture.collect()).astype(low)
-    mixture.share(layer_out)
     copies[3].wait()
     for d in range(1, ep):
         landing = expert_out.at[lax.rem(f + ep - d, ep)]
         remote(landing, landing, swap_send.at[d], swap_recv.at[d], core).wait_recv()
     wo.from_z(wo_out)
-    mixture.finish(layer_out)
+    half, other_half = (pl.ds(pl.multiple_of(part * (tokens // 2), 16), tokens // 2) for part in (t, 1 - t))
+    layer_out[half, :] = (middle_ref[half, :] + mixture.collect()).astype(low)
+    layer_copy = remote(layer_out.at[half], layer_out.at[half], layer_send, layer_recv, core)
+    layer_copy.start()
+    sent.append((None, layer_copy))
     qkv.from_z(qkv_out)
+    remote(layer_out.at[other_half], layer_out.at[other_half], layer_send, layer_recv, core).wait_recv()
     all_sent(sent)
 
 
 def rear(
     returned, gates, middle, inputs, outer, normed1, query, pair, mixed, log_total, cosine, sine, segments, extra,
-    mixed_sum, mixture, relay, own, attn, collective_id,
+    mixture, relay, own, attn, collective_id,
 ):
     ep = lax.axis_size("fsdp")
     tokens, model = inputs.shape
-    rows = own.shape[1]
+    rows = own.shape[2]
     heads, key_heads = query.shape[1] // HD, pair.shape[1] // (2 * HD)
     width, kv_width = heads * HD, key_heads * HD
     qkv_width = width + 2 * kv_width
@@ -1160,6 +1320,7 @@
     vmem = pl.BlockSpec(memory_space=pltpu.VMEM)
     shape = jax.ShapeDtypeStruct
     room = pltpu.VMEM
+    fetched = (returned, middle, outer, extra, mixed, query, pair, inputs, normed1)
     return pl.pallas_call(
         rear_kernel,
         out_shape=(
@@ -1167,11 +1328,13 @@
             shape((tokens, model), low),
             shape((rows, qkv_width + 128), jnp.float32),
             shape((rows, width), jnp.float32),
-            shape(own.shape, low),
+            shape((ep, 2, rows, own.shape[3]), low),
         ),
-        in_specs=[vmem] * 15 + [anywhere] * 4,
+        in_specs=[vmem] * 5 + [anywhere] * 13,
         out_specs=(vmem,) * 4 + (anywhere,),
-        scratch_shapes=[
+        scratch_shapes=[room(each.shape, each.dtype) for each in fetched]
+        + [
+            dma((len(fetched),)),
             room((model, width), low),
             room((model, qkv_width + 128), low),
             room((heads, tokens, HD), low),
@@ -1191,7 +1354,7 @@
             room((tokens, model), low),
             room((model, 128), jnp.float32),
             room((8, model), jnp.float32),
-            room((ep, tokens // 2, model - EARLY), low),
+            room((ep, tokens // 2, model), low),
             room(own.shape, low),
             room(own.shape, low),
             dma((4,)),
@@ -1203,8 +1366,10 @@
             dma((2, ep)),
             dma((ep,)),
             dma((ep,)),
+            dma,
+            dma,
         ]
-        + z_sum_scratch(ep, tokens, model - EARLY, low)
+        + pair_sum_scratch(ep, tokens, model, low)
         + shard_sum_scratch(ep, rows, width, low)
         + shard_sum_scratch(ep, rows, qkv_width + 128, low),
         compiler_params=pltpu.CompilerParams(
@@ -1212,21 +1377,23 @@
         ),
         cost_estimate=lasting(170),
         name="rear",
-    )(
-        returned, gates, middle, inputs, outer, normed1, query, pair, mixed, log_total, cosine, sine, segments,
-        extra, mixed_sum, mixture, relay, own, attn,
-    )
+    )(gates, log_total, cosine, sine, segments, *fetched, mixture, relay, own, attn)
 
 
 def finish_kernel(
-    expert_ref, qkv_ref, wo_ref, query_out, key_out, value_out, output_out, gate_out, up_out, down_out
+    expert_ref, qkv_ref, wo_ref, input_ref, layer_ref,
+    query_out, key_out, value_out, output_out, router_out, gain_one_out, gain_two_out,
+    gate_out, up_out, down_out, input_out, layer_out,
 ):
     local, _, hidden = gate_out.shape
+    cut = expert_ref.shape[3] // local
     for e in range(local):
+        at = slice(e * cut, (e + 1) * cut)
+        both = jnp.concatenate([expert_ref[0, 0, :, at], expert_ref[0, 1, :, at]], 1).astype(jnp.float32)
         for kind, out in enumerate((gate_out, up_out, down_out)):
-            start = (kind * local + e) * hidden
-            block = expert_ref[0, :, start : start + hidden].astype(jnp.float32)
-            out[e] = block.T if kind == 2 else block
+            out[e] = both[:, kind * hidden : (kind + 1) * hidden]
+    input_out[...] = input_ref[...]
+    layer_out[...] = layer_ref[...]
 
     @pl.when(pl.program_id(0) == 0)
     def _():
@@ -1234,18 +1401,25 @@
         query_out[...] = qkv_ref[:, :width]
         key_out[...] = qkv_ref[:, width : width + kv_width]
         value_out[...] = qkv_ref[:, width + kv_width : width + 2 * kv_width]
-        output_out[...] = wo_ref[...].T
-
-
-def finish(experts, qkv, wo, kv_width, hidden):
-    ep, rows, full = experts.shape
+        small = qkv_ref[:, width + 2 * kv_width :].T
+        router_out[...] = small[:EXPERTS]
+        gain_one_out[...] = small[EXPERTS : EXPERTS + 1]
+        gain_two_out[...] = small[EXPERTS + 1 : EXPERTS + 2]
+        output_out[...] = wo_ref[...]
+
+
+def finish(experts, qkv, wo, input_grad, layer_output, kv_width, hidden):
+    ep, _, rows, half = experts.shape
     width = wo.shape[1]
-    local = full // (3 * hidden)
+    local = 2 * half // (3 * hidden)
+    tokens, model = input_grad.shape
     shape = jax.ShapeDtypeStruct
 
     def whole(*dims):
         return pl.BlockSpec(dims, lambda i: (0, 0))
 
+    by_z = pl.BlockSpec((local, rows, hidden), lambda i: (i, 0, 0))
+    by_rows = pl.BlockSpec((tokens // ep, model), lambda i: (i, 0))
     return pl.pallas_call(
         finish_kernel,
         grid=(ep,),
@@ -1253,29 +1427,41 @@
             shape((rows, width), jnp.float32),
             shape((rows, kv_width), jnp.float32),
             shape((rows, kv_width), jnp.float32),
-            shape((width, rows), jnp.float32),
+            shape((rows, width), jnp.float32),
+            shape((EXPERTS, rows), jnp.float32),
+            shape((1, rows), jnp.float32),
+            shape((1, rows), jnp.float32),
             shape((ep * local, rows, hidden), jnp.float32),
             shape((ep * local, rows, hidden), jnp.float32),
-            shape((ep * local, hidden, rows), jnp.float32),
+            shape((ep * local, rows, hidden), jnp.float32),
+            shape((tokens, model), jnp.float32),
+            shape((tokens, model), layer_output.dtype),
         ),
         in_specs=[
-            pl.BlockSpec((1, rows, full), lambda i: (i, 0, 0)),
+            pl.BlockSpec((1, 2, rows, half), lambda i: (i, 0, 0, 0)),
             whole(*qkv.shape),
             whole(*wo.shape),
+            by_rows,
+            by_rows,
         ],
         out_specs=(
             whole(rows, width),
             whole(rows, kv_width),
             whole(rows, kv_width),
-            whole(width, rows),
-            pl.BlockSpec((local, rows, hidden), lambda i: (i, 0, 0)),
-            pl.BlockSpec((local, rows, hidden), lambda i: (i, 0, 0)),
-            pl.BlockSpec((local, hidden, rows), lambda i: (i, 0, 0)),
+            whole(rows, width),
+            whole(EXPERTS, rows),
+            whole(1, rows),
+            whole(1, rows),
+            by_z,
+            by_z,
+            by_z,
+            by_rows,
+            by_rows,
         ),
-        compiler_params=pltpu.CompilerParams(vmem_limit_bytes=32 * 1024 * 1024),
+        compiler_params=pltpu.CompilerParams(vmem_limit_bytes=60 * 1024 * 1024),
         cost_estimate=lasting(6),
         name="finish",
-    )(experts, qkv, wo)
+    )(experts, qkv, wo, input_grad, layer_output)
 
 
 def plain_shards(
@@ -1554,45 +1740,41 @@
     down_weight,
     cotangent,
 ):
-    low = jnp.bfloat16
-    width = query_weight.shape[1]
-    kv_width = key_weight.shape[1]
-    hidden_width = gate_weight.shape[2]
     extra = jnp.concatenate([router_weight, norm_gain[:, None], ffn_gain[:, None]], 1)
     extra = jnp.pad(extra, ((0, 0), (0, 128 - extra.shape[1])))
-    attn_shard = jnp.concatenate([query_weight, key_weight, value_weight, extra, output_weight.T], 1)
-    freq = 10000.0 ** (-2.0 * jnp.arange(HD // 2, dtype=jnp.float32) / HD)
+    freq = 10000.0 ** (-2.0 * np.arange(HD // 2) / HD)
     (
         expert_full, outer_all, routes_all, normed2_all,
-        attn_full, normed1, query, pair_all, mixed, log_total, middle, cosine, sine, extra_all,
+        attn_full, normed1, query, pair_all, mixed, middle, log_total, cosine, sine, extra_all,
     ) = front(
-        attn_shard, gate_weight, up_weight, down_weight.transpose(0, 2, 1), cotangent, routes, layer_input,
-        segments, jnp.tile(freq, 4)[None, :], width // HD, kv_width // HD,
-    )
-    returned, mixed_sum, mixture, relay, own, gates = run_experts(
+        query_weight, key_weight, value_weight, extra, output_weight.T, gate_weight, up_weight,
+        down_weight.transpose(0, 2, 1), cotangent, routes.T, layer_input, segments,
+        np.tile(freq.astype(np.float32), 4)[None, :],
+    )
+    returned, mixture, relay, own, gates = run_experts(
         normed2_all, outer_all, routes_all, extra_all, expert_full, 2
     )
     input_grad, layer_output, qkv_out, wo_out, expert_out = rear(
         returned, gates, middle, layer_input, cotangent, normed1, query, pair_all, mixed, log_total, cosine, sine,
-        segments, extra_all, mixed_sum, mixture, relay, own, attn_full, 3,
-    )
-    small_out = qkv_out[:, width + 2 * kv_width :]
-    query_out, key_out, value_out, output_out, gate_out, up_out, down_out = finish(
-        expert_out, qkv_out, wo_out, kv_width, hidden_width
-    )
+        segments, extra_all, mixture, relay, own, attn_full, 3,
+    )
+    (
+        query_out, key_out, value_out, output_out, router_out, gain_one_out, gain_two_out,
+        gate_out, up_out, down_out, input_grad, layer_output,
+    ) = finish(expert_out, qkv_out, wo_out, input_grad, layer_output, key_weight.shape[1], gate_weight.shape[2])
     return (
         layer_output,
         input_grad,
-        small_out[:, EXPERTS],
+        gain_one_out[0],
         query_out,
         key_out,
         value_out,
-        output_out,
-        small_out[:, EXPERTS + 1],
-        small_out[:, :EXPERTS],
+        output_out.T,
+        gain_two_out[0],
+        router_out.T,
         gate_out,
         up_out,
-        down_out,
+        down_out.transpose(0, 2, 1),
     )
 
 
@@ -1627,5 +1809,6 @@
         P(None, ("fsdp", "ctx"), "tp"),
         P(None, "tp", ("fsdp", "ctx")),
     )
-    body = shards if mesh.shape["ctx"] == 4 else plain_shards
+    fits = mesh.shape["ctx"] == 4 and mesh.shape["fsdp"] == 4 and mesh.shape["tp"] == 2
+    body = shards if fits else plain_shards
     return jax.shard_map(body, mesh=mesh, in_specs=in_specs, out_specs=out_specs, check_vma=False)

time: 398 us -> 375 us (0.942)
  local copies, waits for them, and re-layouts: 18.6 us -> 0.74 us
  Pallas kernels: 373 us -> 367 us
    unnamed x22 -> x0, local copies, waits for them, and re-layouts: 14.5 us -> none
    pallas_call x1, Pallas kernels: 98 us -> 85.1 us  [run_experts(): pl.pallas_call(experts_kernel, out_shape=(shape((tokens, model + 128), jn...]
    pallas_call x1, Pallas kernels: 114 us -> 123 us  [rear(): pl.pallas_call(rear_kernel, out_shape=(shape((tokens, model), jnp.float32...]
    pallas_call x1, Pallas kernels: 158 us -> 153 us  [front(): pl.pallas_call(front_kernel, out_shape=(shape((total, 3 * local * gate.sh...]
where the time goes in v5:
time: 375 us; the launch traced here: 370 us
  Pallas kernels  367 us (98%)
    pallas_call x1, Pallas kernels, front(): pl.pallas_call(front_kernel, out_shape=(shape((total, 3 * local * gate.sh...  153 us
    pallas_call x1, Pallas kernels, rear(): pl.pallas_call(rear_kernel, out_shape=(shape((tokens, model), jnp.float32...  123 us
    pallas_call x1, Pallas kernels, run_experts(): pl.pallas_call(experts_kernel, out_shape=(shape((tokens, model + 128), jn...  85.1 us

profile of v5, /device:TPU:9, one launch (start us, length us, event | category | flops | bytes accessed | tf_op | source)
XLA Modules:
  0.0 369.6 jit_solution(13525085843300519634)
XLA Ops:
  0.6 0.7 pad_maximum_fusion
  1.4 0.1 copy.30
  1.5 0.6 pad.4.extra_ref
  2.1 152.6 %front.1 = (bf16[1536,3072]{1,0:T(8,128)(2,1)}, bf16[1024,1536]{1,0:T(8,128)(2,1)}, s32[8,1024]{1,0:T(8,128)}, bf16[1024,1536]{1,0:T(8,128)(2,1)}, bf16[1536,217...) custom-call(bf16[96,768]{1,0:T(8,128)(2,1)} %query_ref.1, ...), custom_call_target="tpu_custom_call" | custom-call | bytes 608849984 | tf_op jit(solution)/shard_map/front/pallas_call | solution.py:466
  154.7 85.1 %experts.1 = (f32[256,1664]{1,0:T(8,128)}, bf16[1024,1536]{1,0:T(8,128)(2,1)}, bf16[2,4,96,1536]{3,2,1,0:T(8,128)(2,1)}, bf16[2,4,96,1536]{3,2,1,0:T(8,128)(2,1)}, f32[256,128]{1,0:T(8,128)}) custom-call(s32[8,1024]{1,0:T(8,128)} %get-tuple-element.48.routes_ref, bf16[1536,128]{1,0:T(8,128)(2,1)} %get-tuple-element.49.extra_ref.extra_hbm, ...), custom_call_target="tpu_custom_call" | custom-call | bytes 332100000 | tf_op jit(solution)/shard_map/experts/pallas_call | solution.py:1010
  239.8 123.2 %rear.1 = (f32[256,1536]{1,0:T(8,128)}, bf16[256,1536]{1,0:T(8,128)(2,1)}, f32[96,1408]{1,0:T(8,128)}, f32[96,768]{1,0:T(8,128)}, bf16[4,2,96,1536]{3,2,1,0:T(8,128)(2,1)}) custom-call(f32[256,128]{1,0:T(8,128)} %get-tuple-element.53.gates_ref, f32[12,1,256]{2,1,0:T(1,128)} %get-tuple-element.54.log_ref, f32[256,128]{1,0:T(8,128)} %get-tuple-element.55.cos_ref, ...), custom_call_target="tpu_custom_call" | custom-call | bytes 627299968 | tf_op jit(solution)/shard_map/rear/pallas_call | solution.py:1324
  363.0 6.3 %finish.1 = (f32[96,768]{1,0:T(8,128)}, f32[96,256]{1,0:T(8,128)}, f32[96,256]{1,0:T(8,128)}, f32[96,768]{1,0:T(8,128)}, f32[16,96]{1,0:T(8,128)}, /*index=5*/f3...) custom-call(bf16[4,2,96,1536]{3,2,1,0:T(8,128)(2,1)} %get-tuple-elem, ...), custom_call_target="tpu_custom_call" | custom-call | bytes 22140000 | tf_op jit(solution)/shard_map/finish/pallas_call | solution.py:1423

commit v6 on v5

--- a/solution.py
+++ b/solution.py
@@ -709,7 +709,7 @@
         scratch += [
             pltpu.VMEM((ep, 2, rows, part), low),
             pltpu.VMEM((ep, rows, part), low),
-            pltpu.VMEM((ep - 1, rows, part), low),
+            pltpu.VMEM((ep, rows, part), low),
         ]
     return scratch + [
         dma((2, ep, 2)), dma((2, ep, 2)), dma((2, ep)), dma((2, ep)), dma((2, ep)), dma((2, ep))
@@ -812,6 +812,62 @@
                     landing, landing, self.z_send.at[way, d], self.z_recv.at[way, d], self.neighbours[0]
                 ).wait_recv()
                 out[:, self.columns[way]] += self.z_in[way][d - 1].astype(jnp.float32)
+
+    def halves(self):
+        others = [2 - (self.f & 2) + j for j in range(2)]
+        return (self.f == 1) | (self.f == 2), list(enumerate(others, 1)), self.f ^ 1
+
+    def distance(self, g):
+        return lax.rem(g + self.ep - self.f, self.ep)
+
+    def pair_begin(self, out):
+        inner, others, partner = self.halves()
+        beside = at_device(partner, self.c, self.t)
+        for way in self.ways:
+            for slot, g in others + [(0, partner)]:
+                d = self.distance(g)
+                self.first_in[way][d, 1] = self.total(d, way).astype(self.part.dtype)
+                copy = remote(
+                    self.first_in[way].at[d, 1], self.z_in[way].at[slot],
+                    self.z_send.at[way, slot], self.z_recv.at[way, slot], beside,
+                )
+                when = None if slot == 0 else jnp.logical_not(inner)
+                if when is None:
+                    copy.start()
+                else:
+                    pl.when(when)(copy.start)
+                self.sent.append((when, copy))
+            out[:, self.columns[way]] = self.total(0, way)
+
+    def pair_cross(self):
+        inner, others, partner = self.halves()
+        beside = at_device(partner, self.c, self.t)
+        for way in self.ways:
+            for slot, g in others:
+                d = self.distance(g)
+
+                @pl.when(inner)
+                def _():
+                    block = self.z_in[way].at[slot]
+                    remote(block, block, self.z_send.at[way, slot], self.z_recv.at[way, slot], beside).wait_recv()
+                    added = self.first_in[way][d, 1].astype(jnp.float32) + self.z_in[way][slot].astype(jnp.float32)
+                    self.first_in[way][d, 1] = added.astype(self.part.dtype)
+
+                copy = remote(
+                    self.first_in[way].at[d, 1], self.z_in[way].at[3],
+                    self.z_send.at[way, slot], self.z_recv.at[way, 3], at_device(g, self.c, self.t),
+                )
+                pl.when(inner)(copy.start)
+                self.sent.append((inner, copy))
+
+    def pair_collect(self, out):
+        for way in self.ways:
+            for slot in (0, 3):
+                block = self.z_in[way].at[slot]
+                remote(
+                    block, block, self.z_send.at[way, slot], self.z_recv.at[way, slot], self.neighbours[0]
+                ).wait_recv()
+                out[:, self.columns[way]] += self.z_in[way][slot].astype(jnp.float32)
 
 
 def all_partners(ep):
@@ -980,6 +1036,8 @@
     lax.fori_loop(0, model // 256, mixtures, 0)
     mixture_copy = pltpu.make_async_copy(mixture_s, mixture_out, local_sem.at[2])
     mixture_copy.start()
+    returned_ref[back.rows(back.t), :] = back.collect()
+    back.share(returned_ref)
     for d in order:
         plane.finish(d)
         for way in range(2):
@@ -987,8 +1045,6 @@
                 pltpu.make_async_copy(
                     plane.landings[way].at[d, number], out.at[way, d], local_sem.at[number]
                 ).start()
-    returned_ref[back.rows(back.t), :] = back.collect()
-    back.share(returned_ref)
     mixture_copy.wait()
     back.finish(returned_ref)
     for number, out in enumerate((relay_out, own_out)):
@@ -1276,29 +1332,25 @@
     input_grad[...] += inverse * scaled - inputs * (inverse * inverse * inverse) * mean_term
     qkv.second(1)
     qkv.first(3)
-    wo.to_z(1, wo_out)
+    wo.pair_begin(wo_out)
     qkv.second(2)
     qkv.first(0)
-    qkv.to_z(1, qkv_out)
-    wo.to_z(2, wo_out)
     qkv.second(3)
-    qkv.to_z(2, qkv_out)
-    wo.to_z(3, wo_out)
+    wo.pair_cross()
     qkv.second(0)
-    qkv.to_z(3, qkv_out)
-    wo.to_z(0, wo_out)
-    qkv.to_z(0, qkv_out)
+    qkv.pair_begin(qkv_out)
+    qkv.pair_cross()
     copies[3].wait()
     for d in range(1, ep):
         landing = expert_out.at[lax.rem(f + ep - d, ep)]
         remote(landing, landing, swap_send.at[d], swap_recv.at[d], core).wait_recv()
-    wo.from_z(wo_out)
+    wo.pair_collect(wo_out)
     half, other_half = (pl.ds(pl.multiple_of(part * (tokens // 2), 16), tokens // 2) for part in (t, 1 - t))
     layer_out[half, :] = (middle_ref[half, :] + mixture.collect()).astype(low)
     layer_copy = remote(layer_out.at[half], layer_out.at[half], layer_send, layer_recv, core)
     layer_copy.start()
     sent.append((None, layer_copy))
-    qkv.from_z(qkv_out)
+    qkv.pair_collect(qkv_out)
     remote(layer_out.at[other_half], layer_out.at[other_half], layer_send, layer_recv, core).wait_recv()
     all_sent(sent)
 

time: 375 us -> 367 us (0.979)
  Pallas kernels: 367 us -> 358 us
    pallas_call x1, Pallas kernels: 123 us -> 114 us  [rear(): pl.pallas_call(rear_kernel, out_shape=(shape((tokens, model), jnp.float32...]
where the time goes in v6:
time: 367 us; the launch traced here: 360 us
  Pallas kernels  358 us (98%)
    pallas_call x1, Pallas kernels, front(): pl.pallas_call(front_kernel, out_shape=(shape((total, 3 * local * gate.sh...  153 us
    pallas_call x1, Pallas kernels, rear(): pl.pallas_call(rear_kernel, out_shape=(shape((tokens, model), jnp.float32...  114 us
    pallas_call x1, Pallas kernels, run_experts(): pl.pallas_call(experts_kernel, out_shape=(shape((tokens, model + 128), jn...  85.1 us

profile of v6, /device:TPU:9, one launch (start us, length us, event | category | flops | bytes accessed | tf_op | source)
XLA Modules:
  0.0 360.3 jit_solution(16422295861647795865)
XLA Ops:
  0.6 0.7 pad_maximum_fusion
  1.4 0.1 copy.30
  1.5 0.6 pad.4.extra_ref
  2.1 152.6 %front.1 = (bf16[1536,3072]{1,0:T(8,128)(2,1)}, bf16[1024,1536]{1,0:T(8,128)(2,1)}, s32[8,1024]{1,0:T(8,128)}, bf16[1024,1536]{1,0:T(8,128)(2,1)}, bf16[1536,217...) custom-call(bf16[96,768]{1,0:T(8,128)(2,1)} %query_ref.1, ...), custom_call_target="tpu_custom_call" | custom-call | bytes 608849984 | tf_op jit(solution)/shard_map/front/pallas_call | solution.py:466
  154.7 85.1 %experts.1 = (f32[256,1664]{1,0:T(8,128)}, bf16[1024,1536]{1,0:T(8,128)(2,1)}, bf16[2,4,96,1536]{3,2,1,0:T(8,128)(2,1)}, bf16[2,4,96,1536]{3,2,1,0:T(8,128)(2,1)}, f32[256,128]{1,0:T(8,128)}) custom-call(s32[8,1024]{1,0:T(8,128)} %get-tuple-element.48.routes_ref, bf16[1536,128]{1,0:T(8,128)(2,1)} %get-tuple-element.49.extra_ref.extra_hbm, ...), custom_call_target="tpu_custom_call" | custom-call | bytes 332100000 | tf_op jit(solution)/shard_map/experts/pallas_call | solution.py:1066
  239.9 113.9 %rear.1 = (f32[256,1536]{1,0:T(8,128)}, bf16[256,1536]{1,0:T(8,128)(2,1)}, f32[96,1408]{1,0:T(8,128)}, f32[96,768]{1,0:T(8,128)}, bf16[4,2,96,1536]{3,2,1,0:T(8,128)(2,1)}) custom-call(f32[256,128]{1,0:T(8,128)} %get-tuple-element.53.gates_ref, f32[12,1,256]{2,1,0:T(1,128)} %get-tuple-element.54.log_ref, f32[256,128]{1,0:T(8,128)} %get-tuple-element.55.cos_ref, ...), custom_call_target="tpu_custom_call" | custom-call | bytes 627299968 | tf_op jit(solution)/shard_map/rear/pallas_call | solution.py:1376
  353.7 6.3 %finish.1 = (f32[96,768]{1,0:T(8,128)}, f32[96,256]{1,0:T(8,128)}, f32[96,256]{1,0:T(8,128)}, f32[96,768]{1,0:T(8,128)}, f32[16,96]{1,0:T(8,128)}, /*index=5*/f3...) custom-call(bf16[4,2,96,1536]{3,2,1,0:T(8,128)(2,1)} %get-tuple-elem, ...), custom_call_target="tpu_custom_call" | custom-call | bytes 22140000 | tf_op jit(solution)/shard_map/finish/pallas_call | solution.py:1475

commit v7 on v6

--- a/solution.py
+++ b/solution.py
@@ -107,14 +107,14 @@
 
 
 def front_kernel(
-    query_ref, key_ref, value_ref, extra_ref, wo_ref, gate_ref, up_ref, down_ref, outer_ref, routes_ref,
-    input_ref, segment_ref, freq_ref,
+    query_ref, key_ref, value_ref, wo_ref, gate_ref, up_ref, down_ref, outer_ref, routes_ref,
+    input_ref, segment_ref, freq_ref, router_ref, gain_one_ref, gain_two_ref,
     expert_out, outer_out, routes_out, normed2_out,
     attn_hbm, normed1_hbm, query_hbm, pair_hbm, mixed_hbm, middle_hbm, log_out, cos_out, sin_out, extra_out,
     attn_out, normed1_out, query_out, pair_out, mixed_out, middle_out, out_sem,
     query_s, key_s, value_s, mixed_s, bias_s, part_s, other_s, normed2_s,
     local_sem, z_send, z_recv, plane_send, plane_recv, relay_send, relay_recv, core_send, core_recv,
-    key_send, key_recv, pair_send, pair_recv, chain_send, chain_recv,
+    key_send, key_recv, pair_send, pair_recv, chain_send, chain_recv, own_sem,
 ):
     ep = z_send.shape[1] + 1
     f, c, t = lax.axis_index("fsdp"), lax.axis_index("ctx"), lax.axis_index("tp")
@@ -145,9 +145,20 @@
     plane = [at_device(f, c ^ k, t) for k in range(1, 4)]
     x_device, y_device = plane[0], plane[1]
     core = at_device(f, c, 1 - t)
+    mine = shard_rows(f, c)
+    own_attn = []
+    for start, ref in (
+        (0, query_ref), (width, key_ref), (width + kv_width, value_ref), (qkv_width + 128, wo_ref)
+    ):
+        target = attn_out.at[mine, pl.ds(start, ref.shape[1])]
+        own_attn.append(pltpu.make_async_copy(ref, target, own_sem.at[len(own_attn)]))
+        own_attn[-1].start()
+    shown = jnp.concatenate([router_ref[...].astype(jnp.float32), jnp.zeros((128 - EXPERTS, rows), jnp.float32)], 0)
+    row = lax.broadcasted_iota(jnp.int32, (128, rows), 0)
+    shown = jnp.where(row == EXPERTS, gain_one_ref[...].astype(jnp.float32), shown)
+    shown = jnp.where(row == EXPERTS + 1, gain_two_ref[...].astype(jnp.float32), shown)
+    attn_out[mine, qkv_width : qkv_width + 128] = shown.T.astype(low)
     greet(line + plane + [core])
-
-    mine = shard_rows(f, c)
     sent = []
 
     def send(copy, when=None):
@@ -256,13 +267,8 @@
                 remote(block, block, core_send.at[kind - 1, g], core_recv.at[kind - 1, g], core), f != g
             )
 
-    start = 0
-    for ref in (query_ref, key_ref, value_ref, extra_ref, wo_ref):
-        pltpu.make_async_copy(
-            ref, attn_out.at[mine, pl.ds(start, ref.shape[1])], local_sem.at[0]
-        ).start()
-        start += ref.shape[1]
-    pltpu.make_async_copy(attn_out.at[mine], attn_out.at[mine], local_sem.at[0]).wait()
+    for copy in own_attn:
+        copy.wait()
     chain_begin(0, attn_out.at[mine], attn_out.at[mine])
     own_outer = pltpu.make_async_copy(outer_ref, outer_out.at[own_tokens], local_sem.at[2])
     own_outer.start()
@@ -440,12 +446,12 @@
 
 
 def front(
-    query, key, value, extra, wo, gate, up, down, outer, routes, inputs, segments, freq
+    query, key, value, wo, gate, up, down, outer, routes, inputs, segments, freq, router, gain_one, gain_two
 ):
     ep = lax.axis_size("fsdp")
     rows = query.shape[0]
     heads, key_heads = query.shape[1] // HD, key.shape[1] // HD
-    width = sum(part.shape[1] for part in (query, key, value, extra, wo))
+    width = sum(part.shape[1] for part in (query, key, value, wo)) + 128
     total = rows * ep * lax.axis_size("ctx")
     local = gate.shape[0] // ep
     tokens, model = inputs.shape
@@ -478,7 +484,7 @@
             shape((tokens, 128), jnp.float32),
             shape((total, 128), low),
         ),
-        in_specs=[anywhere] * 10 + [vmem] * 3,
+        in_specs=[anywhere] * 9 + [vmem] * 6,
         out_specs=(anywhere,) * 10 + (vmem,) * 4,
         scratch_shapes=[pltpu.VMEM(*each) for each in kept]
         + [
@@ -506,13 +512,14 @@
             dma,
             dma((3, 2, ep - 1)),
             dma((3, 2, ep - 1)),
+            dma((4,)),
         ],
         compiler_params=pltpu.CompilerParams(
             collective_id=1, has_side_effects=True, vmem_limit_bytes=60 * 1024 * 1024
         ),
         cost_estimate=lasting(165),
         name="front",
-    )(query, key, value, extra, wo, gate, up, down, outer, routes, inputs, segments, freq)
+    )(query, key, value, wo, gate, up, down, outer, routes, inputs, segments, freq, router, gain_one, gain_two)
 
 
 def z_sum_scratch(ep, tokens, width, low):
@@ -1262,6 +1269,10 @@
         copy = remote(pair_s.at[place], landing_s.at[k - 1], key_send.at[k - 1], key_recv.at[k - 1], plane[k - 1])
         copy.start()
         sent.append((None, copy))
+    swap(3)
+    swap(0)
+    mixture.cross()
+
     def wo_sums(n, carry):
         at = pl.ds(pl.multiple_of(n * 256, 256), 256)
         wo_s[at, :] = lax.dot_general(
@@ -1275,9 +1286,6 @@
         preferred_element_type=jnp.float32,
     )
 
-    swap(3)
-    swap(0)
-    mixture.cross()
     first_half = lax.rem(small_lane, HD) < HD // 2
 
     def turned_back(tile):
@@ -1792,16 +1800,14 @@
     down_weight,
     cotangent,
 ):
-    extra = jnp.concatenate([router_weight, norm_gain[:, None], ffn_gain[:, None]], 1)
-    extra = jnp.pad(extra, ((0, 0), (0, 128 - extra.shape[1])))
     freq = 10000.0 ** (-2.0 * np.arange(HD // 2) / HD)
     (
         expert_full, outer_all, routes_all, normed2_all,
         attn_full, normed1, query, pair_all, mixed, middle, log_total, cosine, sine, extra_all,
     ) = front(
-        query_weight, key_weight, value_weight, extra, output_weight.T, gate_weight, up_weight,
+        query_weight, key_weight, value_weight, output_weight.T, gate_weight, up_weight,
         down_weight.transpose(0, 2, 1), cotangent, routes.T, layer_input, segments,
-        np.tile(freq.astype(np.float32), 4)[None, :],
+        np.tile(freq.astype(np.float32), 4)[None, :], router_weight.T, norm_gain[None, :], ffn_gain[None, :],
     )
     returned, mixture, relay, own, gates = run_experts(
         normed2_all, outer_all, routes_all, extra_all, expert_full, 2

time: 367 us -> 365 us (level)
  no operation moved by 1% of the time
where the time goes in v7:
time: 365 us; the launch traced here: 358 us
  Pallas kernels  357 us (98%)
    pallas_call x1, Pallas kernels, front(): pl.pallas_call(front_kernel, out_shape=(shape((total, 3 * local * gate.sh...  152 us
    pallas_call x1, Pallas kernels, rear(): pl.pallas_call(rear_kernel, out_shape=(shape((tokens, model), jnp.float32...  114 us
    pallas_call x1, Pallas kernels, run_experts(): pl.pallas_call(experts_kernel, out_shape=(shape((tokens, model + 128), jn...  85.1 us

profile of v7, /device:TPU:9, one launch (start us, length us, event | category | flops | bytes accessed | tf_op | source)
XLA Modules:
  0.0 357.9 jit_solution(12080000294090143432)
XLA Ops:
  0.6 151.7 %front.1 = (bf16[1536,3072]{1,0:T(8,128)(2,1)}, bf16[1024,1536]{1,0:T(8,128)(2,1)}, s32[8,1024]{1,0:T(8,128)}, bf16[1024,1536]{1,0:T(8,128)(2,1)}, bf16[1536,217...) custom-call(bf16[96,768]{1,0:T(8,128)(2,1)} %query_ref.1, ...), custom_call_target="tpu_custom_call" | custom-call | bytes 608849984 | tf_op jit(solution)/shard_map/front/pallas_call | solution.py:472
  152.4 85.1 %experts.1 = (f32[256,1664]{1,0:T(8,128)}, bf16[1024,1536]{1,0:T(8,128)(2,1)}, bf16[2,4,96,1536]{3,2,1,0:T(8,128)(2,1)}, bf16[2,4,96,1536]{3,2,1,0:T(8,128)(2,1)}, f32[256,128]{1,0:T(8,128)}) custom-call(s32[8,1024]{1,0:T(8,128)} %get-tuple-element.48.routes_ref, bf16[1536,128]{1,0:T(8,128)(2,1)} %get-tuple-element.49.extra_ref.extra_hbm, ...), custom_call_target="tpu_custom_call" | custom-call | bytes 332100000 | tf_op jit(solution)/shard_map/experts/pallas_call | solution.py:1073
  237.5 113.9 %rear.1 = (f32[256,1536]{1,0:T(8,128)}, bf16[256,1536]{1,0:T(8,128)(2,1)}, f32[96,1408]{1,0:T(8,128)}, f32[96,768]{1,0:T(8,128)}, bf16[4,2,96,1536]{3,2,1,0:T(8,128)(2,1)}) custom-call(f32[256,128]{1,0:T(8,128)} %get-tuple-element.53.gates_ref, f32[12,1,256]{2,1,0:T(1,128)} %get-tuple-element.54.log_ref, f32[256,128]{1,0:T(8,128)} %get-tuple-element.55.cos_ref, ...), custom_call_target="tpu_custom_call" | custom-call | bytes 627299968 | tf_op jit(solution)/shard_map/rear/pallas_call | solution.py:1384
  351.4 6.3 %finish.1 = (f32[96,768]{1,0:T(8,128)}, f32[96,256]{1,0:T(8,128)}, f32[96,256]{1,0:T(8,128)}, f32[96,768]{1,0:T(8,128)}, f32[16,96]{1,0:T(8,128)}, /*index=5*/f3...) custom-call(bf16[4,2,96,1536]{3,2,1,0:T(8,128)(2,1)} %get-tuple-elem, ...), custom_call_target="tpu_custom_call" | custom-call | bytes 22140000 | tf_op jit(solution)/shard_map/finish/pallas_call | solution.py:1483
